TPU v7x, 32 devices: a whole 2x2x4 slice. The times are simulated.
32 devices in a mesh: lon: 4 (over z), lat: 2 (over core), mem: 4 (over y, x).
Axes of the slice: x: 2, y: 2, z: 4, core: 2. Of those that a mesh axis runs over, the one named last changes fastest.
Arguments:
- controls: float32 [16, 96, 48, 128], P('mem', 'lon', 'lat'), may hold values from -6 to 6
- ensemble: bfloat16 [16, 96, 48, 128], P('mem', 'lon', 'lat'), may hold values from -1.5 to 1.5
- taps_lon: float32 [17], replicated, may hold values from 0.05 to 0.35
- taps_lat: float32 [17], replicated, may hold values from 0.05 to 0.35
- obs_columns: int32 [4, 2, 4, 16], P('lon', 'lat', 'mem'), may hold values from 0 to 575
- obs_count: int32 [4, 2, 4], P('lon', 'lat', 'mem'), may hold values from 1 to 16, as said below
- obs_quality: int32 [4, 2, 4, 16], P('lon', 'lat', 'mem'), may hold values from 0 to 3
- obs_values: float32 [4, 2, 4, 16, 128], P('lon', 'lat', 'mem'), may hold values from -6 to 6
Outputs:
- new_controls: float32 [16, 96, 48, 128], P('mem', 'lon', 'lat')
- residual: float32 [4, 2, 4, 16, 128], P('lon', 'lat', 'mem')
Inputs may be any that keep to these rules, and one draw needn't show every extreme that they name: `obs_columns`: column within the owner's tile, numbered as longitude offset times 24 plus latitude offset. `obs_count`: slots from this number on are unused; some owner has exactly 16 live slots.
All inputs are finite; a program needn't handle non-finite values.
Results may differ from a plain program's by a relative error of at most 0.0049.
Values may be sent and summed in bfloat16 or wider, within the bound.
No kernel may reach another device: no remote copies, remote signals or barrier semaphores. Data moves between devices by JAX's collectives and lax.ppermute only.
A program may use at most 64 MiB of HBM per device.

v0:
```python
import jax
import jax.numpy as jnp
from jax import lax
from jax.sharding import PartitionSpec as P

descent = 0.5


def extended_2(x, sides, width):
    for axis, dim in sides:
        peers, length = (lax.axis_size(axis), x.shape[dim])
        up = [(i, (i + 1) % peers) for i in range(peers)]
        down = [(j, i) for i, j in up]
        last = lax.slice_in_dim(x, length - width, length, axis=dim)
        initial = lax.slice_in_dim(x, 0, width, axis=dim)
        before = lax.ppermute(last, axis, up)
        after = lax.ppermute(initial, axis, down)
        x = jnp.concatenate([before, x, after], axis=dim)
    return x


def band_matrix(kernel, row_count, flipped):
    tap_count = kernel.shape[0]
    if flipped:
        kernel = kernel[::-1]
    offset = jnp.arange(row_count + tap_count - 1)[None, :] - jnp.arange(row_count)[:, None]
    chosen = (offset[:, :, None] == jnp.arange(tap_count)[None, None, :]).astype(jnp.float32)
    return jnp.sum(chosen * kernel.astype(jnp.float32), axis=-1).astype(jnp.bfloat16)


def open_edges(extended, rim_width):
    tile_lat = extended.shape[2] - 2 * rim_width
    position = lax.axis_index("lat") * tile_lat + jnp.arange(extended.shape[2]) - rim_width
    inside = (position >= 0) & (position < lax.axis_size("lat") * tile_lat)
    return jnp.where(inside[None, None, :, None], extended, jnp.zeros((), extended.dtype))


def shards(controls, ensemble, taps_lon, taps_lat, obs_columns, obs_count, obs_quality, obs_values):
    tap_count = taps_lon.shape[0]
    rim_width = tap_count // 2
    lon_tile = controls.shape[1]
    lat_tile = controls.shape[2]
    levels = controls.shape[3]
    kernel_lon = taps_lon.astype(jnp.bfloat16)
    kernel_lat = taps_lat.astype(jnp.bfloat16)
    low = controls.astype(jnp.bfloat16)
    extended = extended_2(low, (("lon", 1), ("lat", 2)), rim_width)
    extended = open_edges(extended, rim_width)
    lon_pass = jnp.einsum(
        "ie,mejl->mijl",
        band_matrix(kernel_lon, lon_tile, False),
        extended,
        preferred_element_type=jnp.float32,
    ).astype(jnp.bfloat16)
    spread = jnp.einsum(
        "je,miel->mijl",
        band_matrix(kernel_lat, lat_tile, False),
        lon_pass,
        preferred_element_type=jnp.float32,
    )
    partial_value = jnp.sum(ensemble.astype(jnp.float32) * spread, axis=0)
    flat_part = partial_value.reshape(lon_tile * lat_tile, levels)
    columns = obs_columns[0, 0, 0]
    slot_count = columns.shape[0]
    increment = lax.psum(flat_part, "mem")
    observed = jnp.take(increment, columns, axis=0)
    active = jnp.arange(slot_count) < obs_count[0, 0, 0]
    weights = jnp.where(
        active, 0.5 * obs_quality[0, 0, 0].astype(jnp.float32), jnp.zeros((), jnp.float32)
    )
    residual = weights[:, None] * (observed - obs_values[0, 0, 0])
    empty = jnp.zeros((lon_tile * lat_tile, levels), jnp.float32)
    all_resid, all_columns = (
        lax.all_gather(residual, "mem", axis=0, tiled=True),
        lax.all_gather(columns, "mem", axis=0, tiled=True),
    )
    adjoint = empty.at[all_columns].add(all_resid)
    adjoint = adjoint.reshape(lon_tile, lat_tile, levels)
    product = (ensemble.astype(jnp.float32) * adjoint[None]).astype(jnp.bfloat16)
    extended_back = extended_2(product, (("lon", 1), ("lat", 2)), rim_width)
    extended_back = open_edges(extended_back, rim_width)
    lat_back = jnp.einsum(
        "je,miel->mijl",
        band_matrix(kernel_lat, lat_tile, True),
        extended_back,
        preferred_element_type=jnp.float32,
    ).astype(jnp.bfloat16)
    lon_back = jnp.einsum(
        "ie,mejl->mijl",
        band_matrix(kernel_lon, lon_tile, True),
        lat_back,
        preferred_element_type=jnp.float32,
    )
    new_controls = controls - descent * (controls + lon_back)
    return (new_controls, residual[None, None, None])


def solution(mesh):
    placed = (
        P("mem", "lon", "lat", None),
        P("mem", "lon", "lat", None),
        P(),
        P(),
        P("lon", "lat", "mem", None),
        P("lon", "lat", "mem"),
        P("lon", "lat", "mem", None),
        P("lon", "lat", "mem", None, None),
    )
    return jax.shard_map(
        shards,
        mesh=mesh,
        in_specs=placed,
        out_specs=(P("mem", "lon", "lat", None), P("lon", "lat", "mem", None, None)),
        check_vma=False,
    )
```

profile of v0, /device:TPU:1, one launch (start us, length us, event | category | flops | bytes accessed | tf_op | source)
XLA Modules:
  0.0 102.7 jit_solution(14261250568788644362)
XLA Ops:
  7.3 1.4 %convert_element_type.66 = bf16[4,24,24,128]{3,2,1,0:T(8,128)(2,1)S(1)} convert(f32[4,24,24,128]{3,2,1,0:T(8,128)} %param.8) | non-fusion elementwise | flops 294912 | bytes 1769472 | tf_op jit(solution)/shard_map/convert_element_type | solution.py:46
  8.7 2.2 %collective-permute-start = (bf16[4,8,24,128]{3,2,1,0:T(8,128)(2,1)S(1)}, bf16[4,8,24,128]{3,2,1,0:T(8,128)(2,1)S(1)}, u32[]{:S(2)}, u32[]{:S(2)}) collective-permute-start(bf16[4,8,24,128]{3,2,1,0:T(8,128)(2,1)S(1)} %get-tuple-element.16), channel_id=1, source_target_pairs={{0,8},{8,16},{16,24},{24,0},{1,9},{9,17},{17,25},{25,1},{2,10},{10... | collective-permute-start | bytes 589832 | tf_op jit(solution)/shard_map/ppermute | solution.py:16
  10.8 2.1 %collective-permute-start.1 = (bf16[4,8,24,128]{3,2,1,0:T(8,128)(2,1)S(1)}, bf16[4,8,24,128]{3,2,1,0:T(8,128)(2,1)S(1)}, u32[]{:S(2)}, u32[]{:S(2)}) collective-permute-start(bf16[4,8,24,128]{3,2,1,0:T(8,128)(2,1)S(1)} %get-tuple-element.17), channel_id=1, source_target_pairs={{8,0},{16,8},{24,16},{0,24},{9,1},{17,9},{25,17},{1,25},{10,2},{18... | collective-permute-start | bytes 589832 | tf_op jit(solution)/shard_map/ppermute | solution.py:17
  13.8 0.6 dynamic-slice
  15.2 5.9 %all-reduce = s32[64]{0:T(128)S(1)} all-reduce(s32[64]{0:T(128)S(1)} %bitcast_dynamic-update-slice_fusion), channel_id=2, replica_groups=mesh['lon'=4,'lat'=2,'mem'=4] {'mem'}, use_global_device_ids=true, to_apply=%add | all-reduce | flops 64 | bytes 512 | tf_op jit(solution)/shard_map/all_gather | solution.py:75
  21.5 2.6 %collective-permute-start.2 = (bf16[4,40,8,128]{3,2,1,0:T(8,128)(2,1)S(1)}, bf16[4,40,8,128]{3,2,1,0:T(8,128)(2,1)S(1)}, u32[]{:S(2)}, u32[]{:S(2)}) collective-permute-start(bf16[4,40,8,128]{3,2,1,0:T(8,128)(2,1)S(1)} %get-tuple-element.12), channel_id=1, source_target_pairs={{0,4},{4,0},{1,5},{5,1},{2,6},{6,2},{3,7},{7,3},{8,12},{12,8},{9,1... | collective-permute-start | bytes 983048 | tf_op jit(solution)/shard_map/ppermute | solution.py:16
  24.2 1.2 %collective-permute-done.2 = bf16[4,40,8,128]{3,2,1,0:T(8,128)(2,1)S(1)} collective-permute-done((bf16[4,40,8,128]{3,2,1,0:T(8,128)(2,1)S(1)}, bf16[4,40,8,128]{3,2,1,0:T(8,128)(2,1)S(1)}, u32[]{:S(2)}, u32[]{:S(2)}) %collective-permute-start.2) | collective-permute-done | bytes 327712 | tf_op jit(solution)/shard_map/ppermute | solution.py:16
  25.3 0.5 collective-permute-done.3
  26.6 0.6 copy-done.1
  27.2 1.0 fusion.15
  28.3 41.2 %all-reduce.3.cloned.1.call-done = f32[576,128]{1,0:T(8,128)} async-done(((f32[576,128]{1,0:T(8,128)}), f32[576,128]{1,0:T(8,128)}) %all-reduce.3.cloned.1.call-update) | async-done | bytes 294928 | tf_op jit(solution)/shard_map/psum | solution.py:65
  69.5 1.5 %gather_fusion = f32[16,128]{1,0:T(8,128)S(1)} fusion(f32[576,128]{1,0:T(8,128)} %all-reduce.3.cloned.1.call-done, s32[1024]{0:T(1024)S(1)} %pad_clamp_fusion), kind=kCustom, calls=%fused_computation | custom fusion | bytes 16448 | tf_op jit(solution)/shard_map/jit(_take)/gather | solution.py:66
  71.2 6.1 %all_gather.7 = f32[64,128]{1,0:T(8,128)S(1)} all-gather(f32[16,128]{1,0:T(8,128)S(1)} %fusion.26), channel_id=1, replica_groups=mesh['lon'=4,'lat'=2,'mem'=4] {'mem'}, dimensions={0}, use_global_device_ids=true | all-gather | bytes 40960 | tf_op jit(solution)/shard_map/all_gather | solution.py:74
  77.2 0.9 scatter_custom_fusion
  78.3 1.3 %collective-permute-start.4 = (bf16[4,8,24,128]{3,2,1,0:T(8,128)(2,1)S(1)}, bf16[4,8,24,128]{3,2,1,0:T(8,128)(2,1)S(1)}, u32[]{:S(2)}, u32[]{:S(2)}) collective-permute-start(bf16[4,8,24,128]{3,2,1,0:T(8,128)(2,1)S(1)} %get-tuple-element.14), channel_id=1, source_target_pairs={{0,8},{8,16},{16,24},{24,0},{1,9},{9,17},{17,25},{25,1},{2,10},{10... | collective-permute-start | bytes 589832 | tf_op jit(solution)/shard_map/ppermute | solution.py:16
  79.5 2.1 %collective-permute-start.5 = (bf16[4,8,24,128]{3,2,1,0:T(8,128)(2,1)S(1)}, bf16[4,8,24,128]{3,2,1,0:T(8,128)(2,1)S(1)}, u32[]{:S(2)}, u32[]{:S(2)}) collective-permute-start(bf16[4,8,24,128]{3,2,1,0:T(8,128)(2,1)S(1)} %get-tuple-element.15), channel_id=1, source_target_pairs={{8,0},{16,8},{24,16},{0,24},{9,1},{17,9},{25,17},{1,25},{10,2},{18... | collective-permute-start | bytes 589832 | tf_op jit(solution)/shard_map/ppermute | solution.py:17
  81.6 3.2 %collective-permute-done.4 = bf16[4,8,24,128]{3,2,1,0:T(8,128)(2,1)S(1)} collective-permute-done((bf16[4,8,24,128]{3,2,1,0:T(8,128)(2,1)S(1)}, bf16[4,8,24,128]{3,2,1,0:T(8,128)(2,1)S(1)}, u32[]{:S(2)}, u32[]{:S(2)}) %collective-permute-start.4) | collective-permute-done | bytes 196640 | tf_op jit(solution)/shard_map/ppermute | solution.py:16
  84.8 2.1 %collective-permute-done.5 = bf16[4,8,24,128]{3,2,1,0:T(8,128)(2,1)S(1)} collective-permute-done((bf16[4,8,24,128]{3,2,1,0:T(8,128)(2,1)S(1)}, bf16[4,8,24,128]{3,2,1,0:T(8,128)(2,1)S(1)}, u32[]{:S(2)}, u32[]{:S(2)}) %collective-permute-start.5) | collective-permute-done | bytes 196640 | tf_op jit(solution)/shard_map/ppermute | solution.py:17
  87.0 4.2 %collective-permute-start.6 = (bf16[4,40,8,128]{3,2,1,0:T(8,128)(2,1)S(1)}, bf16[4,40,8,128]{3,2,1,0:T(8,128)(2,1)S(1)}, u32[]{:S(2)}, u32[]{:S(2)}) collective-permute-start(bf16[4,40,8,128]{3,2,1,0:T(8,128)(2,1)S(1)} %get-tuple-element.10), channel_id=1, source_target_pairs={{0,4},{4,0},{1,5},{5,1},{2,6},{6,2},{3,7},{7,3},{8,12},{12,8},{9,1... | collective-permute-start | bytes 983048 | tf_op jit(solution)/shard_map/ppermute | solution.py:16
  91.3 0.7 fusion.25
  92.0 0.5 collective-permute-done.6
  93.0 0.5 fusion
  93.5 0.8 copy-done
  94.6 1.2 %copy.15 = f32[4,24,24,128]{3,2,1,0:T(8,128)} copy(f32[4,24,24,128]{3,1,2,0:T(8,128)S(1)} %fusion.14) | data formatting | bytes 2359296
  (45 shorter events, 2.9 us)
Async XLA Ops:
  7.2 6.7 %copy-start.7 = (u32[32]{0:T(128)S(1)}, u32[32]{0:T(128)}, u32[]{:S(2)}) copy-start(u32[32]{0:T(128)} %constant.50) | copy-start | bytes 388
  7.2 5.8 %copy-start.4 = (f32[17]{0:T(128)S(1)}, f32[17]{0:T(128)}, u32[]{:S(2)}) copy-start(f32[17]{0:T(128)} %param.10) | copy-start | bytes 208
  7.2 5.8 %copy-start.3 = (f32[17]{0:T(128)S(1)}, f32[17]{0:T(128)}, u32[]{:S(2)}) copy-start(f32[17]{0:T(128)} %param.11) | copy-start | bytes 208
  7.2 6.0 %copy-start.5 = (s32[1,1,1,16]{3,2,1,0:T(1,128)S(1)}, s32[1,1,1,16]{3,2,1,0:T(1,128)}, u32[]{:S(2)}) copy-start(s32[1,1,1,16]{3,2,1,0:T(1,128)} %param.12) | copy-start | bytes 196
  7.2 62.3 %all-reduce.3.cloned.1.call-start = ((), (), s32[]{:S(2)}) async-start(), calls=%async_computation | async-start | bytes 589824 | tf_op jit(solution)/shard_map/psum | solution.py:65
  8.7 12.7 %collective-permute-start = (bf16[4,8,24,128]{3,2,1,0:T(8,128)(2,1)S(1)}, bf16[4,8,24,128]{3,2,1,0:T(8,128)(2,1)S(1)}, u32[]{:S(2)}, u32[]{:S(2)}) collective-permute-start(bf16[4,8,24,128]{3,2,1,0:T(8,128)(2,1)S(1)} %get-tuple-element.16), channel_id=1, source_target_pairs={{0,8},{8,16},{16,24},{24,0},{1,9},{9,17},{17,25},{25,1},{2,10},{10... | collective-permute-start | bytes 589832 | tf_op jit(solution)/shard_map/ppermute | solution.py:16
  10.8 10.5 %collective-permute-start.1 = (bf16[4,8,24,128]{3,2,1,0:T(8,128)(2,1)S(1)}, bf16[4,8,24,128]{3,2,1,0:T(8,128)(2,1)S(1)}, u32[]{:S(2)}, u32[]{:S(2)}) collective-permute-start(bf16[4,8,24,128]{3,2,1,0:T(8,128)(2,1)S(1)} %get-tuple-element.17), channel_id=1, source_target_pairs={{8,0},{16,8},{24,16},{0,24},{9,1},{17,9},{25,17},{1,25},{10,2},{18... | collective-permute-start | bytes 589832 | tf_op jit(solution)/shard_map/ppermute | solution.py:17
  21.5 3.9 %collective-permute-start.2 = (bf16[4,40,8,128]{3,2,1,0:T(8,128)(2,1)S(1)}, bf16[4,40,8,128]{3,2,1,0:T(8,128)(2,1)S(1)}, u32[]{:S(2)}, u32[]{:S(2)}) collective-permute-start(bf16[4,40,8,128]{3,2,1,0:T(8,128)(2,1)S(1)} %get-tuple-element.12), channel_id=1, source_target_pairs={{0,4},{4,0},{1,5},{5,1},{2,6},{6,2},{3,7},{7,3},{8,12},{12,8},{9,1... | collective-permute-start | bytes 983048 | tf_op jit(solution)/shard_map/ppermute | solution.py:16
  24.1 1.7 %collective-permute-start.3 = (bf16[4,40,8,128]{3,2,1,0:T(8,128)(2,1)S(1)}, bf16[4,40,8,128]{3,2,1,0:T(8,128)(2,1)S(1)}, u32[]{:S(2)}, u32[]{:S(2)}) collective-permute-start(bf16[4,40,8,128]{3,2,1,0:T(8,128)(2,1)S(1)} %get-tuple-element.13), channel_id=1, source_target_pairs={{4,0},{0,4},{5,1},{1,5},{6,2},{2,6},{7,3},{3,7},{12,8},{8,12},{13,... | collective-permute-start | bytes 983048 | tf_op jit(solution)/shard_map/ppermute | solution.py:17
  26.2 1.1 %copy-start.1 = (bf16[4,24,24,128]{3,2,1,0:T(8,128)(2,1)S(1)}, bf16[4,24,24,128]{3,2,1,0:T(8,128)(2,1)}, u32[]{:S(2)}) copy-start(bf16[4,24,24,128]{3,2,1,0:T(8,128)(2,1)} %param.9) | copy-start | bytes 1769476
  26.6 1.7 %copy-start.6 = (s32[1,1,1,16]{3,2,1,0:T(1,128)S(1)}, s32[1,1,1,16]{3,2,1,0:T(1,128)}, u32[]{:S(2)}) copy-start(s32[1,1,1,16]{3,2,1,0:T(1,128)} %param.14) | copy-start | bytes 196
  26.6 44.5 %copy-start.2 = (f32[1,1,1,16,128]{4,3,2,1,0:T(8,128)S(1)}, f32[1,1,1,16,128]{4,3,2,1,0:T(8,128)}, u32[]{:S(2)}) copy-start(f32[1,1,1,16,128]{4,3,2,1,0:T(8,128)} %param.15) | copy-start | bytes 24580
  78.3 6.5 %collective-permute-start.4 = (bf16[4,8,24,128]{3,2,1,0:T(8,128)(2,1)S(1)}, bf16[4,8,24,128]{3,2,1,0:T(8,128)(2,1)S(1)}, u32[]{:S(2)}, u32[]{:S(2)}) collective-permute-start(bf16[4,8,24,128]{3,2,1,0:T(8,128)(2,1)S(1)} %get-tuple-element.14), channel_id=1, source_target_pairs={{0,8},{8,16},{16,24},{24,0},{1,9},{9,17},{17,25},{25,1},{2,10},{10... | collective-permute-start | bytes 589832 | tf_op jit(solution)/shard_map/ppermute | solution.py:16
  79.5 7.4 %collective-permute-start.5 = (bf16[4,8,24,128]{3,2,1,0:T(8,128)(2,1)S(1)}, bf16[4,8,24,128]{3,2,1,0:T(8,128)(2,1)S(1)}, u32[]{:S(2)}, u32[]{:S(2)}) collective-permute-start(bf16[4,8,24,128]{3,2,1,0:T(8,128)(2,1)S(1)} %get-tuple-element.15), channel_id=1, source_target_pairs={{8,0},{16,8},{24,16},{0,24},{9,1},{17,9},{25,17},{1,25},{10,2},{18... | collective-permute-start | bytes 589832 | tf_op jit(solution)/shard_map/ppermute | solution.py:17
  87.0 5.5 %collective-permute-start.6 = (bf16[4,40,8,128]{3,2,1,0:T(8,128)(2,1)S(1)}, bf16[4,40,8,128]{3,2,1,0:T(8,128)(2,1)S(1)}, u32[]{:S(2)}, u32[]{:S(2)}) collective-permute-start(bf16[4,40,8,128]{3,2,1,0:T(8,128)(2,1)S(1)} %get-tuple-element.10), channel_id=1, source_target_pairs={{0,4},{4,0},{1,5},{5,1},{2,6},{6,2},{3,7},{7,3},{8,12},{12,8},{9,1... | collective-permute-start | bytes 983048 | tf_op jit(solution)/shard_map/ppermute | solution.py:16
  91.3 1.7 %collective-permute-start.7 = (bf16[4,40,8,128]{3,2,1,0:T(8,128)(2,1)S(1)}, bf16[4,40,8,128]{3,2,1,0:T(8,128)(2,1)S(1)}, u32[]{:S(2)}, u32[]{:S(2)}) collective-permute-start(bf16[4,40,8,128]{3,2,1,0:T(8,128)(2,1)S(1)} %get-tuple-element.11), channel_id=1, source_target_pairs={{4,0},{0,4},{5,1},{1,5},{6,2},{2,6},{7,3},{3,7},{12,8},{8,12},{13,... | collective-permute-start | bytes 983048 | tf_op jit(solution)/shard_map/ppermute | solution.py:17
  93.0 1.3 %copy-start = (f32[4,24,24,128]{3,2,1,0:T(8,128)S(1)}, f32[4,24,24,128]{3,2,1,0:T(8,128)}, u32[]{:S(2)}) copy-start(f32[4,24,24,128]{3,2,1,0:T(8,128)} %param.8) | copy-start | bytes 3538948
Sparse Core Ops, SparseCore 0:
  28.4 41.0 all-reduce.2
where the time goes:
time: 103 us
  waiting for transfers between devices  49.2 us (48%)
  between operations  15.6 us (15%)
  starting transfers between devices  14.6 us (14%)
  blocking collectives  12 us (12%)
  local copies, waits for them, and re-layouts  5.14 us (5%)
  other arithmetic  3.93 us (4%)
  matrix products  2.29 us (2%)
    psum x1, waiting for transfers between devices, shards(): increment = lax.psum(flat_part, 'mem')  41.2 us
    ppermute x4, starting transfers between devices, extended_2(): before = lax.ppermute(last, axis, up)  10.3 us
    all_gather x1, blocking collectives, shards(): lax.all_gather(residual, 'mem', axis=0, tiled=True)  6.05 us
    all_gather x1, blocking collectives, shards(): lax.all_gather(columns, 'mem', axis=0, tiled=True)  5.94 us
    ppermute x4, waiting for transfers between devices, extended_2(): before = lax.ppermute(last, axis, up)  4.88 us
    ppermute x4, starting transfers between devices, extended_2(): after = lax.ppermute(initial, axis, down)  4.31 us
    unnamed x20, local copies, waits for them, and re-layouts  3.34 us
    ppermute x4, waiting for transfers between devices, extended_2(): after = lax.ppermute(initial, axis, down)  3.05 us
  transfers between devices with their start and end apart: 9, of which 7 were waited for; matrix products, arithmetic and copies ran while one was open for 2% of the time, Pallas kernels for 0%

commit v1 on v0

v1 whole, which is shorter than its diff:
```python
import functools

import jax
import jax.numpy as jnp
from jax import lax
from jax.experimental import pallas as pl
from jax.experimental.pallas import tpu as pltpu
from jax.sharding import PartitionSpec as P

descent = 0.5
f32 = jnp.float32
bf16 = jnp.bfloat16


def pairings(size, wraps):
    even = [(i, i ^ 1) for i in range(size)]
    odd = []
    for i in range(size):
        j = i + 1 if i % 2 else i - 1
        if wraps:
            j = j % size
        if 0 <= j < size:
            odd.append((i, j))
    return [even, odd] if odd else [even]


def band(distance, taps_ref):
    out = jnp.zeros_like(distance)
    for k in range(taps_ref.shape[0]):
        out = jnp.where(distance == float(k), taps_ref[k], out)
    return out


def fiota(shape, dim):
    return lax.broadcasted_iota(jnp.int32, shape, dim).astype(f32)


def dot(a, b):
    return jnp.dot(a, b, preferred_element_type=f32)


def obs_by_cell(lon_pos, lat_pos, taps_lon, taps_lat, lon_count, lat_count, start):
    slots, rim = lon_pos.shape[0], taps_lon.shape[0] // 2
    wide = 128
    lon_w = band(fiota((slots, wide), 1) + (start + rim) - lon_pos, taps_lon)
    lat_w = band(fiota((slots, wide), 1) + rim - lat_pos, taps_lat)
    cells = lon_count * lat_count
    cell = fiota((wide, cells), 1)
    lon_of = jnp.zeros((wide, cells), f32)
    for t in range(1, lon_count):
        lon_of = lon_of + (cell >= float(t * lat_count)).astype(f32)
    lat_of = cell - lon_of * float(lat_count)
    place = fiota((wide, cells), 0)
    lon_e = dot(lon_w.astype(bf16), (place == lon_of).astype(bf16))
    lat_e = dot(lat_w.astype(bf16), (place == lat_of).astype(bf16))
    return (lon_e * lat_e).astype(bf16)


def cell_by_obs(lon_pos, lat_pos, taps_lon, taps_lat, lon_count, lat_count, start):
    slots, rim = lon_pos.shape[1], taps_lon.shape[0] // 2
    tall = 32
    lon_w = band(fiota((tall, slots), 0) + (start + rim) - lon_pos, taps_lon)
    lat_w = band(fiota((tall, slots), 0) + rim - lat_pos, taps_lat)
    cells = lon_count * lat_count
    lon_of = fiota((lon_count, lat_count, tall), 0).reshape(cells, tall)
    lat_of = fiota((lon_count, lat_count, tall), 1).reshape(cells, tall)
    place = fiota((cells, tall), 1)
    lon_e = dot((place == lon_of).astype(bf16), lon_w.astype(bf16))
    lat_e = dot((place == lat_of).astype(bf16), lat_w.astype(bf16))
    return (lon_e * lat_e).astype(bf16)


def pick_kernel(lat_tile, info_ref, ens_ref, out_ref):
    members, cells, levels = ens_ref.shape
    slots = info_ref.shape[0]
    cell_of = info_ref[:, 0:1] * float(lat_tile) + info_ref[:, 1:2]
    chosen = (fiota((slots, cells), 1) == cell_of).astype(bf16)
    for m in range(members):
        out_ref[:, m * levels:(m + 1) * levels] = dot(chosen, ens_ref[m]).astype(bf16)
    out_ref[:, members * levels:] = info_ref[...].astype(bf16)


def prep_kernel(dims, nbrs, *refs):
    lon_tile, lat_tile, rim = dims
    taps_lon, taps_lat, off_ref, con_ref = refs[:4]
    sets = refs[4:5 + nbrs]
    base_ref, rim1_ref, rim2_ref, turned_ref = refs[5 + nbrs:]
    members, cells, levels = con_ref.shape
    slots = sets[0].shape[0]
    at = members * levels
    for s in range(1 + nbrs):
        lon_pos = sets[s][:, at:at + 128].astype(f32)[:, 0:1]
        lat_pos = sets[s][:, at:at + 128].astype(f32)[:, 1:2]
        if s == 0:
            square = (slots, slots)
            same = lax.broadcasted_iota(jnp.int32, square, 0) == lax.broadcasted_iota(jnp.int32, square, 1)
            turned_ref[...] = jnp.zeros_like(turned_ref)
            turned_ref[0:1, 0:slots] = jnp.sum(jnp.where(same, lon_pos, 0.0), axis=0, keepdims=True)
            turned_ref[1:2, 0:slots] = jnp.sum(jnp.where(same, lat_pos, 0.0), axis=0, keepdims=True)
        else:
            lat_pos = lat_pos + off_ref[1 + s]
        rows = slice(s * slots, (s + 1) * slots)
        weight = obs_by_cell(lon_pos, lat_pos, taps_lon, taps_lat, lon_tile, lat_tile, 0.0)
        for m in range(members):
            base_ref[rows, m * levels:(m + 1) * levels] = dot(weight, con_ref[m].astype(bf16))
        for ref, off in ((rim1_ref, off_ref[0]), (rim2_ref, off_ref[1])):
            ref[rows, :] = obs_by_cell(lon_pos, lat_pos, taps_lon, taps_lat, rim, lat_tile, off)


def part_kernel(nbrs, *refs):
    base_ref, w1_ref, w2_ref, h1_ref, h2_ref = refs[:5]
    sets = refs[5:6 + nbrs]
    outs = refs[6 + nbrs:]
    members, _, levels = h1_ref.shape
    slots = sets[0].shape[0]
    total = [jnp.zeros((slots, levels), f32) for _ in sets]
    for m in range(members):
        lanes = slice(m * levels, (m + 1) * levels)
        spread = base_ref[:, lanes] + dot(w1_ref[...], h1_ref[m]) + dot(w2_ref[...], h2_ref[m])
        for s in range(1 + nbrs):
            total[s] += spread[s * slots:(s + 1) * slots] * sets[s][:, lanes].astype(f32)
    for s in range(1 + nbrs):
        outs[s][...] = total[s]


def resid_kernel(a_ref, b_ref, meta_ref, own_ref, turned_ref, resid_ref, send_ref):
    slots, levels = a_ref.shape
    wide = send_ref.shape[1]
    weight = meta_ref[:, levels + 2:levels + 3]
    resid = weight * (a_ref[...] + b_ref[...] - meta_ref[:, :levels])
    resid_ref[...] = resid
    for m in range(wide // levels):
        lanes = slice(m * levels, (m + 1) * levels)
        send_ref[0:slots, lanes] = (own_ref[:, lanes].astype(f32) * resid).astype(bf16)
    send_ref[slots:, :] = turned_ref[...].astype(bf16)


def back_kernel(dims, count, taps_lon, taps_lat, off_ref, con_ref, *refs):
    lon_tile, lat_tile, lon_step = dims
    sets, out_ref, all_ref = refs[:count], refs[count], refs[count + 1]
    members, block, levels = con_ref.shape
    slots = sets[0].shape[0] - 16
    step = pl.program_id(0)
    lon_pos, lat_pos = [], []
    for s in range(count):
        tail = sets[s][slots:, 0:slots].astype(f32)
        lon_pos.append(tail[0:1] + off_ref[2 * s])
        lat_pos.append(tail[1:2] + off_ref[2 * s + 1])

    @pl.when(step == 0)
    def _():
        for s in range(count):
            all_ref[s * slots:(s + 1) * slots, :] = sets[s][0:slots, :]

    weight = cell_by_obs(
        jnp.concatenate(lon_pos, axis=1), jnp.concatenate(lat_pos, axis=1), taps_lon, taps_lat, lon_step, lat_tile,
        (step * lon_step).astype(f32),
    )
    back = dot(weight, all_ref[...])
    for m in range(members):
        con = con_ref[m]
        out_ref[m] = con - descent * (con + back[:, m * levels:(m + 1) * levels])


def shards(controls, ensemble, taps_lon, taps_lat, obs_columns, obs_count, obs_quality, obs_values):
    rim = taps_lon.shape[0] // 2
    members, lon_tile, lat_tile, levels = controls.shape
    n_slots = obs_columns.shape[-1]
    n_mem = lax.axis_size("mem")
    slots = n_slots * n_mem
    cells = lon_tile * lat_tile
    wide = members * levels
    lon_pairs = pairings(lax.axis_size("lon"), True)
    lat_pairs = pairings(lax.axis_size("lat"), False)
    nbrs = len(lat_pairs)
    mem_bits = [b for b in range(n_mem.bit_length() - 1)]
    lon_even = lax.axis_index("lon") % 2 == 0
    lat_even = lax.axis_index("lat") % 2 == 0
    mem = lax.axis_index("mem")
    vmem = pl.BlockSpec(memory_space=pltpu.VMEM)
    smem = pl.BlockSpec(memory_space=pltpu.SMEM)
    params = pltpu.CompilerParams(vmem_limit_bytes=32 * 1024 * 1024)

    taps_lon = taps_lon.astype(bf16).astype(f32)
    taps_lat = taps_lat.astype(bf16).astype(f32)

    starts = [jnp.where(lon_even, lon_tile - rim, 0), jnp.where(lon_even, 0, lon_tile - rim)]
    rims = [lax.dynamic_slice_in_dim(controls, s, rim, axis=1).astype(bf16).reshape(members, rim * lat_tile, levels) for s in starts]
    halos = [lax.ppermute(r, "lon", p) for r, p in zip(rims, lon_pairs)]
    lon_sign = [jnp.where(lon_even, 1.0, -1.0), jnp.where(lon_even, -1.0, 1.0)]
    lat_sign = [jnp.where(lat_even, 1.0, -1.0), jnp.where(lat_even, -1.0, 1.0)][:nbrs]

    active = jnp.arange(n_slots) < obs_count[0, 0, 0]
    weights = jnp.where(active, 0.5 * obs_quality[0, 0, 0].astype(f32), 0.0)
    columns = obs_columns[0, 0, 0]
    info = jnp.stack([(columns // lat_tile).astype(f32), (columns % lat_tile).astype(f32), weights], axis=1)
    meta = jnp.concatenate([obs_values[0, 0, 0], jnp.pad(info, ((0, 0), (0, 128 - 3)))], axis=1)
    for b in mem_bits:
        other = lax.ppermute(meta, "mem", [(i, i ^ (1 << b)) for i in range(n_mem)])
        upper = (mem >> b) % 2 == 1
        meta = jnp.concatenate([jnp.where(upper, other, meta), jnp.where(upper, meta, other)], axis=0)

    own = pl.pallas_call(
        functools.partial(pick_kernel, lat_tile),
        out_shape=jax.ShapeDtypeStruct((slots, wide + 128), bf16),
        in_specs=[vmem] * 2, out_specs=vmem, compiler_params=params,
    )(meta[:, levels:], ensemble.reshape(members, cells, levels))
    sets = [own] + [lax.ppermute(own, "lat", p) for p in lat_pairs]

    rim_off = [jnp.where(s > 0, float(lon_tile), float(-rim)) for s in lon_sign]
    offs = jnp.stack(rim_off + [s * lat_tile for s in lat_sign])
    total = slots * (1 + nbrs)
    base, w1, w2, turned = pl.pallas_call(
        functools.partial(prep_kernel, (lon_tile, lat_tile, rim), nbrs),
        out_shape=[
            jax.ShapeDtypeStruct((total, wide), f32),
            jax.ShapeDtypeStruct((total, rim * lat_tile), bf16),
            jax.ShapeDtypeStruct((total, rim * lat_tile), bf16),
            jax.ShapeDtypeStruct((16, wide), f32),
        ],
        in_specs=[smem] * 3 + [vmem] * (2 + nbrs), out_specs=[vmem] * 4, compiler_params=params,
    )(taps_lon, taps_lat, offs, controls.reshape(members, cells, levels), *sets)

    parts = pl.pallas_call(
        functools.partial(part_kernel, nbrs),
        out_shape=[jax.ShapeDtypeStruct((slots, levels), f32)] * (1 + nbrs),
        in_specs=[vmem] * (6 + nbrs), out_specs=[vmem] * (1 + nbrs), compiler_params=params,
    )(base, w1, w2, halos[0], halos[1], *sets)
    mine = parts[0]
    for p, q in zip(parts[1:], lat_pairs):
        mine = mine + lax.ppermute(p, "lat", q)
    for b in mem_bits:
        other = lax.ppermute(mine, "mem", [(i, i ^ (1 << b)) for i in range(n_mem)])
        if b + 1 < len(mem_bits):
            mine = mine + other

    resid, send = pl.pallas_call(
        resid_kernel,
        out_shape=[jax.ShapeDtypeStruct((slots, levels), f32), jax.ShapeDtypeStruct((slots + 16, wide), bf16)],
        in_specs=[vmem] * 5, out_specs=[vmem] * 2, compiler_params=params,
    )(mine, other, meta, own, turned)

    row = [send] + [lax.ppermute(send, "lon", p) for p in lon_pairs]
    row_off = [jnp.zeros(())] + [s * lon_tile for s in lon_sign]
    around = list(row)
    around_off = []
    for o in row_off:
        around_off += [o, jnp.zeros(())]
    for q, s in zip(lat_pairs, lat_sign):
        for r, o in zip(row, row_off):
            around.append(lax.ppermute(r, "lat", q))
            around_off += [o, s * lat_tile]
    count = len(around)
    lon_step = 8
    blocks = lon_tile // lon_step
    spec = pl.BlockSpec((members, lon_step * lat_tile, levels), lambda i: (0, i, 0))
    whole = pl.BlockSpec((slots + 16, wide), lambda i: (0, 0))
    new = pl.pallas_call(
        functools.partial(back_kernel, (lon_tile, lat_tile, lon_step), count),
        grid=(blocks,),
        out_shape=jax.ShapeDtypeStruct((members, cells, levels), f32),
        in_specs=[smem] * 3 + [spec] + [whole] * count, out_specs=spec,
        scratch_shapes=[pltpu.VMEM((count * slots, wide), bf16)],
        compiler_params=params,
    )(taps_lon, taps_lat, jnp.stack(around_off).astype(f32), controls.reshape(members, cells, levels), *around)
    mine = lax.dynamic_slice_in_dim(resid, mem * n_slots, n_slots, axis=0)
    return (new.reshape(controls.shape), mine[None, None, None])


def solution(mesh):
    placed = (
        P("mem", "lon", "lat", None),
        P("mem", "lon", "lat", None),
        P(),
        P(),
        P("lon", "lat", "mem", None),
        P("lon", "lat", "mem"),
        P("lon", "lat", "mem", None),
        P("lon", "lat", "mem", None, None),
    )
    return jax.shard_map(
        shards,
        mesh=mesh,
        in_specs=placed,
        out_specs=(P("mem", "lon", "lat", None), P("lon", "lat", "mem", None, None)),
        check_vma=False,
    )
```

time: 103 us -> 41.9 us (0.41)
  waiting for transfers between devices: 49.2 us -> 7.45 us
  between operations: 15.6 us -> 1.47 us
  blocking collectives: 12 us -> 0 us
  starting transfers between devices: 14.6 us -> 20.3 us
  Pallas kernels: 0 us -> 5.53 us
  matrix products: 2.29 us -> 0 us
  local copies, waits for them, and re-layouts: 5.14 us -> 3 us
    psum x1 -> x0, waiting for transfers between devices: 41.2 us -> none  [shards(): increment = lax.psum(flat_part, 'mem')]
    all_gather x2 -> x0, blocking collectives: 12 us -> none  [the longest x1 6.05 us: shards(): lax.all_gather(residual, 'mem', axis=0, tiled=True)]
    ppermute x8 -> x13, starting transfers between devices: 14.6 us -> 20.3 us  [the longest x3 7.37 us: shards(): around.append(lax.ppermute(r, 'lat', q))]
    pallas_call x0 -> x5, Pallas kernels: none -> 5.53 us  [the longest x1 3.26 us: shards(): pl.pallas_call(functools.partial(back_kernel, (lon_tile, lat_tile, lon_st...]
    dot_general x4 -> x0, matrix products: 2.29 us -> none  [the longest x1 1.02 us: shards(): jnp.einsum('je,miel->mijl', band_matrix(kernel_lat, lat_tile, False), lon...]
    unnamed x20 -> x4, local copies, waits for them, and re-layouts: 3.34 us -> 1.07 us
    gather x1 -> x0, local copies, waits for them, and re-layouts: 1.52 us -> none  [shards(): observed = jnp.take(increment, columns, axis=0)]
    convert_element_type x0 -> x1, local copies, waits for them, and re-layouts: none -> 1.17 us  [shards(): lax.dynamic_slice_in_dim(controls, s, rim, axis=1).astype(bf16)]
  transfers between devices with their start and end apart: 9 -> 13, of which waited for: 7 -> 7; matrix products, arithmetic and copies ran while one was open for 2% -> 8% of each run, Pallas kernels for 0% -> 5%
where the time goes in v1:
time: 41.9 us; the launch traced here: 41.3 us
  starting transfers between devices  20.3 us (48%)
  waiting for transfers between devices  7.45 us (18%)
  Pallas kernels  5.53 us (13%)
  other arithmetic  3.53 us (8%)
  local copies, waits for them, and re-layouts  3 us (7%)
  between operations  1.47 us (4%)
    ppermute x3, starting transfers between devices, shards(): around.append(lax.ppermute(r, 'lat', q))  7.37 us
    ppermute x2, waiting for transfers between devices, shards(): other = lax.ppermute(mine, 'mem', [(i, i ^ 1 << b) for i in range(n_mem)])  4.03 us
    ppermute x2, starting transfers between devices, shards(): halos = [lax.ppermute(r, 'lon', p) for r, p in zip(rims, lon_pairs)]  3.56 us
    ppermute x2, starting transfers between devices, shards(): other = lax.ppermute(meta, 'mem', [(i, i ^ 1 << b) for i in range(n_mem)])  3.34 us
    pallas_call x1, Pallas kernels, shards(): pl.pallas_call(functools.partial(back_kernel, (lon_tile, lat_tile, lon_st...  3.26 us
    ppermute x1, starting transfers between devices, shards(): sets = [own] + [lax.ppermute(own, 'lat', p) for p in lat_pairs]  2.73 us
    pallas_call x1, Pallas kernels, shards(): pl.pallas_call(functools.partial(prep_kernel, (lon_tile, lat_tile, rim),...  1.51 us
    ppermute x2, starting transfers between devices, shards(): other = lax.ppermute(mine, 'mem', [(i, i ^ 1 << b) for i in range(n_mem)])  1.49 us
  transfers between devices with their start and end apart: 13, of which 7 were waited for; matrix products, arithmetic and copies ran while one was open for 8% of the time, Pallas kernels for 5%

profile of v1, /device:TPU:1, one launch (start us, length us, event | category | flops | bytes accessed | tf_op | source)
XLA Modules:
  0.0 41.3 jit_solution(17848831236095099860)
XLA Ops:
  1.4 0.7 %fusion.3 = (f32[16,1]{0,1:T(1,128)S(1)}, f32[16,1]{0,1:T(1,128)S(1)}) fusion(s32[1,1,1,16]{3,2,1,0:T(1,128)} %param.12), kind=kLoop, calls=%fused_computation.23 | loop fusion | flops 224 | bytes 192 | tf_op jit(solution)/shard_map/convert_element_type | solution.py:196
  2.1 0.7 %compare_select_fusion = f32[16,1]{0,1:T(1,128)S(1)} fusion(s32[1,1,1,16]{3,2,1,0:T(1,128)} %param.14, s32[]{:T(128)} %bitcast.31), kind=kLoop, calls=%fused_computation.17 | loop fusion | flops 64 | bytes 132 | tf_op jit(solution)/shard_map/jit(_where)/select_n | solution.py:194
  2.8 0.7 %select_maximum_fusion = f32[16,256]{1,0:T(8,128)S(1)} fusion(f32[16,3]{1,0:T(8,128)S(1)} %copy.18, f32[16,128]{1,0:T(8,128)} %bitcast.38), kind=kLoop, calls=%fused_computation.7 | loop fusion | flops 12288 | bytes 24768 | tf_op jit(solution)/shard_map/concatenate | solution.py:197
  3.5 2.0 %collective-permute-start = (f32[16,256]{1,0:T(8,128)S(1)}, f32[16,256]{1,0:T(8,128)S(1)}, u32[]{:S(2)}, u32[]{:S(2)}) collective-permute-start(f32[16,256]{1,0:T(8,128)S(1)} %select_maximum_fusion), channel_id=1, source_target_pairs={{0,1},{1,0},{2,3},{3,2},{4,5},{5,4},{6,7},{7,6},{8,9},{9,8},{10,11... | collective-permute-start | bytes 49160 | tf_op jit(solution)/shard_map/ppermute | solution.py:199
  5.6 1.2 %dynamic-slice_convert_fusion = (bf16[4,8,24,128]{3,2,1,0:T(8,128)(2,1)S(1)}, bf16[4,8,24,128]{3,2,1,0:T(8,128)(2,1)S(1)}) fusion(f32[4,24,24,128]{3,2,1,0:T(8,128)} %param.8, s32[]{:T(128)S(6)} %select_n.127, s32[]{:T(128)S(6)} %select_n.126), kind=kLoop, calls=%fused_computation | loop fusion | bytes 786440 | tf_op jit(solution)/shard_map/convert_element_type | solution.py:188
  6.7 1.4 %collective-permute-start.3 = (bf16[4,192,128]{2,1,0:T(8,128)(2,1)S(1)}, bf16[4,192,128]{2,1,0:T(8,128)(2,1)S(1)}, u32[]{:S(2)}, u32[]{:S(2)}) collective-permute-start(bf16[4,192,128]{2,1,0:T(8,128)(2,1)S(1)} %bitcast.37), channel_id=1, source_target_pairs={{0,8},{8,0},{16,24},{24,16},{1,9},{9,1},{17,25},{25,17},{2,10},{10... | collective-permute-start | bytes 589832 | tf_op jit(solution)/shard_map/ppermute | solution.py:189
  8.1 2.2 %collective-permute-start.4 = (bf16[4,192,128]{2,1,0:T(8,128)(2,1)S(1)}, bf16[4,192,128]{2,1,0:T(8,128)(2,1)S(1)}, u32[]{:S(2)}, u32[]{:S(2)}) collective-permute-start(bf16[4,192,128]{2,1,0:T(8,128)(2,1)S(1)} %bitcast.36), channel_id=1, source_target_pairs={{0,24},{8,16},{16,8},{24,0},{1,25},{9,17},{17,9},{25,1},{2,26},{10... | collective-permute-start | bytes 589832 | tf_op jit(solution)/shard_map/ppermute | solution.py:189
  10.3 0.7 %broadcast_select_fusion.3 = (f32[16,256]{1,0:T(8,128)S(1)}, f32[16,256]{1,0:T(8,128)S(1)}) fusion(f32[16,256]{1,0:T(8,128)S(1)} %collective-permute-done, pred[]{:T(512)S(6)} %eq.22, f32[16,3]{1,0:T(8,128)S(1)} %copy.18, f32[16,128]{1,0:T(8,128)} %bitcast.39), kind=kLoop, calls=%fused_computation.13 | loop fusion | flops 20480 | bytes 57537 | tf_op jit(solution)/shard_map/jit(_where)/select_n | solution.py:201
  11.0 1.3 %collective-permute-start.1 = (f32[32,256]{1,0:T(8,128)S(1)}, f32[32,256]{1,0:T(8,128)S(1)}, u32[]{:S(2)}, u32[]{:S(2)}) collective-permute-start(f32[32,256]{1,0:T(8,128)S(1)} %pad_maximum_fusion.1), channel_id=1, source_target_pairs={{0,2},{1,3},{2,0},{3,1},{4,6},{5,7},{6,4},{7,5},{8,10},{9,11},{10,... | collective-permute-start | bytes 98312 | tf_op jit(solution)/shard_map/ppermute | solution.py:199
  12.3 0.7 %convert_convert_fusion = (f32[17]{0:T(128)S(1)}, f32[17]{0:T(128)S(1)}) fusion(f32[17]{0:T(128)} %param.11, f32[17]{0:T(128)} %param.10), kind=kLoop, calls=%fused_computation.21 | loop fusion | flops 68 | bytes 272 | tf_op jit(solution)/shard_map/convert_element_type | solution.py:185
  13.0 0.9 %collective-permute-done.1 = f32[32,256]{1,0:T(8,128)S(1)} collective-permute-done((f32[32,256]{1,0:T(8,128)S(1)}, f32[32,256]{1,0:T(8,128)S(1)}, u32[]{:S(2)}, u32[]{:S(2)}) %collective-permute-start.1) | collective-permute-done | bytes 32800 | tf_op jit(solution)/shard_map/ppermute | solution.py:199
  13.9 1.1 %copy-done.1 = bf16[4,24,24,128]{3,2,1,0:T(8,128)(2,1)S(1)} copy-done((bf16[4,24,24,128]{3,2,1,0:T(8,128)(2,1)S(1)}, bf16[4,24,24,128]{3,2,1,0:T(8,128)(2,1)}, u32[]{:S(2)}) %copy-start.1) | copy-done | bytes 589848
  15.3 2.7 %collective-permute-start.2 = (bf16[64,640]{1,0:T(8,128)(2,1)S(1)}, bf16[64,640]{1,0:T(8,128)(2,1)S(1)}, u32[]{:S(2)}, u32[]{:S(2)}) collective-permute-start(bf16[64,640]{1,0:T(8,128)(2,1)S(1)} %shard_map.95.refs_4_.refs_5_.own_ref), channel_id=1, source_target_pairs={{0,4},{4,0},{1,5},{5,1},{2,6},{6,2},{3,7},{7,3},{8,12},{12,8},{9,1... | collective-permute-start | bytes 245768 | tf_op jit(solution)/shard_map/ppermute | solution.py:208
  18.1 0.8 %collective-permute-done.2.refs_5_.refs_6_ = bf16[64,640]{1,0:T(8,128)(2,1)S(1)} collective-permute-done((bf16[64,640]{1,0:T(8,128)(2,1)S(1)}, bf16[64,640]{1,0:T(8,128)(2,1)S(1)}, u32[]{:S(2)}, u32[]{:S(2)}) %collective-permute-start.2) | collective-permute-done | bytes 81952 | tf_op jit(solution)/shard_map/ppermute | solution.py:208
  19.0 1.5 %shard_map.96 = (f32[128,512]{1,0:T(8,128)S(1)}, bf16[128,192]{1,0:T(8,128)(2,1)S(1)}, bf16[128,192]{1,0:T(8,128)(2,1)S(1)}, f32[16,512]{1,0:T(8,128)S(1)}) custom-call(f32[17]{0:T(128)S(1)} %get-tuple-element.27.refs_0_.taps_lon, f32[17]{0:T(128)S(1)} %get-tuple-element.26.refs_1_.taps_lat, f32[3]{0:T(128)S(1)} %pad_maximum_fusion.3.refs_2_, ...), custom_call_target="tpu_custom_call" | custom-call | tf_op jit(solution)/shard_map/pallas_call | solution.py:213
  21.2 0.9 %collective-permute-done.5 = f32[64,128]{1,0:T(8,128)S(1)} collective-permute-done((f32[64,128]{1,0:T(8,128)S(1)}, f32[64,128]{1,0:T(8,128)S(1)}, u32[]{:S(2)}, u32[]{:S(2)}) %collective-permute-start.5) | collective-permute-done | bytes 32800 | tf_op jit(solution)/shard_map/ppermute | solution.py:231
  22.3 2.5 %collective-permute-done.6 = f32[64,128]{1,0:T(8,128)S(1)} collective-permute-done((f32[64,128]{1,0:T(8,128)S(1)}, f32[64,128]{1,0:T(8,128)S(1)}, u32[]{:S(2)}, u32[]{:S(2)}) %collective-permute-start.6) | collective-permute-done | bytes 32800 | tf_op jit(solution)/shard_map/ppermute | solution.py:233
  24.9 1.2 %collective-permute-start.7 = (f32[64,128]{1,0:T(8,128)S(1)}, f32[64,128]{1,0:T(8,128)S(1)}, u32[]{:S(2)}, u32[]{:S(2)}) collective-permute-start(f32[64,128]{1,0:T(8,128)S(1)} %add.53.a_ref), channel_id=1, source_target_pairs={{0,2},{1,3},{2,0},{3,1},{4,6},{5,7},{6,4},{7,5},{8,10},{9,11},{10,... | collective-permute-start | bytes 98312 | tf_op jit(solution)/shard_map/ppermute | solution.py:233
  26.1 1.5 %collective-permute-done.7.b_ref = f32[64,128]{1,0:T(8,128)S(1)} collective-permute-done((f32[64,128]{1,0:T(8,128)S(1)}, f32[64,128]{1,0:T(8,128)S(1)}, u32[]{:S(2)}, u32[]{:S(2)}) %collective-permute-start.7) | collective-permute-done | bytes 32800 | tf_op jit(solution)/shard_map/ppermute | solution.py:233
  27.7 1.1 %collective-permute-start.9 = (bf16[80,512]{1,0:T(8,128)(2,1)S(1)}, bf16[80,512]{1,0:T(8,128)(2,1)S(1)}, u32[]{:S(2)}, u32[]{:S(2)}) collective-permute-start(bf16[80,512]{1,0:T(8,128)(2,1)S(1)} %get-tuple-element.16.refs_0_), channel_id=1, source_target_pairs={{0,24},{8,16},{16,8},{24,0},{1,25},{9,17},{17,9},{25,1},{2,26},{10... | collective-permute-start | bytes 245768 | tf_op jit(solution)/shard_map/ppermute | solution.py:243
  29.2 3.3 %collective-permute-start.10 = (bf16[80,512]{1,0:T(8,128)(2,1)S(1)}, bf16[80,512]{1,0:T(8,128)(2,1)S(1)}, u32[]{:S(2)}, u32[]{:S(2)}) collective-permute-start(bf16[80,512]{1,0:T(8,128)(2,1)S(1)} %get-tuple-element.16.refs_0_), channel_id=1, source_target_pairs={{0,4},{4,0},{1,5},{5,1},{2,6},{6,2},{3,7},{7,3},{8,12},{12,8},{9,1... | collective-permute-start | bytes 245768 | tf_op jit(solution)/shard_map/ppermute | solution.py:251
  33.0 3.8 %collective-permute-start.12 = (bf16[80,512]{1,0:T(8,128)(2,1)S(1)}, bf16[80,512]{1,0:T(8,128)(2,1)S(1)}, u32[]{:S(2)}, u32[]{:S(2)}) collective-permute-start(bf16[80,512]{1,0:T(8,128)(2,1)S(1)} %collective-permute-done.9.refs_2_), channel_id=1, source_target_pairs={{0,4},{4,0},{1,5},{5,1},{2,6},{6,2},{3,7},{7,3},{8,12},{12,8},{9,1... | collective-permute-start | bytes 245768 | tf_op jit(solution)/shard_map/ppermute | solution.py:251
  37.1 0.6 %dynamic-slice_bitcast_fusion = f32[1,1,1,16,128]{4,3,2,1,0:T(8,128)} fusion(f32[64,128]{1,0:T(8,128)S(1)} %get-tuple-element.17, s32[]{:T(128)S(6)} %select_n.128), kind=kLoop, calls=%fused_computation.11 | loop fusion | bytes 16388 | tf_op jit(solution)/shard_map/broadcast_in_dim | solution.py:267
  38.1 3.3 %shard_map.99 = f32[4,576,128]{2,1,0:T(8,128)} custom-call(f32[17]{0:T(128)S(1)} %get-tuple-element.27.refs_0_.taps_lon, f32[17]{0:T(128)S(1)} %get-tuple-element.26.refs_1_.taps_lat, f32[12]{0:T(128)S(1)} %stack.35.off_ref, f32[4,576,128]{2,1,0:T(8,128)S(1)} %bitcast.33, bf16[80,512]{1,0:T(8,128)(2,1)S(1)} %get-tuple-element.16.refs_0_, ...), custom_call_target="tpu_custom_call" | custom-call | tf_op jit(solution)/shard_map/pallas_call | solution.py:258
  (29 shorter events, 3.2 us)
Async XLA Ops:
  0.6 18.3 %copy-start = (f32[4,24,24,128]{3,2,1,0:T(8,128)S(1)}, f32[4,24,24,128]{3,2,1,0:T(8,128)}, u32[]{:S(2)}) copy-start(f32[4,24,24,128]{3,2,1,0:T(8,128)} %param.8) | copy-start | bytes 3538948
  3.5 6.8 %collective-permute-start = (f32[16,256]{1,0:T(8,128)S(1)}, f32[16,256]{1,0:T(8,128)S(1)}, u32[]{:S(2)}, u32[]{:S(2)}) collective-permute-start(f32[16,256]{1,0:T(8,128)S(1)} %select_maximum_fusion), channel_id=1, source_target_pairs={{0,1},{1,0},{2,3},{3,2},{4,5},{5,4},{6,7},{7,6},{8,9},{9,8},{10,11... | collective-permute-start | bytes 49160 | tf_op jit(solution)/shard_map/ppermute | solution.py:199
  6.7 13.7 %collective-permute-start.3 = (bf16[4,192,128]{2,1,0:T(8,128)(2,1)S(1)}, bf16[4,192,128]{2,1,0:T(8,128)(2,1)S(1)}, u32[]{:S(2)}, u32[]{:S(2)}) collective-permute-start(bf16[4,192,128]{2,1,0:T(8,128)(2,1)S(1)} %bitcast.37), channel_id=1, source_target_pairs={{0,8},{8,0},{16,24},{24,16},{1,9},{9,1},{17,25},{25,17},{2,10},{10... | collective-permute-start | bytes 589832 | tf_op jit(solution)/shard_map/ppermute | solution.py:189
  8.1 12.4 %collective-permute-start.4 = (bf16[4,192,128]{2,1,0:T(8,128)(2,1)S(1)}, bf16[4,192,128]{2,1,0:T(8,128)(2,1)S(1)}, u32[]{:S(2)}, u32[]{:S(2)}) collective-permute-start(bf16[4,192,128]{2,1,0:T(8,128)(2,1)S(1)} %bitcast.36), channel_id=1, source_target_pairs={{0,24},{8,16},{16,8},{24,0},{1,25},{9,17},{17,9},{25,1},{2,26},{10... | collective-permute-start | bytes 589832 | tf_op jit(solution)/shard_map/ppermute | solution.py:189
  11.0 2.8 %collective-permute-start.1 = (f32[32,256]{1,0:T(8,128)S(1)}, f32[32,256]{1,0:T(8,128)S(1)}, u32[]{:S(2)}, u32[]{:S(2)}) collective-permute-start(f32[32,256]{1,0:T(8,128)S(1)} %pad_maximum_fusion.1), channel_id=1, source_target_pairs={{0,2},{1,3},{2,0},{3,1},{4,6},{5,7},{6,4},{7,5},{8,10},{9,11},{10,... | collective-permute-start | bytes 98312 | tf_op jit(solution)/shard_map/ppermute | solution.py:199
  13.9 1.1 %copy-start.1 = (bf16[4,24,24,128]{3,2,1,0:T(8,128)(2,1)S(1)}, bf16[4,24,24,128]{3,2,1,0:T(8,128)(2,1)}, u32[]{:S(2)}) copy-start(bf16[4,24,24,128]{3,2,1,0:T(8,128)(2,1)} %param.9) | copy-start | bytes 1769476
  15.3 3.7 %collective-permute-start.2 = (bf16[64,640]{1,0:T(8,128)(2,1)S(1)}, bf16[64,640]{1,0:T(8,128)(2,1)S(1)}, u32[]{:S(2)}, u32[]{:S(2)}) collective-permute-start(bf16[64,640]{1,0:T(8,128)(2,1)S(1)} %shard_map.95.refs_4_.refs_5_.own_ref), channel_id=1, source_target_pairs={{0,4},{4,0},{1,5},{5,1},{2,6},{6,2},{3,7},{7,3},{8,12},{12,8},{9,1... | collective-permute-start | bytes 245768 | tf_op jit(solution)/shard_map/ppermute | solution.py:208
  20.8 1.3 %collective-permute-start.5 = (f32[64,128]{1,0:T(8,128)S(1)}, f32[64,128]{1,0:T(8,128)S(1)}, u32[]{:S(2)}, u32[]{:S(2)}) collective-permute-start(f32[64,128]{1,0:T(8,128)S(1)} %get-tuple-element.14), channel_id=1, source_target_pairs={{0,4},{4,0},{1,5},{5,1},{2,6},{6,2},{3,7},{7,3},{8,12},{12,8},{9,1... | collective-permute-start | bytes 98312 | tf_op jit(solution)/shard_map/ppermute | solution.py:231
  22.1 2.8 %collective-permute-start.6 = (f32[64,128]{1,0:T(8,128)S(1)}, f32[64,128]{1,0:T(8,128)S(1)}, u32[]{:S(2)}, u32[]{:S(2)}) collective-permute-start(f32[64,128]{1,0:T(8,128)S(1)} %add.52), channel_id=1, source_target_pairs={{0,1},{1,0},{2,3},{3,2},{4,5},{5,4},{6,7},{7,6},{8,9},{9,8},{10,11... | collective-permute-start | bytes 98312 | tf_op jit(solution)/shard_map/ppermute | solution.py:233
  24.9 2.8 %collective-permute-start.7 = (f32[64,128]{1,0:T(8,128)S(1)}, f32[64,128]{1,0:T(8,128)S(1)}, u32[]{:S(2)}, u32[]{:S(2)}) collective-permute-start(f32[64,128]{1,0:T(8,128)S(1)} %add.53.a_ref), channel_id=1, source_target_pairs={{0,2},{1,3},{2,0},{3,1},{4,6},{5,7},{6,4},{7,5},{8,10},{9,11},{10,... | collective-permute-start | bytes 98312 | tf_op jit(solution)/shard_map/ppermute | solution.py:233
  27.7 5.3 %collective-permute-start.9 = (bf16[80,512]{1,0:T(8,128)(2,1)S(1)}, bf16[80,512]{1,0:T(8,128)(2,1)S(1)}, u32[]{:S(2)}, u32[]{:S(2)}) collective-permute-start(bf16[80,512]{1,0:T(8,128)(2,1)S(1)} %get-tuple-element.16.refs_0_), channel_id=1, source_target_pairs={{0,24},{8,16},{16,8},{24,0},{1,25},{9,17},{17,9},{25,1},{2,26},{10... | collective-permute-start | bytes 245768 | tf_op jit(solution)/shard_map/ppermute | solution.py:243
  28.8 7.9 %collective-permute-start.8 = (bf16[80,512]{1,0:T(8,128)(2,1)S(1)}, bf16[80,512]{1,0:T(8,128)(2,1)S(1)}, u32[]{:S(2)}, u32[]{:S(2)}) collective-permute-start(bf16[80,512]{1,0:T(8,128)(2,1)S(1)} %get-tuple-element.16.refs_0_), channel_id=1, source_target_pairs={{0,8},{8,0},{16,24},{24,16},{1,9},{9,1},{17,25},{25,17},{2,10},{10... | collective-permute-start | bytes 245768 | tf_op jit(solution)/shard_map/ppermute | solution.py:243
  29.2 8.5 %collective-permute-start.10 = (bf16[80,512]{1,0:T(8,128)(2,1)S(1)}, bf16[80,512]{1,0:T(8,128)(2,1)S(1)}, u32[]{:S(2)}, u32[]{:S(2)}) collective-permute-start(bf16[80,512]{1,0:T(8,128)(2,1)S(1)} %get-tuple-element.16.refs_0_), channel_id=1, source_target_pairs={{0,4},{4,0},{1,5},{5,1},{2,6},{6,2},{3,7},{7,3},{8,12},{12,8},{9,1... | collective-permute-start | bytes 245768 | tf_op jit(solution)/shard_map/ppermute | solution.py:251
  33.0 4.7 %collective-permute-start.12 = (bf16[80,512]{1,0:T(8,128)(2,1)S(1)}, bf16[80,512]{1,0:T(8,128)(2,1)S(1)}, u32[]{:S(2)}, u32[]{:S(2)}) collective-permute-start(bf16[80,512]{1,0:T(8,128)(2,1)S(1)} %collective-permute-done.9.refs_2_), channel_id=1, source_target_pairs={{0,4},{4,0},{1,5},{5,1},{2,6},{6,2},{3,7},{7,3},{8,12},{12,8},{9,1... | collective-permute-start | bytes 245768 | tf_op jit(solution)/shard_map/ppermute | solution.py:251
  36.8 1.3 %collective-permute-start.11 = (bf16[80,512]{1,0:T(8,128)(2,1)S(1)}, bf16[80,512]{1,0:T(8,128)(2,1)S(1)}, u32[]{:S(2)}, u32[]{:S(2)}) collective-permute-start(bf16[80,512]{1,0:T(8,128)(2,1)S(1)} %collective-permute-done.8.refs_1_), channel_id=1, source_target_pairs={{0,4},{4,0},{1,5},{5,1},{2,6},{6,2},{3,7},{7,3},{8,12},{12,8},{9,1... | collective-permute-start | bytes 245768 | tf_op jit(solution)/shard_map/ppermute | solution.py:251

commit v2 on v0

v2 whole, which is shorter than its diff:
```python
import functools

import jax
import jax.numpy as jnp
from jax import lax
from jax.experimental import pallas as pl
from jax.experimental.pallas import tpu as pltpu
from jax.sharding import PartitionSpec as P

descent = 0.5
f32 = jnp.float32
bf16 = jnp.bfloat16
tail = 16


def pairings(size, wraps):
    even = [(i, i ^ 1) for i in range(size)]
    odd = []
    for i in range(size):
        j = i + 1 if i % 2 else i - 1
        if wraps:
            j = j % size
        if 0 <= j < size:
            odd.append((i, j))
    return [even, odd] if odd else [even]


def sum_terms(x, count, direct=4):
    if count <= direct:
        return [x] + [lax.ppermute(x, "mem", [(i, i ^ b) for i in range(count)]) for b in range(count - 1, 0, -1)]
    step = 1
    while step < count:
        other = lax.ppermute(x, "mem", [(i, i ^ step) for i in range(count)])
        step *= 2
        if step < count:
            x = x + other
    return [x, other]


def up8(n):
    return (n + 7) // 8 * 8


def signs(axis):
    even = lax.axis_index(axis) % 2 == 0
    return [jnp.where(even, 1.0, -1.0).astype(f32), jnp.where(even, -1.0, 1.0).astype(f32)]


def fiota(shape, dim):
    return lax.broadcasted_iota(jnp.int32, shape, dim).astype(f32)


def diagonal(rows, lanes, shift=0.0):
    return fiota((rows, lanes), 0) + shift == fiota((rows, lanes), 1)


def to_rows(lanes):
    n = lanes.shape[1]
    return jnp.sum(jnp.where(diagonal(n, n), lanes, 0.0), axis=1, keepdims=True)


def to_lanes(rows):
    n = rows.shape[0]
    return jnp.sum(jnp.where(diagonal(n, n), rows, 0.0), axis=0, keepdims=True)


def lane_row(ref, first, blocks, slots):
    if blocks == 1:
        return ref[first:first + 1, 0:slots]
    return jnp.concatenate([ref[first + r:first + r + 1, :] for r in range(blocks)], axis=1)[:, 0:slots]


def band(distance, taps_ref):
    out = jnp.zeros_like(distance)
    for k in range(taps_ref.shape[0]):
        out = jnp.where(distance == float(k), taps_ref[k], out)
    return out


def dot(a, b):
    return jnp.dot(a, b, preferred_element_type=f32)


def params(mib=32):
    return pltpu.CompilerParams(vmem_limit_bytes=mib * 1024 * 1024)


def start_kernel(dims, con_ref, raw_ref, low_ref, rim1_ref, rim2_ref, info_ref):
    edge, lat_tile, n_slots, blocks = dims
    members, cells, levels = con_ref.shape
    mem = lax.axis_index("mem")
    column, quality = raw_ref[:, 0:n_slots], raw_ref[:, n_slots:2 * n_slots]
    count = raw_ref[:, 2 * n_slots:2 * n_slots + 1]
    lon_pos = jnp.floor((column + 0.5) * (1.0 / lat_tile))
    lat_pos = column - lon_pos * float(lat_tile)
    weight = jnp.where(fiota((1, n_slots), 1) < count, 0.5 * quality, 0.0)
    info_ref[...] = jnp.zeros_like(info_ref)
    row = lax.broadcasted_iota(jnp.int32, (tail, levels), 0)
    placed = jnp.zeros((tail, levels), f32)
    for f, lanes in enumerate((lon_pos, lat_pos, weight)):
        rows = to_rows(lanes)
        for r in range(blocks):
            here = diagonal(n_slots, levels, (mem * n_slots - r * levels).astype(f32))
            moved = jnp.sum(jnp.where(here, rows, 0.0), axis=0, keepdims=True)
            info_ref[f * blocks + r:f * blocks + r + 1, :] = moved
            if f < 2:
                placed = jnp.where(row == f * blocks + r, moved, placed)
    placed = placed.astype(bf16)
    even = lax.axis_index("lon") % 2 == 0
    far = cells - edge
    for at, ref in ((jnp.where(even, far, 0), rim1_ref), (jnp.where(even, 0, far), rim2_ref)):
        for m in range(members):
            ref[m * edge:(m + 1) * edge, :] = con_ref[m, pl.ds(pl.multiple_of(at, 16), edge), :].astype(bf16)
        ref[members * edge:, :] = placed
    for m in range(members):
        low_ref[m * cells:(m + 1) * cells, :] = con_ref[m].astype(bf16)
    low_ref[members * cells:, :] = placed


def pick_kernel(lat_tile, blocks, info_ref, ens_ref, out_ref):
    members, cells, levels = ens_ref.shape
    slots = out_ref.shape[0]
    lon_pos = to_rows(lane_row(info_ref, 0, blocks, slots))
    lat_pos = to_rows(lane_row(info_ref, blocks, blocks, slots))
    cell_of = lon_pos * float(lat_tile) + lat_pos
    chosen = (fiota((slots, cells), 1) == cell_of).astype(bf16)
    for m in range(members):
        out_ref[:, m * levels:(m + 1) * levels] = dot(chosen, ens_ref[m]).astype(bf16)


def obs_by_cell(lon_pos, lat_pos, taps_lon, taps_lat, lon_count, lat_count, start):
    slots, rim = lon_pos.shape[0], taps_lon.shape[0] // 2
    wide = 128
    lon_w = band(fiota((slots, wide), 1) + (start + rim) - lon_pos, taps_lon)
    lat_w = band(fiota((slots, wide), 1) + rim - lat_pos, taps_lat)
    cells = lon_count * lat_count
    cell = fiota((wide, cells), 1)
    lon_of = jnp.floor((cell + 0.5) * (1.0 / lat_count))
    lat_of = cell - lon_of * float(lat_count)
    place = fiota((wide, cells), 0)
    lon_e = dot(lon_w.astype(bf16), (place == lon_of).astype(bf16))
    lat_e = dot(lat_w.astype(bf16), (place == lat_of).astype(bf16))
    return (lon_e * lat_e).astype(bf16)


def prep_kernel(dims, taps_lon, taps_lat, info_ref, *refs):
    lon_tile, lat_tile, rim, members, blocks = dims
    count = (len(refs) - 1) // 3
    tiles, base_ref, rims = refs[:count], refs[count], refs[count + 1:]
    slots, levels = base_ref.shape[0], tiles[0].shape[1]
    cells = lon_tile * lat_tile
    lon_pos = to_rows(lane_row(info_ref, 0, blocks, slots))
    lat_pos = to_rows(lane_row(info_ref, blocks, blocks, slots))
    for t, tile in enumerate(tiles):
        here = lat_pos if t == 0 else lat_pos - signs("lat")[t - 1] * float(lat_tile)
        weight = obs_by_cell(lon_pos, here, taps_lon, taps_lat, lon_tile, lat_tile, 0.0)
        for m in range(members):
            part = dot(weight, tile[m * cells:(m + 1) * cells, :])
            lanes = slice(m * levels, (m + 1) * levels)
            base_ref[:, lanes] = part if t == 0 else base_ref[:, lanes] + part
        for side, sign in enumerate(signs("lon")):
            off = jnp.where(sign > 0, float(lon_tile), float(-rim))
            rims[2 * t + side][...] = obs_by_cell(lon_pos, here, taps_lon, taps_lat, rim, lat_tile, off)


def part_kernel(blocks, base_ref, own_ref, values_ref, *refs):
    out_ref = refs[-1]
    count = len(refs) // 5
    tiles, weights, halos = refs[:count - 1], refs[count - 1:3 * count - 1], refs[3 * count - 1:-1]
    n_slots, levels = values_ref.shape
    slots, wide = base_ref.shape
    members = wide // levels
    block = weights[0].shape[1]
    total = jnp.zeros((slots, levels), f32)
    for m in range(members):
        lanes = slice(m * levels, (m + 1) * levels)
        spread = base_ref[:, lanes]
        for w, h in zip(weights, halos):
            spread += dot(w[...], h[m * block:(m + 1) * block, :])
        total += spread * own_ref[:, lanes].astype(f32)
    out_ref[slots:, :] = jnp.zeros((out_ref.shape[0] - slots, levels), f32)
    at = slots
    for t in range(count):
        for ref in (halos[2 * t], halos[2 * t + 1]) + ((tiles[t],) if t < count - 1 else ()):
            rows = ref[...] if ref.shape[0] == tail else ref[members * block:, :]
            out_ref[at:at + 2 * blocks, :] = rows.astype(f32)[0:2 * blocks]
            at += 2 * blocks
    out_ref[0:slots, :] = total
    mine = pl.ds(pl.multiple_of(lax.axis_index("mem") * n_slots, n_slots), n_slots)
    out_ref[mine, :] = out_ref[mine, :] - values_ref[...]


def resid_kernel(blocks, info_ref, own_ref, *refs):
    terms, (resid_ref, send_ref, extra_ref) = refs[:-3], refs[-3:]
    slots, wide = send_ref.shape
    levels = resid_ref.shape[1]
    weight = to_rows(lane_row(info_ref, 2 * blocks, blocks, slots))
    total = terms[0][...]
    for t in terms[1:]:
        total = total + t[...]
    resid = weight * total[0:slots]
    for m in range(wide // levels):
        lanes = slice(m * levels, (m + 1) * levels)
        send_ref[:, lanes] = (own_ref[:, lanes].astype(f32) * resid).astype(bf16)
    resid_ref[...] = resid
    extra_ref[...] = total[slots:]


def weight_kernel(dims, taps_lon, taps_lat, info_ref, extra_ref, resid_ref, out_ref, mine_ref):
    lon_tile, lat_tile, blocks, tiles = dims
    slots, levels = resid_ref.shape
    n_slots = mine_ref.shape[0]
    mine_ref[...] = resid_ref[pl.ds(pl.multiple_of(lax.axis_index("mem") * n_slots, n_slots), n_slots), :]
    rim = taps_lon.shape[0] // 2
    lon_sign, lat_sign = signs("lon"), signs("lat")
    at = 0
    lon_pos, lat_pos = [], []
    for t in range(tiles):
        shift = 0.0 if t == 0 else lat_sign[t - 1] * float(lat_tile)
        beside = []
        for side in range(2):
            beside.append((lane_row(extra_ref, at, blocks, slots) + lon_sign[side] * float(lon_tile), lane_row(extra_ref, at + blocks, blocks, slots)))
            at += 2 * blocks
        if t == 0:
            here = (lane_row(info_ref, 0, blocks, slots), lane_row(info_ref, blocks, blocks, slots))
        else:
            here = after
        if t + 1 < tiles:
            after = (lane_row(extra_ref, at, blocks, slots), lane_row(extra_ref, at + blocks, blocks, slots))
            at += 2 * blocks
        for lon_at, lat_at in [here] + beside:
            lon_pos.append(lon_at)
            lat_pos.append(lat_at + shift)
    lon_pos, lat_pos = jnp.concatenate(lon_pos, axis=1), jnp.concatenate(lat_pos, axis=1)
    tall = 32
    lon_w = band(fiota((tall, lon_pos.shape[1]), 0) + rim - lon_pos, taps_lon)
    lat_w = band(fiota((tall, lat_pos.shape[1]), 0) + rim - lat_pos, taps_lat)
    cells = lon_tile * lat_tile
    lon_of = fiota((lon_tile, lat_tile, tall), 0).reshape(cells, tall)
    lat_of = fiota((lon_tile, lat_tile, tall), 1).reshape(cells, tall)
    place = fiota((cells, tall), 1)
    lon_e = dot((place == lon_of).astype(bf16), lon_w.astype(bf16))
    lat_e = dot((place == lat_of).astype(bf16), lat_w.astype(bf16))
    out_ref[...] = (lon_e * lat_e).astype(bf16)


def back_kernel(weight_ref, con_ref, *refs):
    sets, out_ref, all_ref = refs[:-2], refs[-2], refs[-1]
    members, _, levels = con_ref.shape
    slots = sets[0].shape[0]
    for s, ref in enumerate(sets):
        all_ref[s * slots:(s + 1) * slots, :] = ref[...]
    back = dot(weight_ref[...], all_ref[...])
    for m in range(members):
        con = con_ref[m]
        out_ref[m] = con - descent * (con + back[:, m * levels:(m + 1) * levels])


def shards(controls, ensemble, taps_lon, taps_lat, obs_columns, obs_count, obs_quality, obs_values):
    rim = taps_lon.shape[0] // 2
    members, lon_tile, lat_tile, levels = controls.shape
    n_slots = obs_columns.shape[-1]
    n_mem = lax.axis_size("mem")
    slots = n_slots * n_mem
    blocks = (slots + levels - 1) // levels
    cells = lon_tile * lat_tile
    edge = rim * lat_tile
    wide = members * levels
    lon_pairs = pairings(lax.axis_size("lon"), True)
    lat_pairs = pairings(lax.axis_size("lat"), False)
    vmem = pl.BlockSpec(memory_space=pltpu.VMEM)
    smem = pl.BlockSpec(memory_space=pltpu.SMEM)
    shape = jax.ShapeDtypeStruct
    taps_lon = taps_lon.astype(bf16).astype(f32)
    taps_lat = taps_lat.astype(bf16).astype(f32)
    flat = controls.reshape(members, cells, levels)

    lanes = -(-(2 * n_slots + 1) // 128) * 128
    lane = lax.broadcasted_iota(jnp.int32, (1, 1, 1, lanes), 3)
    zeros = ((0, 0),) * 3
    raw = jnp.where(lane == 2 * n_slots, lax.broadcast_in_dim(obs_count, lane.shape, (0, 1, 2)), 0)
    raw += jnp.pad(obs_columns, zeros + ((0, lanes - n_slots),))
    raw += jnp.pad(obs_quality, zeros + ((n_slots, lanes - 2 * n_slots),))
    raw = raw.astype(f32).reshape(1, lanes)
    low, rim1, rim2, info = pl.pallas_call(
        functools.partial(start_kernel, (edge, lat_tile, n_slots, blocks)),
        out_shape=[shape((members * cells + tail, levels), bf16)] + [shape((members * edge + tail, levels), bf16)] * 2
        + [shape((up8(3 * blocks), levels), f32)],
        in_specs=[vmem] * 2, out_specs=[vmem] * 4, compiler_params=params(),
    )(flat, raw)
    halos = [lax.ppermute(r, "lon", p) for r, p in zip((rim1, rim2), lon_pairs)]
    tiles = [low] + [lax.ppermute(low, "lat", p) for p in lat_pairs]
    info = sum(sum_terms(info, n_mem, 2))
    n_rims = 2 * len(tiles)

    own = pl.pallas_call(
        functools.partial(pick_kernel, lat_tile, blocks),
        out_shape=shape((slots, wide), bf16),
        in_specs=[vmem] * 2, out_specs=vmem, compiler_params=params(),
    )(info, ensemble.reshape(members, cells, levels))
    base, *weights = pl.pallas_call(
        functools.partial(prep_kernel, (lon_tile, lat_tile, rim, members, blocks)),
        out_shape=[shape((slots, wide), f32)] + [shape((slots, edge), bf16)] * n_rims,
        in_specs=[smem] * 2 + [vmem] * (1 + len(tiles)), out_specs=[vmem] * (1 + n_rims), compiler_params=params(),
    )(taps_lon, taps_lat, info, *tiles)

    rims = list(halos)
    for p in lat_pairs:
        rims += [lax.ppermute(h, "lat", p) for h in halos]

    tall = slots + up8(2 * blocks * (3 * len(tiles) - 1))
    tails = [t[members * cells:] for t in tiles[1:]]
    mine = pl.pallas_call(
        functools.partial(part_kernel, blocks),
        out_shape=shape((tall, levels), f32),
        in_specs=[vmem] * (3 + len(tails) + 2 * len(rims)), out_specs=vmem, compiler_params=params(),
    )(base, own, obs_values.reshape(n_slots, levels), *tails, *weights, *rims)
    terms = sum_terms(mine, n_mem)

    resid, send, extra = pl.pallas_call(
        functools.partial(resid_kernel, blocks),
        out_shape=[shape((slots, levels), f32), shape((slots, wide), bf16), shape((tall - slots, levels), f32)],
        in_specs=[vmem] * (2 + len(terms)), out_specs=[vmem] * 3, compiler_params=params(),
    )(info, own, *terms)

    row = [send] + [lax.ppermute(send, "lon", p) for p in lon_pairs]
    count = len(row) * len(tiles)
    weight, resid = pl.pallas_call(
        functools.partial(weight_kernel, (lon_tile, lat_tile, blocks, len(tiles))),
        out_shape=[shape((cells, count * slots), bf16), shape((n_slots, levels), f32)],
        in_specs=[smem] * 2 + [vmem] * 3, out_specs=[vmem] * 2, compiler_params=params(),
    )(taps_lon, taps_lat, info, extra, resid)
    *late, weight = lax.optimization_barrier((*row[1:], weight))
    around = list(row)
    for q in lat_pairs:
        around += [lax.ppermute(r, "lat", q) for r in [send] + late]
    group = 2 if members % 2 == 0 else 1
    spec = pl.BlockSpec((group, cells, levels), lambda i: (i, 0, 0))
    part = pl.BlockSpec((slots, group * levels), lambda i: (0, i))
    whole = pl.BlockSpec((cells, count * slots), lambda i: (0, 0))
    new = pl.pallas_call(
        back_kernel,
        grid=(members // group,),
        out_shape=shape((members, cells, levels), f32),
        in_specs=[whole, spec] + [part] * count, out_specs=spec,
        scratch_shapes=[pltpu.VMEM((count * slots, group * levels), bf16)],
        compiler_params=params(),
    )(weight, flat, *around)
    return (new.reshape(controls.shape), resid[None, None, None])


def solution(mesh):
    placed = (
        P("mem", "lon", "lat", None),
        P("mem", "lon", "lat", None),
        P(),
        P(),
        P("lon", "lat", "mem", None),
        P("lon", "lat", "mem"),
        P("lon", "lat", "mem", None),
        P("lon", "lat", "mem", None, None),
    )
    return jax.shard_map(
        shards,
        mesh=mesh,
        in_specs=placed,
        out_specs=(P("mem", "lon", "lat", None), P("lon", "lat", "mem", None, None)),
        check_vma=False,
    )
```

time: 103 us -> 38.2 us (0.37)
  waiting for transfers between devices: 49.2 us -> 9.08 us
  between operations: 15.6 us -> 1.44 us
  blocking collectives: 12 us -> 0 us
  Pallas kernels: 0 us -> 5.59 us
  starting transfers between devices: 14.6 us -> 19.7 us
  local copies, waits for them, and re-layouts: 5.14 us -> 1.3 us
  other arithmetic: 3.93 us -> 0.76 us
  matrix products: 2.29 us -> 0 us
    psum x1 -> x0, waiting for transfers between devices: 41.2 us -> none  [shards(): increment = lax.psum(flat_part, 'mem')]
    all_gather x2 -> x0, blocking collectives: 12 us -> none  [the longest x1 6.05 us: shards(): lax.all_gather(residual, 'mem', axis=0, tiled=True)]
    pallas_call x0 -> x7, Pallas kernels: none -> 5.59 us  [the longest x1 1.61 us: shards(): pl.pallas_call(functools.partial(weight_kernel, (lon_tile, lat_tile, bloc...]
    ppermute x8 -> x15, starting transfers between devices: 14.6 us -> 19.7 us  [the longest x2 4.95 us: shards(): halos = [lax.ppermute(r, 'lon', p) for r, p in zip((rim1, rim2), lon_pairs)]]
    dot_general x4 -> x0, matrix products: 2.29 us -> none  [the longest x1 1.02 us: shards(): jnp.einsum('je,miel->mijl', band_matrix(kernel_lat, lat_tile, False), lon...]
    unnamed x20 -> x12, local copies, waits for them, and re-layouts: 3.34 us -> 1.29 us
    gather x1 -> x0, local copies, waits for them, and re-layouts: 1.52 us -> none  [shards(): observed = jnp.take(increment, columns, axis=0)]
    convert_element_type x5 -> x1, other arithmetic: 1.49 us -> 0.01 us  [shards(): taps_lat = taps_lat.astype(bf16).astype(f32)]
  transfers between devices with their start and end apart: 9 -> 15, of which waited for: 7 -> 7; matrix products, arithmetic and copies ran while one was open for 2% -> 0% of each run, Pallas kernels for 0% -> 9%
where the time goes in v2:
time: 38.2 us; the launch traced here: 37.9 us
  starting transfers between devices  19.7 us (52%)
  waiting for transfers between devices  9.08 us (24%)
  Pallas kernels  5.59 us (15%)
  between operations  1.44 us (4%)
  local copies, waits for them, and re-layouts  1.3 us (3%)
  other arithmetic  0.76 us (2%)
    ppermute x2, starting transfers between devices, shards(): halos = [lax.ppermute(r, 'lon', p) for r, p in zip((rim1, rim2), lon_pairs)]  4.95 us
    ppermute x3, starting transfers between devices, shards(): around += [lax.ppermute(r, 'lat', q) for r in [send] + late]  4.1 us
    ppermute x2, waiting for transfers between devices, shards(): halos = [lax.ppermute(r, 'lon', p) for r, p in zip((rim1, rim2), lon_pairs)]  3.68 us
    ppermute x2, starting transfers between devices, shards(): row = [send] + [lax.ppermute(send, 'lon', p) for p in lon_pairs]  2.72 us
    ppermute x3, starting transfers between devices, sum_terms(): lax.ppermute(x, 'mem', [(i, i ^ b) for i in range(count)])  2.71 us
    ppermute x2, starting transfers between devices, shards(): rims += [lax.ppermute(h, 'lat', p) for h in halos]  2.67 us
    ppermute x3, waiting for transfers between devices, sum_terms(): lax.ppermute(x, 'mem', [(i, i ^ b) for i in range(count)])  2.59 us
    ppermute x2, starting transfers between devices, sum_terms(): other = lax.ppermute(x, 'mem', [(i, i ^ step) for i in range(count)])  2.45 us
  transfers between devices with their start and end apart: 15, of which 7 were waited for; matrix products, arithmetic and copies ran while one was open for 0% of the time, Pallas kernels for 9%

profile of v2, /device:TPU:1, one launch (start us, length us, event | category | flops | bytes accessed | tf_op | source)
XLA Modules:
  0.0 37.9 jit_solution(9393035346755353600)
XLA Ops:
  1.3 0.7 %convert_bitcast_fusion.raw_ref = f32[1,128]{1,0:T(1,128)S(1)} fusion(s32[1,1,1,16]{3,2,1,0:T(1,128)} %param.14, s32[1,1,1,16]{3,2,1,0:T(1,128)} %param.12, s32[]{:T(128)} %bitcast.8), kind=kLoop, calls=%fused_computation.5 | loop fusion | flops 640 | bytes 644 | tf_op jit(solution)/shard_map/reshape | solution.py:284
  2.1 1.3 %copy-done = f32[4,24,24,128]{3,2,1,0:T(8,128)S(1)} copy-done((f32[4,24,24,128]{3,2,1,0:T(8,128)S(1)}, f32[4,24,24,128]{3,2,1,0:T(8,128)}, u32[]{:S(2)}) %copy-start) | copy-done | bytes 1179672
  3.6 2.8 %collective-permute-start.3 = (bf16[784,128]{1,0:T(8,128)(2,1)S(1)}, bf16[784,128]{1,0:T(8,128)(2,1)S(1)}, u32[]{:S(2)}, u32[]{:S(2)}) collective-permute-start(bf16[784,128]{1,0:T(8,128)(2,1)S(1)} %get-tuple-element.26), channel_id=1, source_target_pairs={{0,8},{8,0},{16,24},{24,16},{1,9},{9,1},{17,25},{25,17},{2,10},{10... | collective-permute-start | bytes 602120 | tf_op jit(solution)/shard_map/ppermute | solution.py:291
  6.4 2.2 %collective-permute-start.4 = (bf16[784,128]{1,0:T(8,128)(2,1)S(1)}, bf16[784,128]{1,0:T(8,128)(2,1)S(1)}, u32[]{:S(2)}, u32[]{:S(2)}) collective-permute-start(bf16[784,128]{1,0:T(8,128)(2,1)S(1)} %get-tuple-element.27), channel_id=1, source_target_pairs={{0,24},{8,16},{16,8},{24,0},{1,25},{9,17},{17,9},{25,1},{2,26},{10... | collective-permute-start | bytes 602120 | tf_op jit(solution)/shard_map/ppermute | solution.py:291
  8.6 1.2 %collective-permute-start = (f32[8,128]{1,0:T(8,128)S(1)}, f32[8,128]{1,0:T(8,128)S(1)}, u32[]{:S(2)}, u32[]{:S(2)}) collective-permute-start(f32[8,128]{1,0:T(8,128)S(1)} %get-tuple-element.19), channel_id=1, source_target_pairs={{0,1},{1,0},{2,3},{3,2},{4,5},{5,4},{6,7},{7,6},{8,9},{9,8},{10,11... | collective-permute-start | bytes 12296 | tf_op jit(solution)/shard_map/ppermute | solution.py:33
  9.8 1.5 %collective-permute-done = f32[8,128]{1,0:T(8,128)S(1)} collective-permute-done((f32[8,128]{1,0:T(8,128)S(1)}, f32[8,128]{1,0:T(8,128)S(1)}, u32[]{:S(2)}, u32[]{:S(2)}) %collective-permute-start) | collective-permute-done | bytes 4128 | tf_op jit(solution)/shard_map/ppermute | solution.py:33
  11.4 1.2 %collective-permute-start.1 = (f32[8,128]{1,0:T(8,128)S(1)}, f32[8,128]{1,0:T(8,128)S(1)}, u32[]{:S(2)}, u32[]{:S(2)}) collective-permute-start(f32[8,128]{1,0:T(8,128)S(1)} %add.18), channel_id=1, source_target_pairs={{0,2},{1,3},{2,0},{3,1},{4,6},{5,7},{6,4},{7,5},{8,10},{9,11},{10,... | collective-permute-start | bytes 12296 | tf_op jit(solution)/shard_map/ppermute | solution.py:33
  12.6 1.8 %collective-permute-start.5 = (bf16[784,128]{1,0:T(8,128)(2,1)S(1)}, bf16[784,128]{1,0:T(8,128)(2,1)S(1)}, u32[]{:S(2)}, u32[]{:S(2)}) collective-permute-start(bf16[784,128]{1,0:T(8,128)(2,1)S(1)} %collective-permute-done.3.refs_5_), channel_id=1, source_target_pairs={{0,4},{4,0},{1,5},{5,1},{2,6},{6,2},{3,7},{7,3},{8,12},{12,8},{9,1... | collective-permute-start | bytes 602120 | tf_op jit(solution)/shard_map/ppermute | solution.py:309
  14.4 3.7 %collective-permute-done.4.refs_6_ = bf16[784,128]{1,0:T(8,128)(2,1)S(1)} collective-permute-done((bf16[784,128]{1,0:T(8,128)(2,1)S(1)}, bf16[784,128]{1,0:T(8,128)(2,1)S(1)}, u32[]{:S(2)}, u32[]{:S(2)}) %collective-permute-start.4) | collective-permute-done | bytes 200736 | tf_op jit(solution)/shard_map/ppermute | solution.py:291
  18.0 0.9 %collective-permute-start.6 = (bf16[784,128]{1,0:T(8,128)(2,1)S(1)}, bf16[784,128]{1,0:T(8,128)(2,1)S(1)}, u32[]{:S(2)}, u32[]{:S(2)}) collective-permute-start(bf16[784,128]{1,0:T(8,128)(2,1)S(1)} %collective-permute-done.4.refs_6_), channel_id=1, source_target_pairs={{0,4},{4,0},{1,5},{5,1},{2,6},{6,2},{3,7},{7,3},{8,12},{12,8},{9,1... | collective-permute-start | bytes 602120 | tf_op jit(solution)/shard_map/ppermute | solution.py:309
  19.0 0.3 shard_map.99.own_ref
  19.3 1.5 %shard_map.100 = (f32[64,512]{1,0:T(8,128)S(1)}, bf16[64,192]{1,0:T(8,128)(2,1)S(1)}, bf16[64,192]{1,0:T(8,128)(2,1)S(1)}, bf16[64,192]{1,0:T(8,128)(2,1)S(1)}, bf16[64,192]{1,0:T(8,128)(2,1)S(1)}) custom-call(f32[17]{0:T(128)S(1)} %get-tuple-element.37.taps_lon, f32[17]{0:T(128)S(1)} %get-tuple-element.36.taps_lat, f32[8,128]{1,0:T(8,128)S(1)} %add.19.info_ref, ...), custom_call_target="tpu_custom_call" | custom-call | tf_op jit(solution)/shard_map/pallas_call | solution.py:301
  20.8 0.4 %shard_map.101.refs_0_ = f32[80,128]{1,0:T(8,128)S(1)} custom-call(f32[64,512]{1,0:T(8,128)S(1)} %get-tuple-element.21.base_ref, bf16[64,512]{1,0:T(8,128)(2,1)S(1)} %shard_map.99.own_ref, f32[16,128]{1,0:T(8,128)S(1)} %bitcast.12, bf16[16,128]{1,0:T(8,128)(2,1)S(1)} %slice.4.refs_0_, bf16[64,192]{1,0:T(8,128)(2,1)S(1)} %get-tuple-element.22.refs_1_, ...), custom_call_target="tpu_custom_call" | custom-call | tf_op jit(solution)/shard_map/pallas_call | solution.py:313
  21.3 2.2 %collective-permute-start.7 = (f32[80,128]{1,0:T(8,128)S(1)}, f32[80,128]{1,0:T(8,128)S(1)}, u32[]{:S(2)}, u32[]{:S(2)}) collective-permute-start(f32[80,128]{1,0:T(8,128)S(1)} %shard_map.101.refs_0_), channel_id=1, source_target_pairs={{0,3},{1,2},{2,1},{3,0},{4,7},{5,6},{6,5},{7,4},{8,11},{9,10},{10,... | collective-permute-start | bytes 122888 | tf_op jit(solution)/shard_map/ppermute | solution.py:30
  24.0 1.1 %collective-permute-done.7.refs_1_ = f32[80,128]{1,0:T(8,128)S(1)} collective-permute-done((f32[80,128]{1,0:T(8,128)S(1)}, f32[80,128]{1,0:T(8,128)S(1)}, u32[]{:S(2)}, u32[]{:S(2)}) %collective-permute-start.7) | collective-permute-done | bytes 40992 | tf_op jit(solution)/shard_map/ppermute | solution.py:30
  25.1 1.3 %collective-permute-done.8.refs_2_ = f32[80,128]{1,0:T(8,128)S(1)} collective-permute-done((f32[80,128]{1,0:T(8,128)S(1)}, f32[80,128]{1,0:T(8,128)S(1)}, u32[]{:S(2)}, u32[]{:S(2)}) %collective-permute-start.8) | collective-permute-done | bytes 40992 | tf_op jit(solution)/shard_map/ppermute | solution.py:30
  26.7 0.4 collective-permute-start.10
  27.0 2.4 %collective-permute-start.11 = (bf16[64,512]{1,0:T(8,128)(2,1)S(1)}, bf16[64,512]{1,0:T(8,128)(2,1)S(1)}, u32[]{:S(2)}, u32[]{:S(2)}) collective-permute-start(bf16[64,512]{1,0:T(8,128)(2,1)S(1)} %get-tuple-element.28.refs_0_), channel_id=1, source_target_pairs={{0,24},{8,16},{16,8},{24,0},{1,25},{9,17},{17,9},{25,1},{2,26},{10... | collective-permute-start | bytes 196616 | tf_op jit(solution)/shard_map/ppermute | solution.py:326
  29.4 2.3 %collective-permute-start.12 = (bf16[64,512]{1,0:T(8,128)(2,1)S(1)}, bf16[64,512]{1,0:T(8,128)(2,1)S(1)}, u32[]{:S(2)}, u32[]{:S(2)}) collective-permute-start(bf16[64,512]{1,0:T(8,128)(2,1)S(1)} %get-tuple-element.28.refs_0_), channel_id=1, source_target_pairs={{0,4},{4,0},{1,5},{5,1},{2,6},{6,2},{3,7},{7,3},{8,12},{12,8},{9,1... | collective-permute-start | bytes 196616 | tf_op jit(solution)/shard_map/ppermute | solution.py:336
  31.7 1.6 %shard_map.103 = (bf16[576,384]{1,0:T(8,128)(2,1)S(1)}, f32[16,128]{1,0:T(8,128)}) custom-call(f32[17]{0:T(128)S(1)} %get-tuple-element.37.taps_lon, f32[17]{0:T(128)S(1)} %get-tuple-element.36.taps_lat, f32[8,128]{1,0:T(8,128)S(1)} %add.19.info_ref, f32[16,128]{1,0:T(8,128)S(1)} %get-tuple-element.29.extra_ref, f32[64,128]{1,0:T(8,128)S(1)} %get-tuple-element.30.resid_ref), custom_call_target="tpu_custom_call" | custom-call | tf_op jit(solution)/shard_map/pallas_call | solution.py:328
  33.3 1.8 %collective-permute-start.13 = (bf16[64,512]{1,0:T(8,128)(2,1)S(1)}, bf16[64,512]{1,0:T(8,128)(2,1)S(1)}, u32[]{:S(2)}, u32[]{:S(2)}) collective-permute-start(bf16[64,512]{1,0:T(8,128)(2,1)S(1)} %collective-permute-done.10.refs_1_), channel_id=1, source_target_pairs={{0,4},{4,0},{1,5},{5,1},{2,6},{6,2},{3,7},{7,3},{8,12},{12,8},{9,1... | collective-permute-start | bytes 196616 | tf_op jit(solution)/shard_map/ppermute | solution.py:336
  35.1 0.9 %collective-permute-done.13.refs_4_ = bf16[64,512]{1,0:T(8,128)(2,1)S(1)} collective-permute-done((bf16[64,512]{1,0:T(8,128)(2,1)S(1)}, bf16[64,512]{1,0:T(8,128)(2,1)S(1)}, u32[]{:S(2)}, u32[]{:S(2)}) %collective-permute-start.13) | collective-permute-done | bytes 65568 | tf_op jit(solution)/shard_map/ppermute | solution.py:336
  36.0 0.4 collective-permute-done.14.refs_5_
  36.4 1.5 %shard_map.104 = f32[4,576,128]{2,1,0:T(8,128)} custom-call(bf16[576,384]{1,0:T(8,128)(2,1)S(1)} %get-tuple-element.32.weight_ref, f32[4,576,128]{2,1,0:T(8,128)S(1)} %bitcast.10, bf16[64,512]{1,0:T(8,128)(2,1)S(1)} %get-tuple-element.28.refs_0_, bf16[64,512]{1,0:T(8,128)(2,1)S(1)} %collective-permute-done.10.refs_1_, ...), custom_call_target="tpu_custom_call" | custom-call | tf_op jit(solution)/shard_map/pallas_call | solution.py:341
  (30 shorter events, 1.2 us)
Async XLA Ops:
  0.6 18.3 %copy-start.5 = (f32[17]{0:T(128)S(1)}, f32[17]{0:T(128)}, u32[]{:S(2)}) copy-start(f32[17]{0:T(128)} %param.10) | copy-start | bytes 208
  0.6 18.3 %copy-start.4 = (f32[17]{0:T(128)S(1)}, f32[17]{0:T(128)}, u32[]{:S(2)}) copy-start(f32[17]{0:T(128)} %param.11) | copy-start | bytes 208
  2.1 1.3 %copy-start = (f32[4,24,24,128]{3,2,1,0:T(8,128)S(1)}, f32[4,24,24,128]{3,2,1,0:T(8,128)}, u32[]{:S(2)}) copy-start(f32[4,24,24,128]{3,2,1,0:T(8,128)} %param.8) | copy-start | bytes 3538948
  3.3 15.6 %copy-start.2 = (bf16[4,24,24,128]{3,2,1,0:T(8,128)(2,1)S(1)}, bf16[4,24,24,128]{3,2,1,0:T(8,128)(2,1)}, u32[]{:S(2)}) copy-start(bf16[4,24,24,128]{3,2,1,0:T(8,128)(2,1)} %param.9) | copy-start | bytes 1769476
  3.5 17.3 %copy-start.3 = (f32[1,1,1,16,128]{4,3,2,1,0:T(8,128)S(1)}, f32[1,1,1,16,128]{4,3,2,1,0:T(8,128)}, u32[]{:S(2)}) copy-start(f32[1,1,1,16,128]{4,3,2,1,0:T(8,128)} %param.15) | copy-start | bytes 24580
  3.5 15.8 %collective-permute-start.2 = (bf16[2320,128]{1,0:T(8,128)(2,1)S(1)}, bf16[2320,128]{1,0:T(8,128)(2,1)S(1)}, u32[]{:S(2)}, u32[]{:S(2)}) collective-permute-start(bf16[2320,128]{1,0:T(8,128)(2,1)S(1)} %get-tuple-element.20.refs_0_), channel_id=1, source_target_pairs={{0,4},{4,0},{1,5},{5,1},{2,6},{6,2},{3,7},{7,3},{8,12},{12,8},{9,1... | collective-permute-start | bytes 1781768 | tf_op jit(solution)/shard_map/ppermute | solution.py:292
  3.6 9.0 %collective-permute-start.3 = (bf16[784,128]{1,0:T(8,128)(2,1)S(1)}, bf16[784,128]{1,0:T(8,128)(2,1)S(1)}, u32[]{:S(2)}, u32[]{:S(2)}) collective-permute-start(bf16[784,128]{1,0:T(8,128)(2,1)S(1)} %get-tuple-element.26), channel_id=1, source_target_pairs={{0,8},{8,0},{16,24},{24,16},{1,9},{9,1},{17,25},{25,17},{2,10},{10... | collective-permute-start | bytes 602120 | tf_op jit(solution)/shard_map/ppermute | solution.py:291
  6.4 11.6 %collective-permute-start.4 = (bf16[784,128]{1,0:T(8,128)(2,1)S(1)}, bf16[784,128]{1,0:T(8,128)(2,1)S(1)}, u32[]{:S(2)}, u32[]{:S(2)}) collective-permute-start(bf16[784,128]{1,0:T(8,128)(2,1)S(1)} %get-tuple-element.27), channel_id=1, source_target_pairs={{0,24},{8,16},{16,8},{24,0},{1,25},{9,17},{17,9},{25,1},{2,26},{10... | collective-permute-start | bytes 602120 | tf_op jit(solution)/shard_map/ppermute | solution.py:291
  8.6 2.8 %collective-permute-start = (f32[8,128]{1,0:T(8,128)S(1)}, f32[8,128]{1,0:T(8,128)S(1)}, u32[]{:S(2)}, u32[]{:S(2)}) collective-permute-start(f32[8,128]{1,0:T(8,128)S(1)} %get-tuple-element.19), channel_id=1, source_target_pairs={{0,1},{1,0},{2,3},{3,2},{4,5},{5,4},{6,7},{7,6},{8,9},{9,8},{10,11... | collective-permute-start | bytes 12296 | tf_op jit(solution)/shard_map/ppermute | solution.py:33
  11.4 7.6 %collective-permute-start.1 = (f32[8,128]{1,0:T(8,128)S(1)}, f32[8,128]{1,0:T(8,128)S(1)}, u32[]{:S(2)}, u32[]{:S(2)}) collective-permute-start(f32[8,128]{1,0:T(8,128)S(1)} %add.18), channel_id=1, source_target_pairs={{0,2},{1,3},{2,0},{3,1},{4,6},{5,7},{6,4},{7,5},{8,10},{9,11},{10,... | collective-permute-start | bytes 12296 | tf_op jit(solution)/shard_map/ppermute | solution.py:33
  12.6 8.2 %collective-permute-start.5 = (bf16[784,128]{1,0:T(8,128)(2,1)S(1)}, bf16[784,128]{1,0:T(8,128)(2,1)S(1)}, u32[]{:S(2)}, u32[]{:S(2)}) collective-permute-start(bf16[784,128]{1,0:T(8,128)(2,1)S(1)} %collective-permute-done.3.refs_5_), channel_id=1, source_target_pairs={{0,4},{4,0},{1,5},{5,1},{2,6},{6,2},{3,7},{7,3},{8,12},{12,8},{9,1... | collective-permute-start | bytes 602120 | tf_op jit(solution)/shard_map/ppermute | solution.py:309
  18.0 2.8 %collective-permute-start.6 = (bf16[784,128]{1,0:T(8,128)(2,1)S(1)}, bf16[784,128]{1,0:T(8,128)(2,1)S(1)}, u32[]{:S(2)}, u32[]{:S(2)}) collective-permute-start(bf16[784,128]{1,0:T(8,128)(2,1)S(1)} %collective-permute-done.4.refs_6_), channel_id=1, source_target_pairs={{0,4},{4,0},{1,5},{5,1},{2,6},{6,2},{3,7},{7,3},{8,12},{12,8},{9,1... | collective-permute-start | bytes 602120 | tf_op jit(solution)/shard_map/ppermute | solution.py:309
  19.3 17.0 %copy-start.1 = (f32[4,24,24,128]{3,2,1,0:T(8,128)S(1)}, f32[4,24,24,128]{3,2,1,0:T(8,128)}, u32[]{:S(2)}) copy-start(f32[4,24,24,128]{3,2,1,0:T(8,128)} %param.8) | copy-start | bytes 3538948
  21.3 3.8 %collective-permute-start.7 = (f32[80,128]{1,0:T(8,128)S(1)}, f32[80,128]{1,0:T(8,128)S(1)}, u32[]{:S(2)}, u32[]{:S(2)}) collective-permute-start(f32[80,128]{1,0:T(8,128)S(1)} %shard_map.101.refs_0_), channel_id=1, source_target_pairs={{0,3},{1,2},{2,1},{3,0},{4,7},{5,6},{6,5},{7,4},{8,11},{9,10},{10,... | collective-permute-start | bytes 122888 | tf_op jit(solution)/shard_map/ppermute | solution.py:30
  23.5 2.9 %collective-permute-start.8 = (f32[80,128]{1,0:T(8,128)S(1)}, f32[80,128]{1,0:T(8,128)S(1)}, u32[]{:S(2)}, u32[]{:S(2)}) collective-permute-start(f32[80,128]{1,0:T(8,128)S(1)} %shard_map.101.refs_0_), channel_id=1, source_target_pairs={{0,2},{1,3},{2,0},{3,1},{4,6},{5,7},{6,4},{7,5},{8,10},{9,11},{10,... | collective-permute-start | bytes 122888 | tf_op jit(solution)/shard_map/ppermute | solution.py:30
  23.7 2.9 %collective-permute-start.9 = (f32[80,128]{1,0:T(8,128)S(1)}, f32[80,128]{1,0:T(8,128)S(1)}, u32[]{:S(2)}, u32[]{:S(2)}) collective-permute-start(f32[80,128]{1,0:T(8,128)S(1)} %shard_map.101.refs_0_), channel_id=1, source_target_pairs={{0,1},{1,0},{2,3},{3,2},{4,5},{5,4},{6,7},{7,6},{8,9},{9,8},{10,11... | collective-permute-start | bytes 122888 | tf_op jit(solution)/shard_map/ppermute | solution.py:30
  26.7 6.6 %collective-permute-start.10 = (bf16[64,512]{1,0:T(8,128)(2,1)S(1)}, bf16[64,512]{1,0:T(8,128)(2,1)S(1)}, u32[]{:S(2)}, u32[]{:S(2)}) collective-permute-start(bf16[64,512]{1,0:T(8,128)(2,1)S(1)} %get-tuple-element.28.refs_0_), channel_id=1, source_target_pairs={{0,8},{8,0},{16,24},{24,16},{1,9},{9,1},{17,25},{25,17},{2,10},{10... | collective-permute-start | bytes 196616 | tf_op jit(solution)/shard_map/ppermute | solution.py:326
  27.0 6.3 %collective-permute-start.11 = (bf16[64,512]{1,0:T(8,128)(2,1)S(1)}, bf16[64,512]{1,0:T(8,128)(2,1)S(1)}, u32[]{:S(2)}, u32[]{:S(2)}) collective-permute-start(bf16[64,512]{1,0:T(8,128)(2,1)S(1)} %get-tuple-element.28.refs_0_), channel_id=1, source_target_pairs={{0,24},{8,16},{16,8},{24,0},{1,25},{9,17},{17,9},{25,1},{2,26},{10... | collective-permute-start | bytes 196616 | tf_op jit(solution)/shard_map/ppermute | solution.py:326
  29.4 5.7 %collective-permute-start.12 = (bf16[64,512]{1,0:T(8,128)(2,1)S(1)}, bf16[64,512]{1,0:T(8,128)(2,1)S(1)}, u32[]{:S(2)}, u32[]{:S(2)}) collective-permute-start(bf16[64,512]{1,0:T(8,128)(2,1)S(1)} %get-tuple-element.28.refs_0_), channel_id=1, source_target_pairs={{0,4},{4,0},{1,5},{5,1},{2,6},{6,2},{3,7},{7,3},{8,12},{12,8},{9,1... | collective-permute-start | bytes 196616 | tf_op jit(solution)/shard_map/ppermute | solution.py:336
  33.3 2.7 %collective-permute-start.13 = (bf16[64,512]{1,0:T(8,128)(2,1)S(1)}, bf16[64,512]{1,0:T(8,128)(2,1)S(1)}, u32[]{:S(2)}, u32[]{:S(2)}) collective-permute-start(bf16[64,512]{1,0:T(8,128)(2,1)S(1)} %collective-permute-done.10.refs_1_), channel_id=1, source_target_pairs={{0,4},{4,0},{1,5},{5,1},{2,6},{6,2},{3,7},{7,3},{8,12},{12,8},{9,1... | collective-permute-start | bytes 196616 | tf_op jit(solution)/shard_map/ppermute | solution.py:336
  35.1 1.3 %collective-permute-start.14 = (bf16[64,512]{1,0:T(8,128)(2,1)S(1)}, bf16[64,512]{1,0:T(8,128)(2,1)S(1)}, u32[]{:S(2)}, u32[]{:S(2)}) collective-permute-start(bf16[64,512]{1,0:T(8,128)(2,1)S(1)} %collective-permute-done.11.refs_2_), channel_id=1, source_target_pairs={{0,4},{4,0},{1,5},{5,1},{2,6},{6,2},{3,7},{7,3},{8,12},{12,8},{9,1... | collective-permute-start | bytes 196616 | tf_op jit(solution)/shard_map/ppermute | solution.py:336

commit v3 on v2

v3 whole, which is shorter than its diff:
```python
import functools

import jax
import jax.numpy as jnp
from jax import lax
from jax.experimental import pallas as pl
from jax.experimental.pallas import tpu as pltpu
from jax.sharding import PartitionSpec as P

descent = 0.5
f32 = jnp.float32
bf16 = jnp.bfloat16
tail = 16


def pairings(size, wraps):
    even = [(i, i ^ 1) for i in range(size)]
    odd = []
    for i in range(size):
        j = i + 1 if i % 2 else i - 1
        if wraps:
            j = j % size
        if 0 <= j < size:
            odd.append((i, j))
    return [even, odd] if odd else [even]


def sum_terms(x, count):
    if count <= 4:
        return [x] + [lax.ppermute(x, "mem", [(i, i ^ b) for i in range(count)]) for b in range(1, count)]
    step = 1
    while step < count:
        other = lax.ppermute(x, "mem", [(i, i ^ step) for i in range(count)])
        step *= 2
        if step < count:
            x = x + other
    return [x, other]


def up8(n):
    return (n + 7) // 8 * 8


def signs(axis):
    even = lax.axis_index(axis) % 2 == 0
    return [jnp.where(even, 1.0, -1.0).astype(f32), jnp.where(even, -1.0, 1.0).astype(f32)]


def fiota(shape, dim):
    return lax.broadcasted_iota(jnp.int32, shape, dim).astype(f32)


def diagonal(rows, lanes, shift=0.0):
    return fiota((rows, lanes), 0) + shift == fiota((rows, lanes), 1)


def to_rows(lanes):
    n = lanes.shape[1]
    return jnp.sum(jnp.where(diagonal(n, n), lanes, 0.0), axis=1, keepdims=True)


def to_lanes(rows):
    n = rows.shape[0]
    return jnp.sum(jnp.where(diagonal(n, n), rows, 0.0), axis=0, keepdims=True)


def owner_lanes(lanes, first, width):
    here = diagonal(lanes.shape[1], width, first.astype(f32))
    return jnp.sum(jnp.where(here, to_rows(lanes), 0.0), axis=0, keepdims=True)


def lane_row(ref, first, blocks, slots):
    if blocks == 1:
        return ref[first:first + 1, 0:slots]
    return jnp.concatenate([ref[first + r:first + r + 1, :] for r in range(blocks)], axis=1)[:, 0:slots]


def band(distance, taps_ref):
    out = jnp.zeros_like(distance)
    for k in range(taps_ref.shape[0]):
        out = jnp.where(distance == float(k), taps_ref[k], out)
    return out


def dot(a, b):
    return jnp.dot(a, b, preferred_element_type=f32)


def params(mib=32):
    return pltpu.CompilerParams(vmem_limit_bytes=mib * 1024 * 1024)


def start_kernel(dims, con_ref, col_ref, low_ref, rim1_ref, rim2_ref, info_ref, *side_refs):
    rim, lon_tile, lat_tile, blocks = dims
    edge = rim * lat_tile
    members, cells, levels = con_ref.shape
    n_slots = col_ref.shape[1]
    mem = lax.axis_index("mem")
    column = col_ref[...].astype(f32)
    lon_pos = jnp.floor((column + 0.5) * (1.0 / lat_tile))
    lat_pos = column - lon_pos * float(lat_tile)
    info_ref[...] = jnp.zeros_like(info_ref)
    row = lax.broadcasted_iota(jnp.int32, (tail, levels), 0)
    placed = jnp.zeros((tail, levels), f32)
    for f, lanes in enumerate((lon_pos, lat_pos)):
        for r in range(blocks):
            moved = owner_lanes(lanes, mem * n_slots - r * levels, levels)
            info_ref[f * blocks + r:f * blocks + r + 1, :] = moved
            placed = jnp.where(row == f * blocks + r, moved, placed)
    placed = placed.astype(bf16)
    even = lax.axis_index("lon") % 2 == 0
    far = cells - edge
    for at, ref in ((jnp.where(even, far, 0), rim1_ref), (jnp.where(even, 0, far), rim2_ref)):
        for m in range(members):
            ref[m * edge:(m + 1) * edge, :] = con_ref[m, pl.ds(pl.multiple_of(at, 16), edge), :].astype(bf16)
        ref[members * edge:, :] = placed
    for ref, sign in zip(side_refs, signs("lat")):
        at = jnp.where(sign > 0, lat_tile - rim, 0)
        for m in range(members):
            for i in range(0, lon_tile, 2):
                pair = [con_ref[m, pl.ds(pl.multiple_of(at + (i + k) * lat_tile, 8), rim), :] for k in range(2)]
                row_at = (m * lon_tile + i) * rim
                ref[row_at:row_at + 2 * rim, :] = jnp.concatenate(pair, axis=0).astype(bf16)
        ref[members * lon_tile * rim:, :] = placed
    for m in range(members):
        low_ref[m * cells:(m + 1) * cells, :] = con_ref[m].astype(bf16)


def pick_kernel(lat_tile, blocks, info_ref, ens_ref, out_ref):
    members, cells, levels = ens_ref.shape
    slots = out_ref.shape[0]
    lon_pos = to_rows(lane_row(info_ref, 0, blocks, slots))
    lat_pos = to_rows(lane_row(info_ref, blocks, blocks, slots))
    cell_of = lon_pos * float(lat_tile) + lat_pos
    chosen = (fiota((slots, cells), 1) == cell_of).astype(bf16)
    for m in range(members):
        out_ref[:, m * levels:(m + 1) * levels] = dot(chosen, ens_ref[m]).astype(bf16)


def prep_kernel(dims, taps_lon, taps_lat, info_ref, low_ref, *refs):
    lon_tile, lat_tile, rim, members, blocks = dims
    count = (len(refs) - 3) // 3
    sides, base_ref, rims = refs[:count], refs[count], refs[count + 1:]
    slots, levels = base_ref.shape[0], low_ref.shape[1]
    cells, edge, flank = lon_tile * lat_tile, rim * lat_tile, rim * lon_tile
    lon_pos = to_rows(lane_row(info_ref, 0, blocks, slots))
    lat_pos = to_rows(lane_row(info_ref, blocks, blocks, slots))
    lane = fiota((slots, 128), 1)
    lon_w = band(lane - lon_pos, taps_lon).astype(bf16)
    lat_w = band(lane + float(rim - lat_tile) - lat_pos, taps_lat).astype(bf16)
    lon_side = [jnp.where(s > 0, float(lon_tile), float(-rim)) for s in signs("lon")]
    sections = [(cells, 0.0, 0.0, lat_tile)] + [(edge, o, 0.0, lat_tile) for o in lon_side]
    for s in signs("lat")[:count]:
        sections += [(edge, o, s * float(lat_tile), lat_tile) for o in lon_side]
        sections.append((flank, 0.0, jnp.where(s > 0, float(lat_tile), float(-rim)), rim))
    lon_at, lat_at = [], []
    for size, lon_off, lat_off, width in sections:
        cell = fiota((1, -(-size // 128) * 128), 1)
        lon_of = jnp.floor((cell + 0.5) * (1.0 / width))
        lon_at.append(jnp.where(cell < size, lon_of + (lon_off + float(rim)), -1.0))
        lat_at.append(cell - lon_of * float(width) + (lat_off + float(lat_tile)))
    lon_at, lat_at = jnp.concatenate(lon_at, axis=1), jnp.concatenate(lat_at, axis=1)
    place = fiota((128, lon_at.shape[1]), 0)
    lon_e = dot(lon_w[:, 0:64], (place[0:64] == lon_at).astype(bf16))
    lat_e = dot(lat_w, (place == lat_at).astype(bf16))
    weight = (lon_e * lat_e).astype(bf16)
    ends = [0]
    for size, _, _, _ in sections:
        ends.append(ends[-1] + -(-size // 128) * 128)
    pieces = [weight[:, e:e + section[0]] for e, section in zip(ends, sections)]
    for m in range(members):
        part = dot(pieces[0], low_ref[m * cells:(m + 1) * cells, :])
        for t, side in enumerate(sides):
            part += dot(pieces[3 * t + 5], side[m * flank:(m + 1) * flank, :])
        base_ref[:, m * levels:(m + 1) * levels] = part
    kept = pieces[1:3]
    for t in range(count):
        kept += pieces[3 * t + 3:3 * t + 5]
    for ref, piece in zip(rims, kept):
        ref[...] = piece


def part_kernel(blocks, base_ref, own_ref, values_ref, scale_ref, *refs):
    out_ref = refs[-1]
    count = len(refs) // 5
    tiles, weights, halos = refs[:count - 1], refs[count - 1:3 * count - 1], refs[3 * count - 1:-1]
    n_slots, levels = values_ref.shape
    slots, wide = base_ref.shape
    members = wide // levels
    block = weights[0].shape[1]
    total = jnp.zeros((slots, levels), f32)
    for m in range(members):
        lanes = slice(m * levels, (m + 1) * levels)
        spread = base_ref[:, lanes]
        for w, h in zip(weights, halos):
            spread += dot(w[...], h[m * block:(m + 1) * block, :])
        total += spread * own_ref[:, lanes].astype(f32)
    out_ref[slots:, :] = jnp.zeros((out_ref.shape[0] - slots, levels), f32)
    at = slots
    for t in range(count):
        for ref in (halos[2 * t], halos[2 * t + 1]) + ((tiles[t],) if t < count - 1 else ()):
            rows = ref[...] if ref.shape[0] == tail else ref[members * block:, :]
            out_ref[at:at + 2 * blocks, :] = rows.astype(f32)[0:2 * blocks]
            at += 2 * blocks
    mem = lax.axis_index("mem")
    for r in range(blocks):
        out_ref[at + r:at + r + 1, :] = owner_lanes(scale_ref[...], mem * n_slots - r * levels, levels)
    out_ref[0:slots, :] = total
    mine = pl.ds(pl.multiple_of(mem * n_slots, n_slots), n_slots)
    out_ref[mine, :] = out_ref[mine, :] - values_ref[...]


def resid_kernel(blocks, tiles, own_ref, *refs):
    terms, (resid_ref, send_ref, extra_ref) = refs[:-3], refs[-3:]
    slots, wide = send_ref.shape
    levels = resid_ref.shape[1]
    total = terms[0][...]
    for t in terms[1:]:
        total = total + t[...]
    extra_ref[...] = total[slots:]
    resid = to_rows(lane_row(extra_ref, 2 * blocks * (3 * tiles - 1), blocks, slots)) * total[0:slots]
    for m in range(wide // levels):
        lanes = slice(m * levels, (m + 1) * levels)
        send_ref[:, lanes] = (own_ref[:, lanes].astype(f32) * resid).astype(bf16)
    resid_ref[...] = resid


def weight_kernel(dims, taps_lon, taps_lat, info_ref, extra_ref, resid_ref, out_ref, mine_ref):
    lon_tile, lat_tile, blocks, tiles = dims
    slots, levels = resid_ref.shape
    n_slots = mine_ref.shape[0]
    mine_ref[...] = resid_ref[pl.ds(pl.multiple_of(lax.axis_index("mem") * n_slots, n_slots), n_slots), :]
    rim = taps_lon.shape[0] // 2
    lon_sign, lat_sign = signs("lon"), signs("lat")
    at = 0
    lon_pos, lat_pos = [], []
    for t in range(tiles):
        shift = 0.0 if t == 0 else lat_sign[t - 1] * float(lat_tile)
        beside = []
        for side in range(2):
            beside.append((lane_row(extra_ref, at, blocks, slots) + lon_sign[side] * float(lon_tile), lane_row(extra_ref, at + blocks, blocks, slots)))
            at += 2 * blocks
        if t == 0:
            here = (lane_row(info_ref, 0, blocks, slots), lane_row(info_ref, blocks, blocks, slots))
        else:
            here = after
        if t + 1 < tiles:
            after = (lane_row(extra_ref, at, blocks, slots), lane_row(extra_ref, at + blocks, blocks, slots))
            at += 2 * blocks
        for lon_at, lat_at in [here] + beside:
            lon_pos.append(lon_at)
            lat_pos.append(lat_at + shift)
    lon_pos, lat_pos = jnp.concatenate(lon_pos, axis=1), jnp.concatenate(lat_pos, axis=1)
    tall = 32
    lon_w = band(fiota((tall, lon_pos.shape[1]), 0) + rim - lon_pos, taps_lon)
    lat_w = band(fiota((tall, lat_pos.shape[1]), 0) + rim - lat_pos, taps_lat)
    cells = lon_tile * lat_tile
    lon_of = fiota((lon_tile, lat_tile, tall), 0).reshape(cells, tall)
    lat_of = fiota((lon_tile, lat_tile, tall), 1).reshape(cells, tall)
    place = fiota((cells, tall), 1)
    lon_e = dot((place == lon_of).astype(bf16), lon_w.astype(bf16))
    lat_e = dot((place == lat_of).astype(bf16), lat_w.astype(bf16))
    out_ref[...] = (lon_e * lat_e).astype(bf16)


def back_kernel(group, pieces, weight_ref, con_ref, *refs):
    sets, out_hbm, all_ref, buf, sem = refs[:-4], refs[-4], refs[-3], refs[-2], refs[-1]
    members, cells, levels = con_ref.shape
    slots = sets[0].shape[0]
    for s, ref in enumerate(sets):
        all_ref[s * slots:(s + 1) * slots, :] = ref[...]
    step = cells // pieces
    copies = []
    for g in range(members // group):
        back = dot(weight_ref[...], all_ref[:, g * group * levels:(g + 1) * group * levels])
        for k in range(group):
            m = g * group + k
            for p in range(pieces):
                rows = slice(p * step, (p + 1) * step)
                con = con_ref[m, rows, :]
                buf[m, rows, :] = con - descent * (con + back[rows, k * levels:(k + 1) * levels])
                copies.append(pltpu.make_async_copy(buf.at[m, rows], out_hbm.at[m, rows], sem.at[m * pieces + p]))
                copies[-1].start()
    for copy in copies:
        copy.wait()


def shards(controls, ensemble, taps_lon, taps_lat, obs_columns, obs_count, obs_quality, obs_values):
    rim = taps_lon.shape[0] // 2
    members, lon_tile, lat_tile, levels = controls.shape
    n_slots = obs_columns.shape[-1]
    n_mem = lax.axis_size("mem")
    slots = n_slots * n_mem
    blocks = (slots + levels - 1) // levels
    cells = lon_tile * lat_tile
    edge = rim * lat_tile
    wide = members * levels
    lon_pairs = pairings(lax.axis_size("lon"), True)
    lat_pairs = pairings(lax.axis_size("lat"), False)
    vmem = pl.BlockSpec(memory_space=pltpu.VMEM)
    smem = pl.BlockSpec(memory_space=pltpu.SMEM)
    shape = jax.ShapeDtypeStruct
    taps_lon = taps_lon.astype(bf16).astype(f32)
    taps_lat = taps_lat.astype(bf16).astype(f32)
    flat = controls.reshape(members, cells, levels)

    flank = rim * lon_tile
    low, rim1, rim2, info, *sides = pl.pallas_call(
        functools.partial(start_kernel, (rim, lon_tile, lat_tile, blocks)),
        out_shape=[shape((members * cells, levels), bf16)] + [shape((members * edge + tail, levels), bf16)] * 2
        + [shape((up8(2 * blocks), levels), f32)] + [shape((members * flank + tail, levels), bf16)] * len(lat_pairs),
        in_specs=[vmem] * 2, out_specs=[vmem] * (4 + len(lat_pairs)), compiler_params=params(),
    )(flat, obs_columns.reshape(1, n_slots))
    halos = [lax.ppermute(r, "lon", p) for r, p in zip((rim1, rim2), lon_pairs)]
    sides = [lax.ppermute(r, "lat", p) for r, p in zip(sides, lat_pairs)]
    n_tiles = 1 + len(lat_pairs)
    live = lax.broadcasted_iota(jnp.int32, (1, n_slots), 1) < obs_count[0]
    scale = jnp.where(live, 0.5 * obs_quality[0, 0].astype(f32), 0.0)
    info, scale = lax.optimization_barrier((info, scale))
    step = 1
    while step < n_mem:
        info = info + lax.ppermute(info, "mem", [(i, i ^ step) for i in range(n_mem)])
        step *= 2
    n_rims = 2 * n_tiles

    own = pl.pallas_call(
        functools.partial(pick_kernel, lat_tile, blocks),
        out_shape=shape((slots, wide), bf16),
        in_specs=[vmem] * 2, out_specs=vmem, compiler_params=params(),
    )(info, ensemble.reshape(members, cells, levels))
    base, *weights = pl.pallas_call(
        functools.partial(prep_kernel, (lon_tile, lat_tile, rim, members, blocks)),
        out_shape=[shape((slots, wide), f32)] + [shape((slots, edge), bf16)] * n_rims,
        in_specs=[smem] * 2 + [vmem] * (1 + n_tiles), out_specs=[vmem] * (1 + n_rims), compiler_params=params(),
    )(taps_lon, taps_lat, info, low, *sides)

    rims = list(halos)
    for p in lat_pairs:
        rims += [lax.ppermute(h, "lat", p) for h in halos]

    tall = slots + up8(2 * blocks * (3 * n_tiles - 1) + blocks)
    tails = [t[members * flank:] for t in sides]
    mine = pl.pallas_call(
        functools.partial(part_kernel, blocks),
        out_shape=shape((tall, levels), f32),
        in_specs=[vmem] * (4 + len(tails) + 2 * len(rims)), out_specs=vmem, compiler_params=params(),
    )(base, own, obs_values.reshape(n_slots, levels), scale, *tails, *weights, *rims)
    terms = sum_terms(mine, n_mem)

    resid, send, extra = pl.pallas_call(
        functools.partial(resid_kernel, blocks, n_tiles),
        out_shape=[shape((slots, levels), f32), shape((slots, wide), bf16), shape((tall - slots, levels), f32)],
        in_specs=[vmem] * (1 + len(terms)), out_specs=[vmem] * 3, compiler_params=params(),
    )(own, *terms)

    row = [send] + [lax.ppermute(send, "lon", p) for p in lon_pairs]
    count = len(row) * n_tiles
    weight, resid = pl.pallas_call(
        functools.partial(weight_kernel, (lon_tile, lat_tile, blocks, n_tiles)),
        out_shape=[shape((cells, count * slots), bf16), shape((n_slots, levels), f32)],
        in_specs=[smem] * 2 + [vmem] * 3, out_specs=[vmem] * 2, compiler_params=params(),
    )(taps_lon, taps_lat, info, extra, resid)
    row[1], weight = lax.optimization_barrier((row[1], weight))
    around = list(row)
    for q in lat_pairs:
        around += [lax.ppermute(r, "lat", q) for r in row]
    group = 2 if members % 2 == 0 else 1
    pieces = 2
    new = pl.pallas_call(
        functools.partial(back_kernel, group, pieces),
        out_shape=shape((members, cells, levels), f32),
        in_specs=[vmem] * (2 + count), out_specs=pl.BlockSpec(memory_space=pl.ANY),
        scratch_shapes=[
            pltpu.VMEM((count * slots, wide), bf16),
            pltpu.VMEM((members, cells, levels), f32),
            pltpu.SemaphoreType.DMA((members * pieces,)),
        ],
        compiler_params=params(),
    )(weight, flat, *around)
    return (new.reshape(controls.shape), resid[None, None, None])


def solution(mesh):
    placed = (
        P("mem", "lon", "lat", None),
        P("mem", "lon", "lat", None),
        P(),
        P(),
        P("lon", "lat", "mem", None),
        P("lon", "lat", "mem"),
        P("lon", "lat", "mem", None),
        P("lon", "lat", "mem", None, None),
    )
    return jax.shard_map(
        shards,
        mesh=mesh,
        in_specs=placed,
        out_specs=(P("mem", "lon", "lat", None), P("lon", "lat", "mem", None, None)),
        check_vma=False,
    )
```

time: 38.2 us -> 36.4 us (0.953)
  waiting for transfers between devices: 9.08 us -> 5.5 us
  starting transfers between devices: 19.7 us -> 21.9 us
  other arithmetic: 0.76 us -> 0.02 us
  local copies, waits for them, and re-layouts: 1.3 us -> 1.96 us
    ppermute x2, waiting for transfers between devices: 3.68 us -> 1.63 us  [shards(): halos = [lax.ppermute(r, 'lon', p) for r, p in zip((rim1, rim2), lon_pairs)]]
    ppermute x6, waiting for transfers between devices: 2.8 us -> 1.26 us  [the longest x3 1.25 us: shards(): around += [lax.ppermute(r, 'lat', q) for r in row]]
    ppermute x6, starting transfers between devices: 6.67 us -> 8.15 us  [the longest x3 4.09 us: shards(): around += [lax.ppermute(r, 'lat', q) for r in row]]
    ppermute x2, starting transfers between devices: 2.67 us -> 3.98 us  [shards(): rims += [lax.ppermute(h, 'lat', p) for h in halos]]
    reshape x1 -> x0, other arithmetic: 0.75 us -> none  [shards(): raw = raw.astype(f32).reshape(1, lanes)]
    unnamed x12 -> x16, local copies, waits for them, and re-layouts: 1.29 us -> 1.96 us
    ppermute x2, starting transfers between devices: 4.95 us -> 4.39 us  [shards(): halos = [lax.ppermute(r, 'lon', p) for r, p in zip((rim1, rim2), lon_pairs)]]
  transfers between devices with their start and end apart: 15 -> 15, of which waited for: 7 -> 6; matrix products, arithmetic and copies ran while one was open for 0% -> 0% of each run, Pallas kernels for 9% -> 9%
where the time goes in v3:
time: 36.4 us; the launch traced here: 36.1 us
  starting transfers between devices  21.9 us (60%)
  waiting for transfers between devices  5.5 us (15%)
  Pallas kernels  5.25 us (14%)
  local copies, waits for them, and re-layouts  1.96 us (5%)
  between operations  1.44 us (4%)
    ppermute x2, starting transfers between devices, shards(): halos = [lax.ppermute(r, 'lon', p) for r, p in zip((rim1, rim2), lon_pairs)]  4.39 us
    ppermute x3, starting transfers between devices, shards(): around += [lax.ppermute(r, 'lat', q) for r in row]  4.09 us
    ppermute x2, starting transfers between devices, shards(): rims += [lax.ppermute(h, 'lat', p) for h in halos]  3.98 us
    ppermute x2, starting transfers between devices, shards(): row = [send] + [lax.ppermute(send, 'lon', p) for p in lon_pairs]  2.72 us
    ppermute x3, starting transfers between devices, sum_terms(): lax.ppermute(x, 'mem', [(i, i ^ b) for i in range(count)])  2.71 us
    ppermute x3, waiting for transfers between devices, sum_terms(): lax.ppermute(x, 'mem', [(i, i ^ b) for i in range(count)])  2.6 us
    ppermute x2, starting transfers between devices, shards(): lax.ppermute(info, 'mem', [(i, i ^ step) for i in range(n_mem)])  2.54 us
    unnamed x16, local copies, waits for them, and re-layouts  1.96 us
  transfers between devices with their start and end apart: 15, of which 6 were waited for; matrix products, arithmetic and copies ran while one was open for 0% of the time, Pallas kernels for 9%

profile of v3, /device:TPU:1, one launch (start us, length us, event | category | flops | bytes accessed | tf_op | source)
XLA Modules:
  0.0 36.1 jit_solution(17976033434203341123)
XLA Ops:
  0.7 1.3 %copy-done = f32[4,24,24,128]{3,2,1,0:T(8,128)S(1)} copy-done((f32[4,24,24,128]{3,2,1,0:T(8,128)S(1)}, f32[4,24,24,128]{3,2,1,0:T(8,128)}, u32[]{:S(2)}) %copy-start) | copy-done | bytes 1179672
  2.0 0.7 %copy-done.4 = s32[1,1,1,16]{3,2,1,0:T(1,128)S(1)} copy-done((s32[1,1,1,16]{3,2,1,0:T(1,128)S(1)}, s32[1,1,1,16]{3,2,1,0:T(1,128)}, u32[]{:S(2)}) %copy-start.4) | copy-done | bytes 88
  2.7 2.2 %collective-permute-start.3 = (bf16[784,128]{1,0:T(8,128)(2,1)S(1)}, bf16[784,128]{1,0:T(8,128)(2,1)S(1)}, u32[]{:S(2)}, u32[]{:S(2)}) collective-permute-start(bf16[784,128]{1,0:T(8,128)(2,1)S(1)} %get-tuple-element.31), channel_id=1, source_target_pairs={{0,8},{8,0},{16,24},{24,16},{1,9},{9,1},{17,25},{25,17},{2,10},{10... | collective-permute-start | bytes 602120 | tf_op jit(solution)/shard_map/ppermute | solution.py:314
  4.9 2.2 %collective-permute-start.4 = (bf16[784,128]{1,0:T(8,128)(2,1)S(1)}, bf16[784,128]{1,0:T(8,128)(2,1)S(1)}, u32[]{:S(2)}, u32[]{:S(2)}) collective-permute-start(bf16[784,128]{1,0:T(8,128)(2,1)S(1)} %get-tuple-element.32), channel_id=1, source_target_pairs={{0,24},{8,16},{16,8},{24,0},{1,25},{9,17},{17,9},{25,1},{2,26},{10... | collective-permute-start | bytes 602120 | tf_op jit(solution)/shard_map/ppermute | solution.py:314
  7.8 1.3 %collective-permute-start = (f32[8,128]{1,0:T(8,128)S(1)}, f32[8,128]{1,0:T(8,128)S(1)}, u32[]{:S(2)}, u32[]{:S(2)}) collective-permute-start(f32[8,128]{1,0:T(8,128)S(1)} %get-tuple-element.22), channel_id=1, source_target_pairs={{0,1},{1,0},{2,3},{3,2},{4,5},{5,4},{6,7},{7,6},{8,9},{9,8},{10,11... | collective-permute-start | bytes 12296 | tf_op jit(solution)/shard_map/ppermute | solution.py:322
  9.1 1.5 %collective-permute-start.2 = (bf16[784,128]{1,0:T(8,128)(2,1)S(1)}, bf16[784,128]{1,0:T(8,128)(2,1)S(1)}, u32[]{:S(2)}, u32[]{:S(2)}) collective-permute-start(bf16[784,128]{1,0:T(8,128)(2,1)S(1)} %get-tuple-element.24), channel_id=1, source_target_pairs={{0,4},{4,0},{1,5},{5,1},{2,6},{6,2},{3,7},{7,3},{8,12},{12,8},{9,1... | collective-permute-start | bytes 602120 | tf_op jit(solution)/shard_map/ppermute | solution.py:315
  10.6 1.3 %collective-permute-start.1 = (f32[8,128]{1,0:T(8,128)S(1)}, f32[8,128]{1,0:T(8,128)S(1)}, u32[]{:S(2)}, u32[]{:S(2)}) collective-permute-start(f32[8,128]{1,0:T(8,128)S(1)} %add.6), channel_id=1, source_target_pairs={{0,2},{1,3},{2,0},{3,1},{4,6},{5,7},{6,4},{7,5},{8,10},{9,11},{10,... | collective-permute-start | bytes 12296 | tf_op jit(solution)/shard_map/ppermute | solution.py:322
  11.9 2.4 %collective-permute-start.5 = (bf16[784,128]{1,0:T(8,128)(2,1)S(1)}, bf16[784,128]{1,0:T(8,128)(2,1)S(1)}, u32[]{:S(2)}, u32[]{:S(2)}) collective-permute-start(bf16[784,128]{1,0:T(8,128)(2,1)S(1)} %collective-permute-done.3.refs_5_), channel_id=1, source_target_pairs={{0,4},{4,0},{1,5},{5,1},{2,6},{6,2},{3,7},{7,3},{8,12},{12,8},{9,1... | collective-permute-start | bytes 602120 | tf_op jit(solution)/shard_map/ppermute | solution.py:339
  14.2 1.6 %collective-permute-done.4.refs_6_ = bf16[784,128]{1,0:T(8,128)(2,1)S(1)} collective-permute-done((bf16[784,128]{1,0:T(8,128)(2,1)S(1)}, bf16[784,128]{1,0:T(8,128)(2,1)S(1)}, u32[]{:S(2)}, u32[]{:S(2)}) %collective-permute-start.4) | collective-permute-done | bytes 200736 | tf_op jit(solution)/shard_map/ppermute | solution.py:314
  15.9 1.6 %collective-permute-start.6 = (bf16[784,128]{1,0:T(8,128)(2,1)S(1)}, bf16[784,128]{1,0:T(8,128)(2,1)S(1)}, u32[]{:S(2)}, u32[]{:S(2)}) collective-permute-start(bf16[784,128]{1,0:T(8,128)(2,1)S(1)} %collective-permute-done.4.refs_6_), channel_id=1, source_target_pairs={{0,4},{4,0},{1,5},{5,1},{2,6},{6,2},{3,7},{7,3},{8,12},{12,8},{9,1... | collective-permute-start | bytes 602120 | tf_op jit(solution)/shard_map/ppermute | solution.py:339
  17.5 0.3 shard_map.96.own_ref
  17.9 1.2 %shard_map.97 = (f32[64,512]{1,0:T(8,128)S(1)}, bf16[64,192]{1,0:T(8,128)(2,1)S(1)}, bf16[64,192]{1,0:T(8,128)(2,1)S(1)}, bf16[64,192]{1,0:T(8,128)(2,1)S(1)}, bf16[64,192]{1,0:T(8,128)(2,1)S(1)}) custom-call(f32[17]{0:T(128)S(1)} %get-tuple-element.41.taps_lon, f32[17]{0:T(128)S(1)} %get-tuple-element.40.taps_lat, f32[8,128]{1,0:T(8,128)S(1)} %add.7.info_ref, ...), custom_call_target="tpu_custom_call" | custom-call | tf_op jit(solution)/shard_map/pallas_call | solution.py:331
  19.1 0.4 %shard_map.98.refs_0_ = f32[80,128]{1,0:T(8,128)S(1)} custom-call(f32[64,512]{1,0:T(8,128)S(1)} %get-tuple-element.25.base_ref, bf16[64,512]{1,0:T(8,128)(2,1)S(1)} %shard_map.96.own_ref, f32[16,128]{1,0:T(8,128)S(1)} %bitcast.13, f32[1,16]{1,0:T(1,128)S(1)} %compare_select_fusion.scale_ref, bf16[16,128]{1,0:T(8,128)(2,1)S(1)} %slice.4.refs_0_, ...), custom_call_target="tpu_custom_call" | custom-call | tf_op jit(solution)/shard_map/pallas_call | solution.py:343
  19.5 2.2 %collective-permute-start.9 = (f32[80,128]{1,0:T(8,128)S(1)}, f32[80,128]{1,0:T(8,128)S(1)}, u32[]{:S(2)}, u32[]{:S(2)}) collective-permute-start(f32[80,128]{1,0:T(8,128)S(1)} %shard_map.98.refs_0_), channel_id=1, source_target_pairs={{0,3},{1,2},{2,1},{3,0},{4,7},{5,6},{6,5},{7,4},{8,11},{9,10},{10,... | collective-permute-start | bytes 122888 | tf_op jit(solution)/shard_map/ppermute | solution.py:30
  22.2 1.1 %collective-permute-done.9.refs_3_ = f32[80,128]{1,0:T(8,128)S(1)} collective-permute-done((f32[80,128]{1,0:T(8,128)S(1)}, f32[80,128]{1,0:T(8,128)S(1)}, u32[]{:S(2)}, u32[]{:S(2)}) %collective-permute-start.9) | collective-permute-done | bytes 40992 | tf_op jit(solution)/shard_map/ppermute | solution.py:30
  23.3 1.3 %collective-permute-done.8.refs_2_ = f32[80,128]{1,0:T(8,128)S(1)} collective-permute-done((f32[80,128]{1,0:T(8,128)S(1)}, f32[80,128]{1,0:T(8,128)S(1)}, u32[]{:S(2)}, u32[]{:S(2)}) %collective-permute-start.8) | collective-permute-done | bytes 40992 | tf_op jit(solution)/shard_map/ppermute | solution.py:30
  24.9 0.4 collective-permute-start.10
  25.3 2.4 %collective-permute-start.11 = (bf16[64,512]{1,0:T(8,128)(2,1)S(1)}, bf16[64,512]{1,0:T(8,128)(2,1)S(1)}, u32[]{:S(2)}, u32[]{:S(2)}) collective-permute-start(bf16[64,512]{1,0:T(8,128)(2,1)S(1)} %get-tuple-element.33.refs_0_), channel_id=1, source_target_pairs={{0,24},{8,16},{16,8},{24,0},{1,25},{9,17},{17,9},{25,1},{2,26},{10... | collective-permute-start | bytes 196616 | tf_op jit(solution)/shard_map/ppermute | solution.py:356
  27.7 2.3 %collective-permute-start.12 = (bf16[64,512]{1,0:T(8,128)(2,1)S(1)}, bf16[64,512]{1,0:T(8,128)(2,1)S(1)}, u32[]{:S(2)}, u32[]{:S(2)}) collective-permute-start(bf16[64,512]{1,0:T(8,128)(2,1)S(1)} %get-tuple-element.33.refs_0_), channel_id=1, source_target_pairs={{0,4},{4,0},{1,5},{5,1},{2,6},{6,2},{3,7},{7,3},{8,12},{12,8},{9,1... | collective-permute-start | bytes 196616 | tf_op jit(solution)/shard_map/ppermute | solution.py:366
  29.9 1.6 %shard_map.100 = (bf16[576,384]{1,0:T(8,128)(2,1)S(1)}, f32[16,128]{1,0:T(8,128)}) custom-call(f32[17]{0:T(128)S(1)} %get-tuple-element.41.taps_lon, f32[17]{0:T(128)S(1)} %get-tuple-element.40.taps_lat, f32[8,128]{1,0:T(8,128)S(1)} %add.7.info_ref, f32[16,128]{1,0:T(8,128)S(1)} %get-tuple-element.34.extra_ref, f32[64,128]{1,0:T(8,128)S(1)} %get-tuple-element.35.resid_ref), custom_call_target="tpu_custom_call" | custom-call | tf_op jit(solution)/shard_map/pallas_call | solution.py:358
  31.6 1.8 %collective-permute-start.14 = (bf16[64,512]{1,0:T(8,128)(2,1)S(1)}, bf16[64,512]{1,0:T(8,128)(2,1)S(1)}, u32[]{:S(2)}, u32[]{:S(2)}) collective-permute-start(bf16[64,512]{1,0:T(8,128)(2,1)S(1)} %collective-permute-done.11.refs_2_), channel_id=1, source_target_pairs={{0,4},{4,0},{1,5},{5,1},{2,6},{6,2},{3,7},{7,3},{8,12},{12,8},{9,1... | collective-permute-start | bytes 196616 | tf_op jit(solution)/shard_map/ppermute | solution.py:366
  33.4 0.9 %collective-permute-done.14.refs_5_ = bf16[64,512]{1,0:T(8,128)(2,1)S(1)} collective-permute-done((bf16[64,512]{1,0:T(8,128)(2,1)S(1)}, bf16[64,512]{1,0:T(8,128)(2,1)S(1)}, u32[]{:S(2)}, u32[]{:S(2)}) %collective-permute-start.14) | collective-permute-done | bytes 65568 | tf_op jit(solution)/shard_map/ppermute | solution.py:366
  34.3 0.4 collective-permute-done.13.refs_4_
  34.6 1.5 %shard_map.101 = f32[4,576,128]{2,1,0:T(8,128)} custom-call(bf16[576,384]{1,0:T(8,128)(2,1)S(1)} %get-tuple-element.37.weight_ref, f32[4,576,128]{2,1,0:T(8,128)S(1)} %bitcast.11, bf16[64,512]{1,0:T(8,128)(2,1)S(1)} %get-tuple-element.33.refs_0_, bf16[64,512]{1,0:T(8,128)(2,1)S(1)} %collective-permute-done.10.refs_1_, ...), custom_call_target="tpu_custom_call" | custom-call | tf_op jit(solution)/shard_map/pallas_call | solution.py:369
  (34 shorter events, 1.0 us)
Async XLA Ops:
  0.6 7.2 %copy-start.7 = (s32[1,1,1,16]{3,2,1,0:T(1,128)S(1)}, s32[1,1,1,16]{3,2,1,0:T(1,128)}, u32[]{:S(2)}) copy-start(s32[1,1,1,16]{3,2,1,0:T(1,128)} %param.14) | copy-start | bytes 196
  0.6 16.8 %copy-start.5 = (f32[17]{0:T(128)S(1)}, f32[17]{0:T(128)}, u32[]{:S(2)}) copy-start(f32[17]{0:T(128)} %param.11) | copy-start | bytes 208
  0.7 16.8 %copy-start.6 = (f32[17]{0:T(128)S(1)}, f32[17]{0:T(128)}, u32[]{:S(2)}) copy-start(f32[17]{0:T(128)} %param.10) | copy-start | bytes 208
  0.7 1.3 %copy-start = (f32[4,24,24,128]{3,2,1,0:T(8,128)S(1)}, f32[4,24,24,128]{3,2,1,0:T(8,128)}, u32[]{:S(2)}) copy-start(f32[4,24,24,128]{3,2,1,0:T(8,128)} %param.8) | copy-start | bytes 3538948
  2.0 0.7 %copy-start.4 = (s32[1,1,1,16]{3,2,1,0:T(1,128)S(1)}, s32[1,1,1,16]{3,2,1,0:T(1,128)}, u32[]{:S(2)}) copy-start(s32[1,1,1,16]{3,2,1,0:T(1,128)} %param.12) | copy-start | bytes 196
  2.6 14.9 %copy-start.2 = (bf16[4,24,24,128]{3,2,1,0:T(8,128)(2,1)S(1)}, bf16[4,24,24,128]{3,2,1,0:T(8,128)(2,1)}, u32[]{:S(2)}) copy-start(bf16[4,24,24,128]{3,2,1,0:T(8,128)(2,1)} %param.9) | copy-start | bytes 1769476
  2.6 16.5 %copy-start.3 = (f32[1,1,1,16,128]{4,3,2,1,0:T(8,128)S(1)}, f32[1,1,1,16,128]{4,3,2,1,0:T(8,128)}, u32[]{:S(2)}) copy-start(f32[1,1,1,16,128]{4,3,2,1,0:T(8,128)} %param.15) | copy-start | bytes 24580
  2.7 9.1 %collective-permute-start.3 = (bf16[784,128]{1,0:T(8,128)(2,1)S(1)}, bf16[784,128]{1,0:T(8,128)(2,1)S(1)}, u32[]{:S(2)}, u32[]{:S(2)}) collective-permute-start(bf16[784,128]{1,0:T(8,128)(2,1)S(1)} %get-tuple-element.31), channel_id=1, source_target_pairs={{0,8},{8,0},{16,24},{24,16},{1,9},{9,1},{17,25},{25,17},{2,10},{10... | collective-permute-start | bytes 602120 | tf_op jit(solution)/shard_map/ppermute | solution.py:314
  4.9 10.9 %collective-permute-start.4 = (bf16[784,128]{1,0:T(8,128)(2,1)S(1)}, bf16[784,128]{1,0:T(8,128)(2,1)S(1)}, u32[]{:S(2)}, u32[]{:S(2)}) collective-permute-start(bf16[784,128]{1,0:T(8,128)(2,1)S(1)} %get-tuple-element.32), channel_id=1, source_target_pairs={{0,24},{8,16},{16,8},{24,0},{1,25},{9,17},{17,9},{25,1},{2,26},{10... | collective-permute-start | bytes 602120 | tf_op jit(solution)/shard_map/ppermute | solution.py:314
  7.8 2.8 %collective-permute-start = (f32[8,128]{1,0:T(8,128)S(1)}, f32[8,128]{1,0:T(8,128)S(1)}, u32[]{:S(2)}, u32[]{:S(2)}) collective-permute-start(f32[8,128]{1,0:T(8,128)S(1)} %get-tuple-element.22), channel_id=1, source_target_pairs={{0,1},{1,0},{2,3},{3,2},{4,5},{5,4},{6,7},{7,6},{8,9},{9,8},{10,11... | collective-permute-start | bytes 12296 | tf_op jit(solution)/shard_map/ppermute | solution.py:322
  9.1 8.8 %collective-permute-start.2 = (bf16[784,128]{1,0:T(8,128)(2,1)S(1)}, bf16[784,128]{1,0:T(8,128)(2,1)S(1)}, u32[]{:S(2)}, u32[]{:S(2)}) collective-permute-start(bf16[784,128]{1,0:T(8,128)(2,1)S(1)} %get-tuple-element.24), channel_id=1, source_target_pairs={{0,4},{4,0},{1,5},{5,1},{2,6},{6,2},{3,7},{7,3},{8,12},{12,8},{9,1... | collective-permute-start | bytes 602120 | tf_op jit(solution)/shard_map/ppermute | solution.py:315
  10.6 6.9 %collective-permute-start.1 = (f32[8,128]{1,0:T(8,128)S(1)}, f32[8,128]{1,0:T(8,128)S(1)}, u32[]{:S(2)}, u32[]{:S(2)}) collective-permute-start(f32[8,128]{1,0:T(8,128)S(1)} %add.6), channel_id=1, source_target_pairs={{0,2},{1,3},{2,0},{3,1},{4,6},{5,7},{6,4},{7,5},{8,10},{9,11},{10,... | collective-permute-start | bytes 12296 | tf_op jit(solution)/shard_map/ppermute | solution.py:322
  11.9 7.2 %collective-permute-start.5 = (bf16[784,128]{1,0:T(8,128)(2,1)S(1)}, bf16[784,128]{1,0:T(8,128)(2,1)S(1)}, u32[]{:S(2)}, u32[]{:S(2)}) collective-permute-start(bf16[784,128]{1,0:T(8,128)(2,1)S(1)} %collective-permute-done.3.refs_5_), channel_id=1, source_target_pairs={{0,4},{4,0},{1,5},{5,1},{2,6},{6,2},{3,7},{7,3},{8,12},{12,8},{9,1... | collective-permute-start | bytes 602120 | tf_op jit(solution)/shard_map/ppermute | solution.py:339
  15.9 3.2 %collective-permute-start.6 = (bf16[784,128]{1,0:T(8,128)(2,1)S(1)}, bf16[784,128]{1,0:T(8,128)(2,1)S(1)}, u32[]{:S(2)}, u32[]{:S(2)}) collective-permute-start(bf16[784,128]{1,0:T(8,128)(2,1)S(1)} %collective-permute-done.4.refs_6_), channel_id=1, source_target_pairs={{0,4},{4,0},{1,5},{5,1},{2,6},{6,2},{3,7},{7,3},{8,12},{12,8},{9,1... | collective-permute-start | bytes 602120 | tf_op jit(solution)/shard_map/ppermute | solution.py:339
  17.8 16.8 %copy-start.1 = (f32[4,24,24,128]{3,2,1,0:T(8,128)S(1)}, f32[4,24,24,128]{3,2,1,0:T(8,128)}, u32[]{:S(2)}) copy-start(f32[4,24,24,128]{3,2,1,0:T(8,128)} %param.8) | copy-start | bytes 3538948
  19.5 3.8 %collective-permute-start.9 = (f32[80,128]{1,0:T(8,128)S(1)}, f32[80,128]{1,0:T(8,128)S(1)}, u32[]{:S(2)}, u32[]{:S(2)}) collective-permute-start(f32[80,128]{1,0:T(8,128)S(1)} %shard_map.98.refs_0_), channel_id=1, source_target_pairs={{0,3},{1,2},{2,1},{3,0},{4,7},{5,6},{6,5},{7,4},{8,11},{9,10},{10,... | collective-permute-start | bytes 122888 | tf_op jit(solution)/shard_map/ppermute | solution.py:30
  21.7 2.9 %collective-permute-start.8 = (f32[80,128]{1,0:T(8,128)S(1)}, f32[80,128]{1,0:T(8,128)S(1)}, u32[]{:S(2)}, u32[]{:S(2)}) collective-permute-start(f32[80,128]{1,0:T(8,128)S(1)} %shard_map.98.refs_0_), channel_id=1, source_target_pairs={{0,2},{1,3},{2,0},{3,1},{4,6},{5,7},{6,4},{7,5},{8,10},{9,11},{10,... | collective-permute-start | bytes 122888 | tf_op jit(solution)/shard_map/ppermute | solution.py:30
  22.0 2.9 %collective-permute-start.7 = (f32[80,128]{1,0:T(8,128)S(1)}, f32[80,128]{1,0:T(8,128)S(1)}, u32[]{:S(2)}, u32[]{:S(2)}) collective-permute-start(f32[80,128]{1,0:T(8,128)S(1)} %shard_map.98.refs_0_), channel_id=1, source_target_pairs={{0,1},{1,0},{2,3},{3,2},{4,5},{5,4},{6,7},{7,6},{8,9},{9,8},{10,11... | collective-permute-start | bytes 122888 | tf_op jit(solution)/shard_map/ppermute | solution.py:30
  24.9 6.6 %collective-permute-start.10 = (bf16[64,512]{1,0:T(8,128)(2,1)S(1)}, bf16[64,512]{1,0:T(8,128)(2,1)S(1)}, u32[]{:S(2)}, u32[]{:S(2)}) collective-permute-start(bf16[64,512]{1,0:T(8,128)(2,1)S(1)} %get-tuple-element.33.refs_0_), channel_id=1, source_target_pairs={{0,8},{8,0},{16,24},{24,16},{1,9},{9,1},{17,25},{25,17},{2,10},{10... | collective-permute-start | bytes 196616 | tf_op jit(solution)/shard_map/ppermute | solution.py:356
  25.3 6.3 %collective-permute-start.11 = (bf16[64,512]{1,0:T(8,128)(2,1)S(1)}, bf16[64,512]{1,0:T(8,128)(2,1)S(1)}, u32[]{:S(2)}, u32[]{:S(2)}) collective-permute-start(bf16[64,512]{1,0:T(8,128)(2,1)S(1)} %get-tuple-element.33.refs_0_), channel_id=1, source_target_pairs={{0,24},{8,16},{16,8},{24,0},{1,25},{9,17},{17,9},{25,1},{2,26},{10... | collective-permute-start | bytes 196616 | tf_op jit(solution)/shard_map/ppermute | solution.py:356
  27.7 5.7 %collective-permute-start.12 = (bf16[64,512]{1,0:T(8,128)(2,1)S(1)}, bf16[64,512]{1,0:T(8,128)(2,1)S(1)}, u32[]{:S(2)}, u32[]{:S(2)}) collective-permute-start(bf16[64,512]{1,0:T(8,128)(2,1)S(1)} %get-tuple-element.33.refs_0_), channel_id=1, source_target_pairs={{0,4},{4,0},{1,5},{5,1},{2,6},{6,2},{3,7},{7,3},{8,12},{12,8},{9,1... | collective-permute-start | bytes 196616 | tf_op jit(solution)/shard_map/ppermute | solution.py:366
  31.6 2.7 %collective-permute-start.14 = (bf16[64,512]{1,0:T(8,128)(2,1)S(1)}, bf16[64,512]{1,0:T(8,128)(2,1)S(1)}, u32[]{:S(2)}, u32[]{:S(2)}) collective-permute-start(bf16[64,512]{1,0:T(8,128)(2,1)S(1)} %collective-permute-done.11.refs_2_), channel_id=1, source_target_pairs={{0,4},{4,0},{1,5},{5,1},{2,6},{6,2},{3,7},{7,3},{8,12},{12,8},{9,1... | collective-permute-start | bytes 196616 | tf_op jit(solution)/shard_map/ppermute | solution.py:366
  33.4 1.3 %collective-permute-start.13 = (bf16[64,512]{1,0:T(8,128)(2,1)S(1)}, bf16[64,512]{1,0:T(8,128)(2,1)S(1)}, u32[]{:S(2)}, u32[]{:S(2)}) collective-permute-start(bf16[64,512]{1,0:T(8,128)(2,1)S(1)} %collective-permute-done.10.refs_1_), channel_id=1, source_target_pairs={{0,4},{4,0},{1,5},{5,1},{2,6},{6,2},{3,7},{7,3},{8,12},{12,8},{9,1... | collective-permute-start | bytes 196616 | tf_op jit(solution)/shard_map/ppermute | solution.py:366

commit v4 on v3

--- a/solution.py
+++ b/solution.py
@@ -233,7 +233,7 @@
     rim = taps_lon.shape[0] // 2
     lon_sign, lat_sign = signs("lon"), signs("lat")
     at = 0
-    lon_pos, lat_pos = [], []
+    placed = []
     for t in range(tiles):
         shift = 0.0 if t == 0 else lat_sign[t - 1] * float(lat_tile)
         beside = []
@@ -247,9 +247,9 @@
         if t + 1 < tiles:
             after = (lane_row(extra_ref, at, blocks, slots), lane_row(extra_ref, at + blocks, blocks, slots))
             at += 2 * blocks
-        for lon_at, lat_at in [here] + beside:
-            lon_pos.append(lon_at)
-            lat_pos.append(lat_at + shift)
+        placed.append([(lon_at, lat_at + shift) for lon_at, lat_at in [here] + beside])
+    lon_pos = [placed[t][k][0] for k in range(3) for t in range(tiles)]
+    lat_pos = [placed[t][k][1] for k in range(3) for t in range(tiles)]
     lon_pos, lat_pos = jnp.concatenate(lon_pos, axis=1), jnp.concatenate(lat_pos, axis=1)
     tall = 32
     lon_w = band(fiota((tall, lon_pos.shape[1]), 0) + rim - lon_pos, taps_lon)
@@ -263,24 +263,47 @@
     out_ref[...] = (lon_e * lat_e).astype(bf16)
 
 
-def back_kernel(group, pieces, weight_ref, con_ref, *refs):
-    sets, out_hbm, all_ref, buf, sem = refs[:-4], refs[-4], refs[-3], refs[-2], refs[-1]
+def begin_kernel(group, edge, weight_ref, con_ref, *refs):
+    sets, out_hbm, rest_ref, all_ref, buf, sem = refs[:-5], refs[-5], refs[-4], refs[-3], refs[-2], refs[-1]
     members, cells, levels = con_ref.shape
     slots = sets[0].shape[0]
     for s, ref in enumerate(sets):
         all_ref[s * slots:(s + 1) * slots, :] = ref[...]
-    step = cells // pieces
+    depth = len(sets) * slots
+    last = signs("lon")[1] > 0
+    done = pl.ds(pl.multiple_of(jnp.where(last, 0, edge), 16), cells - edge)
+    left = pl.ds(pl.multiple_of(jnp.where(last, cells - edge, 0), 16), edge)
     copies = []
-    for g in range(members // group):
-        back = dot(weight_ref[...], all_ref[:, g * group * levels:(g + 1) * group * levels])
+    for m in range(0, members, group):
+        back = dot(weight_ref[:, 0:depth], all_ref[:, m * levels:(m + group) * levels])
         for k in range(group):
-            m = g * group + k
-            for p in range(pieces):
-                rows = slice(p * step, (p + 1) * step)
-                con = con_ref[m, rows, :]
-                buf[m, rows, :] = con - descent * (con + back[rows, k * levels:(k + 1) * levels])
-                copies.append(pltpu.make_async_copy(buf.at[m, rows], out_hbm.at[m, rows], sem.at[m * pieces + p]))
-                copies[-1].start()
+            con = con_ref[m + k]
+            buf[m + k] = con - descent * (con + back[:, k * levels:(k + 1) * levels])
+            copies.append(pltpu.make_async_copy(buf.at[m + k, done], out_hbm.at[m + k, done], sem.at[m + k]))
+            copies[-1].start()
+    for m in range(members):
+        rest_ref[m] = buf[m, left, :]
+    for copy in copies:
+        copy.wait()
+
+
+def end_kernel(group, weight_ref, rest_ref, begun_hbm, *refs):
+    sets, out_hbm, all_ref, buf, sem = refs[:-4], refs[-4], refs[-3], refs[-2], refs[-1]
+    members, edge, levels = rest_ref.shape
+    cells = weight_ref.shape[0]
+    slots = sets[0].shape[0]
+    for s, ref in enumerate(sets):
+        all_ref[s * slots:(s + 1) * slots, :] = ref[...]
+    begin = weight_ref.shape[1] - len(sets) * slots
+    left = pl.ds(pl.multiple_of(jnp.where(signs("lon")[1] > 0, cells - edge, 0), 16), edge)
+    weight = weight_ref[left, begin:]
+    copies = []
+    for m in range(0, members, group):
+        back = dot(weight, all_ref[:, m * levels:(m + group) * levels])
+        for k in range(group):
+            buf[m + k] = rest_ref[m + k] - descent * back[:, k * levels:(k + 1) * levels]
+            copies.append(pltpu.make_async_copy(buf.at[m + k], out_hbm.at[m + k, left], sem.at[m + k]))
+            copies[-1].start()
     for copy in copies:
         copy.wait()
 
@@ -299,6 +322,7 @@
     lat_pairs = pairings(lax.axis_size("lat"), False)
     vmem = pl.BlockSpec(memory_space=pltpu.VMEM)
     smem = pl.BlockSpec(memory_space=pltpu.SMEM)
+    hbm = pl.BlockSpec(memory_space=pltpu.HBM)
     shape = jax.ShapeDtypeStruct
     taps_lon = taps_lon.astype(bf16).astype(f32)
     taps_lat = taps_lat.astype(bf16).astype(f32)
@@ -334,6 +358,7 @@
         in_specs=[smem] * 2 + [vmem] * (1 + n_tiles), out_specs=[vmem] * (1 + n_rims), compiler_params=params(),
     )(taps_lon, taps_lat, info, low, *sides)
 
+    halos[0], own = lax.optimization_barrier((halos[0], own))
     rims = list(halos)
     for p in lat_pairs:
         rims += [lax.ppermute(h, "lat", p) for h in halos]
@@ -361,22 +386,33 @@
         in_specs=[smem] * 2 + [vmem] * 3, out_specs=[vmem] * 2, compiler_params=params(),
     )(taps_lon, taps_lat, info, extra, resid)
     row[1], weight = lax.optimization_barrier((row[1], weight))
-    around = list(row)
-    for q in lat_pairs:
-        around += [lax.ppermute(r, "lat", q) for r in row]
+    around = []
+    for r in row:
+        around += [r] + [lax.ppermute(r, "lat", q) for q in lat_pairs]
     group = 2 if members % 2 == 0 else 1
-    pieces = 2
-    new = pl.pallas_call(
-        functools.partial(back_kernel, group, pieces),
-        out_shape=shape((members, cells, levels), f32),
-        in_specs=[vmem] * (2 + count), out_specs=pl.BlockSpec(memory_space=pl.ANY),
+    late = n_tiles
+    begun, rest = pl.pallas_call(
+        functools.partial(begin_kernel, group, edge),
+        out_shape=[shape((members, cells, levels), f32), shape((members, edge, levels), f32)],
+        in_specs=[vmem] * (2 + count - late), out_specs=[hbm, vmem],
         scratch_shapes=[
-            pltpu.VMEM((count * slots, wide), bf16),
+            pltpu.VMEM(((count - late) * slots, wide), bf16),
             pltpu.VMEM((members, cells, levels), f32),
-            pltpu.SemaphoreType.DMA((members * pieces,)),
+            pltpu.SemaphoreType.DMA((members,)),
         ],
         compiler_params=params(),
-    )(weight, flat, *around)
+    )(weight, flat, *around[:-late])
+    new = pl.pallas_call(
+        functools.partial(end_kernel, group),
+        out_shape=shape((members, cells, levels), f32),
+        in_specs=[vmem] * 2 + [hbm] + [vmem] * late, out_specs=hbm,
+        scratch_shapes=[
+            pltpu.VMEM((late * slots, wide), bf16),
+            pltpu.VMEM((members, edge, levels), f32),
+            pltpu.SemaphoreType.DMA((members,)),
+        ],
+        input_output_aliases={2: 0}, compiler_params=params(),
+    )(weight, rest, begun, *around[-late:])
     return (new.reshape(controls.shape), resid[None, None, None])
 
 

time: 36.4 us -> 35.6 us (0.978)
  waiting for transfers between devices: 5.5 us -> 4.03 us
  Pallas kernels: 5.25 us -> 6 us
    ppermute x2, waiting for transfers between devices: 1.63 us -> 0.01 us  [shards(): halos = [lax.ppermute(r, 'lon', p) for r, p in zip((rim1, rim2), lon_pairs)]]
    ppermute x2, waiting for transfers between devices: 0.01 us -> 1.41 us  [shards(): lax.ppermute(info, 'mem', [(i, i ^ step) for i in range(n_mem)])]
    ppermute x3, waiting for transfers between devices: 1.25 us -> 0.01 us  [shards(): around += [r] + [lax.ppermute(r, 'lat', q) for q in lat_pairs]]
    ppermute x2, starting transfers between devices: 3.98 us -> 2.88 us  [shards(): rims += [lax.ppermute(h, 'lat', p) for h in halos]]
    ppermute x1, starting transfers between devices: 1.52 us -> 2.37 us  [shards(): sides = [lax.ppermute(r, 'lat', p) for r, p in zip(sides, lat_pairs)]]
    pallas_call x1 -> x2, Pallas kernels: 1.49 us -> 2.23 us  [the longest x1 1.26 us: shards(): pl.pallas_call(functools.partial(begin_kernel, group, edge), out_shape=[s...]
  transfers between devices with their start and end apart: 15 -> 15, of which waited for: 6 -> 4; matrix products, arithmetic and copies ran while one was open for 0% -> 0% of each run, Pallas kernels for 9% -> 12%
where the time goes in v4:
time: 35.6 us; the launch traced here: 35.4 us
  starting transfers between devices  22 us (62%)
  Pallas kernels  6 us (17%)
  waiting for transfers between devices  4.03 us (11%)
  local copies, waits for them, and re-layouts  1.96 us (6%)
  between operations  1.45 us (4%)
    ppermute x2, starting transfers between devices, shards(): halos = [lax.ppermute(r, 'lon', p) for r, p in zip((rim1, rim2), lon_pairs)]  4.39 us
    ppermute x3, starting transfers between devices, shards(): around += [r] + [lax.ppermute(r, 'lat', q) for q in lat_pairs]  4.26 us
    ppermute x2, starting transfers between devices, shards(): rims += [lax.ppermute(h, 'lat', p) for h in halos]  2.88 us
    ppermute x2, starting transfers between devices, shards(): row = [send] + [lax.ppermute(send, 'lon', p) for p in lon_pairs]  2.72 us
    ppermute x3, starting transfers between devices, sum_terms(): lax.ppermute(x, 'mem', [(i, i ^ b) for i in range(count)])  2.71 us
    ppermute x2, starting transfers between devices, shards(): lax.ppermute(info, 'mem', [(i, i ^ step) for i in range(n_mem)])  2.65 us
    ppermute x3, waiting for transfers between devices, sum_terms(): lax.ppermute(x, 'mem', [(i, i ^ b) for i in range(count)])  2.6 us
    ppermute x1, starting transfers between devices, shards(): sides = [lax.ppermute(r, 'lat', p) for r, p in zip(sides, lat_pairs)]  2.37 us
  transfers between devices with their start and end apart: 15, of which 4 were waited for; matrix products, arithmetic and copies ran while one was open for 0% of the time, Pallas kernels for 12%

profile of v4, /device:TPU:1, one launch (start us, length us, event | category | flops | bytes accessed | tf_op | source)
XLA Modules:
  0.0 35.4 jit_solution(5884575142181090350)
XLA Ops:
  0.7 1.3 %copy-done = f32[4,24,24,128]{3,2,1,0:T(8,128)S(1)} copy-done((f32[4,24,24,128]{3,2,1,0:T(8,128)S(1)}, f32[4,24,24,128]{3,2,1,0:T(8,128)}, u32[]{:S(2)}) %copy-start) | copy-done | bytes 1179672
  2.0 0.7 %copy-done.4 = s32[1,1,1,16]{3,2,1,0:T(1,128)S(1)} copy-done((s32[1,1,1,16]{3,2,1,0:T(1,128)S(1)}, s32[1,1,1,16]{3,2,1,0:T(1,128)}, u32[]{:S(2)}) %copy-start.4) | copy-done | bytes 88
  2.7 2.2 %collective-permute-start = (bf16[784,128]{1,0:T(8,128)(2,1)S(1)}, bf16[784,128]{1,0:T(8,128)(2,1)S(1)}, u32[]{:S(2)}, u32[]{:S(2)}) collective-permute-start(bf16[784,128]{1,0:T(8,128)(2,1)S(1)} %get-tuple-element.25), channel_id=1, source_target_pairs={{0,8},{8,0},{16,24},{24,16},{1,9},{9,1},{17,25},{25,17},{2,10},{10... | collective-permute-start | bytes 602120 | tf_op jit(solution)/shard_map/ppermute | solution.py:338
  4.9 2.2 %collective-permute-start.4 = (bf16[784,128]{1,0:T(8,128)(2,1)S(1)}, bf16[784,128]{1,0:T(8,128)(2,1)S(1)}, u32[]{:S(2)}, u32[]{:S(2)}) collective-permute-start(bf16[784,128]{1,0:T(8,128)(2,1)S(1)} %get-tuple-element.38), channel_id=1, source_target_pairs={{0,24},{8,16},{16,8},{24,0},{1,25},{9,17},{17,9},{25,1},{2,26},{10... | collective-permute-start | bytes 602120 | tf_op jit(solution)/shard_map/ppermute | solution.py:338
  7.8 1.3 %collective-permute-start.1 = (f32[8,128]{1,0:T(8,128)S(1)}, f32[8,128]{1,0:T(8,128)S(1)}, u32[]{:S(2)}, u32[]{:S(2)}) collective-permute-start(f32[8,128]{1,0:T(8,128)S(1)} %get-tuple-element.27), channel_id=1, source_target_pairs={{0,1},{1,0},{2,3},{3,2},{4,5},{5,4},{6,7},{7,6},{8,9},{9,8},{10,11... | collective-permute-start | bytes 12296 | tf_op jit(solution)/shard_map/ppermute | solution.py:346
  9.1 1.4 %collective-permute-done.1 = f32[8,128]{1,0:T(8,128)S(1)} collective-permute-done((f32[8,128]{1,0:T(8,128)S(1)}, f32[8,128]{1,0:T(8,128)S(1)}, u32[]{:S(2)}, u32[]{:S(2)}) %collective-permute-start.1) | collective-permute-done | bytes 4128 | tf_op jit(solution)/shard_map/ppermute | solution.py:346
  10.5 1.4 %collective-permute-start.2 = (f32[8,128]{1,0:T(8,128)S(1)}, f32[8,128]{1,0:T(8,128)S(1)}, u32[]{:S(2)}, u32[]{:S(2)}) collective-permute-start(f32[8,128]{1,0:T(8,128)S(1)} %add.6), channel_id=1, source_target_pairs={{0,2},{1,3},{2,0},{3,1},{4,6},{5,7},{6,4},{7,5},{8,10},{9,11},{10,... | collective-permute-start | bytes 12296 | tf_op jit(solution)/shard_map/ppermute | solution.py:346
  11.9 2.4 %collective-permute-start.3 = (bf16[784,128]{1,0:T(8,128)(2,1)S(1)}, bf16[784,128]{1,0:T(8,128)(2,1)S(1)}, u32[]{:S(2)}, u32[]{:S(2)}) collective-permute-start(bf16[784,128]{1,0:T(8,128)(2,1)S(1)} %get-tuple-element.30), channel_id=1, source_target_pairs={{0,4},{4,0},{1,5},{5,1},{2,6},{6,2},{3,7},{7,3},{8,12},{12,8},{9,1... | collective-permute-start | bytes 602120 | tf_op jit(solution)/shard_map/ppermute | solution.py:339
  14.3 0.3 shard_map.96.own_ref
  14.6 2.1 %collective-permute-start.5 = (bf16[784,128]{1,0:T(8,128)(2,1)S(1)}, bf16[784,128]{1,0:T(8,128)(2,1)S(1)}, u32[]{:S(2)}, u32[]{:S(2)}) collective-permute-start(bf16[784,128]{1,0:T(8,128)(2,1)S(1)} %collective-permute-done.refs_5_), channel_id=1, source_target_pairs={{0,4},{4,0},{1,5},{5,1},{2,6},{6,2},{3,7},{7,3},{8,12},{12,8},{9,1... | collective-permute-start | bytes 602120 | tf_op jit(solution)/shard_map/ppermute | solution.py:364
  16.7 0.7 %collective-permute-start.6 = (bf16[784,128]{1,0:T(8,128)(2,1)S(1)}, bf16[784,128]{1,0:T(8,128)(2,1)S(1)}, u32[]{:S(2)}, u32[]{:S(2)}) collective-permute-start(bf16[784,128]{1,0:T(8,128)(2,1)S(1)} %collective-permute-done.4.refs_6_), channel_id=1, source_target_pairs={{0,4},{4,0},{1,5},{5,1},{2,6},{6,2},{3,7},{7,3},{8,12},{12,8},{9,1... | collective-permute-start | bytes 602120 | tf_op jit(solution)/shard_map/ppermute | solution.py:364
  17.5 1.2 %shard_map.97 = (f32[64,512]{1,0:T(8,128)S(1)}, bf16[64,192]{1,0:T(8,128)(2,1)S(1)}, bf16[64,192]{1,0:T(8,128)(2,1)S(1)}, bf16[64,192]{1,0:T(8,128)(2,1)S(1)}, bf16[64,192]{1,0:T(8,128)(2,1)S(1)}) custom-call(f32[17]{0:T(128)S(1)} %get-tuple-element.49.taps_lon, f32[17]{0:T(128)S(1)} %get-tuple-element.48.taps_lat, f32[8,128]{1,0:T(8,128)S(1)} %add.7.info_ref, ...), custom_call_target="tpu_custom_call" | custom-call | tf_op jit(solution)/shard_map/pallas_call | solution.py:355
  18.7 0.4 %shard_map.98.refs_0_ = f32[80,128]{1,0:T(8,128)S(1)} custom-call(f32[64,512]{1,0:T(8,128)S(1)} %get-tuple-element.31.base_ref, bf16[64,512]{1,0:T(8,128)(2,1)S(1)} %shard_map.96.own_ref, f32[16,128]{1,0:T(8,128)S(1)} %bitcast.13, f32[1,16]{1,0:T(1,128)S(1)} %compare_select_fusion.scale_ref, bf16[16,128]{1,0:T(8,128)(2,1)S(1)} %slice.4.refs_0_, ...), custom_call_target="tpu_custom_call" | custom-call | tf_op jit(solution)/shard_map/pallas_call | solution.py:368
  19.1 2.2 %collective-permute-start.9 = (f32[80,128]{1,0:T(8,128)S(1)}, f32[80,128]{1,0:T(8,128)S(1)}, u32[]{:S(2)}, u32[]{:S(2)}) collective-permute-start(f32[80,128]{1,0:T(8,128)S(1)} %shard_map.98.refs_0_), channel_id=1, source_target_pairs={{0,3},{1,2},{2,1},{3,0},{4,7},{5,6},{6,5},{7,4},{8,11},{9,10},{10,... | collective-permute-start | bytes 122888 | tf_op jit(solution)/shard_map/ppermute | solution.py:30
  21.6 0.3 collective-permute-start.7
  21.9 1.1 %collective-permute-done.9.refs_3_ = f32[80,128]{1,0:T(8,128)S(1)} collective-permute-done((f32[80,128]{1,0:T(8,128)S(1)}, f32[80,128]{1,0:T(8,128)S(1)}, u32[]{:S(2)}, u32[]{:S(2)}) %collective-permute-start.9) | collective-permute-done | bytes 40992 | tf_op jit(solution)/shard_map/ppermute | solution.py:30
  23.0 1.3 %collective-permute-done.8.refs_2_ = f32[80,128]{1,0:T(8,128)S(1)} collective-permute-done((f32[80,128]{1,0:T(8,128)S(1)}, f32[80,128]{1,0:T(8,128)S(1)}, u32[]{:S(2)}, u32[]{:S(2)}) %collective-permute-start.8) | collective-permute-done | bytes 40992 | tf_op jit(solution)/shard_map/ppermute | solution.py:30
  24.6 0.4 %collective-permute-start.10 = (bf16[64,512]{1,0:T(8,128)(2,1)S(1)}, bf16[64,512]{1,0:T(8,128)(2,1)S(1)}, u32[]{:S(2)}, u32[]{:S(2)}) collective-permute-start(bf16[64,512]{1,0:T(8,128)(2,1)S(1)} %get-tuple-element.39.refs_0_), channel_id=1, source_target_pairs={{0,8},{8,0},{16,24},{24,16},{1,9},{9,1},{17,25},{25,17},{2,10},{10... | collective-permute-start | bytes 196616 | tf_op jit(solution)/shard_map/ppermute | solution.py:381
  24.9 2.4 %collective-permute-start.13 = (bf16[64,512]{1,0:T(8,128)(2,1)S(1)}, bf16[64,512]{1,0:T(8,128)(2,1)S(1)}, u32[]{:S(2)}, u32[]{:S(2)}) collective-permute-start(bf16[64,512]{1,0:T(8,128)(2,1)S(1)} %get-tuple-element.39.refs_0_), channel_id=1, source_target_pairs={{0,24},{8,16},{16,8},{24,0},{1,25},{9,17},{17,9},{25,1},{2,26},{10... | collective-permute-start | bytes 196616 | tf_op jit(solution)/shard_map/ppermute | solution.py:381
  27.3 2.5 %collective-permute-start.11 = (bf16[64,512]{1,0:T(8,128)(2,1)S(1)}, bf16[64,512]{1,0:T(8,128)(2,1)S(1)}, u32[]{:S(2)}, u32[]{:S(2)}) collective-permute-start(bf16[64,512]{1,0:T(8,128)(2,1)S(1)} %get-tuple-element.39.refs_0_), channel_id=1, source_target_pairs={{0,4},{4,0},{1,5},{5,1},{2,6},{6,2},{3,7},{7,3},{8,12},{12,8},{9,1... | collective-permute-start | bytes 196616 | tf_op jit(solution)/shard_map/ppermute | solution.py:391
  29.8 1.6 %shard_map.100 = (bf16[576,384]{1,0:T(8,128)(2,1)S(1)}, f32[16,128]{1,0:T(8,128)}) custom-call(f32[17]{0:T(128)S(1)} %get-tuple-element.49.taps_lon, f32[17]{0:T(128)S(1)} %get-tuple-element.48.taps_lat, f32[8,128]{1,0:T(8,128)S(1)} %add.7.info_ref, f32[16,128]{1,0:T(8,128)S(1)} %get-tuple-element.40.extra_ref, f32[64,128]{1,0:T(8,128)S(1)} %get-tuple-element.41.resid_ref), custom_call_target="tpu_custom_call" | custom-call | tf_op jit(solution)/shard_map/pallas_call | solution.py:383
  31.4 1.8 %collective-permute-start.14 = (bf16[64,512]{1,0:T(8,128)(2,1)S(1)}, bf16[64,512]{1,0:T(8,128)(2,1)S(1)}, u32[]{:S(2)}, u32[]{:S(2)}) collective-permute-start(bf16[64,512]{1,0:T(8,128)(2,1)S(1)} %collective-permute-done.13.refs_0_), channel_id=1, source_target_pairs={{0,4},{4,0},{1,5},{5,1},{2,6},{6,2},{3,7},{7,3},{8,12},{12,8},{9,1... | collective-permute-start | bytes 196616 | tf_op jit(solution)/shard_map/ppermute | solution.py:391
  33.2 1.3 %shard_map.101 = (f32[4,576,128]{2,1,0:T(8,128)}, f32[4,192,128]{2,1,0:T(8,128)S(1)}) custom-call(bf16[576,384]{1,0:T(8,128)(2,1)S(1)} %get-tuple-element.43.weight_ref, f32[4,576,128]{2,1,0:T(8,128)S(1)} %bitcast.11, bf16[64,512]{1,0:T(8,128)(2,1)S(1)} %get-tuple-element.39.refs_0_, bf16[64,512]{1,0:T(8,128)(2,1)S(1)} %collective-permute-done.11.refs_1_, ...), custom_call_target="tpu_custom_call" | custom-call | tf_op jit(solution)/shard_map/pallas_call | solution.py:394
  34.5 1.0 %shard_map.102 = f32[4,576,128]{2,1,0:T(8,128)} custom-call(bf16[576,384]{1,0:T(8,128)(2,1)S(1)} %get-tuple-element.43.weight_ref, f32[4,192,128]{2,1,0:T(8,128)S(1)} %get-tuple-element.45.rest_ref, f32[4,576,128]{2,1,0:T(8,128)} %get-tuple-element.46.begun_hbm, bf16[64,512]{1,0:T(8,128)(2,1)S(1)} %collective-permute-done.13.refs_0_, ...), custom_call_target="tpu_custom_call", output_to_operand_aliasing={{}: (2, {})} | custom-call | tf_op jit(solution)/shard_map/pallas_call | solution.py:405
  (35 shorter events, 0.8 us)
Async XLA Ops:
  0.6 7.2 %copy-start.7 = (s32[1,1,1,16]{3,2,1,0:T(1,128)S(1)}, s32[1,1,1,16]{3,2,1,0:T(1,128)}, u32[]{:S(2)}) copy-start(s32[1,1,1,16]{3,2,1,0:T(1,128)} %param.14) | copy-start | bytes 196
  0.6 16.8 %copy-start.5 = (f32[17]{0:T(128)S(1)}, f32[17]{0:T(128)}, u32[]{:S(2)}) copy-start(f32[17]{0:T(128)} %param.11) | copy-start | bytes 208
  0.7 16.8 %copy-start.6 = (f32[17]{0:T(128)S(1)}, f32[17]{0:T(128)}, u32[]{:S(2)}) copy-start(f32[17]{0:T(128)} %param.10) | copy-start | bytes 208
  0.7 1.3 %copy-start = (f32[4,24,24,128]{3,2,1,0:T(8,128)S(1)}, f32[4,24,24,128]{3,2,1,0:T(8,128)}, u32[]{:S(2)}) copy-start(f32[4,24,24,128]{3,2,1,0:T(8,128)} %param.8) | copy-start | bytes 3538948
  2.0 0.7 %copy-start.4 = (s32[1,1,1,16]{3,2,1,0:T(1,128)S(1)}, s32[1,1,1,16]{3,2,1,0:T(1,128)}, u32[]{:S(2)}) copy-start(s32[1,1,1,16]{3,2,1,0:T(1,128)} %param.12) | copy-start | bytes 196
  2.6 11.6 %copy-start.2 = (bf16[4,24,24,128]{3,2,1,0:T(8,128)(2,1)S(1)}, bf16[4,24,24,128]{3,2,1,0:T(8,128)(2,1)}, u32[]{:S(2)}) copy-start(bf16[4,24,24,128]{3,2,1,0:T(8,128)(2,1)} %param.9) | copy-start | bytes 1769476
  2.6 16.1 %copy-start.3 = (f32[1,1,1,16,128]{4,3,2,1,0:T(8,128)S(1)}, f32[1,1,1,16,128]{4,3,2,1,0:T(8,128)}, u32[]{:S(2)}) copy-start(f32[1,1,1,16,128]{4,3,2,1,0:T(8,128)} %param.15) | copy-start | bytes 24580
  2.7 11.8 %collective-permute-start = (bf16[784,128]{1,0:T(8,128)(2,1)S(1)}, bf16[784,128]{1,0:T(8,128)(2,1)S(1)}, u32[]{:S(2)}, u32[]{:S(2)}) collective-permute-start(bf16[784,128]{1,0:T(8,128)(2,1)S(1)} %get-tuple-element.25), channel_id=1, source_target_pairs={{0,8},{8,0},{16,24},{24,16},{1,9},{9,1},{17,25},{25,17},{2,10},{10... | collective-permute-start | bytes 602120 | tf_op jit(solution)/shard_map/ppermute | solution.py:338
  4.9 11.8 %collective-permute-start.4 = (bf16[784,128]{1,0:T(8,128)(2,1)S(1)}, bf16[784,128]{1,0:T(8,128)(2,1)S(1)}, u32[]{:S(2)}, u32[]{:S(2)}) collective-permute-start(bf16[784,128]{1,0:T(8,128)(2,1)S(1)} %get-tuple-element.38), channel_id=1, source_target_pairs={{0,24},{8,16},{16,8},{24,0},{1,25},{9,17},{17,9},{25,1},{2,26},{10... | collective-permute-start | bytes 602120 | tf_op jit(solution)/shard_map/ppermute | solution.py:338
  7.8 2.7 %collective-permute-start.1 = (f32[8,128]{1,0:T(8,128)S(1)}, f32[8,128]{1,0:T(8,128)S(1)}, u32[]{:S(2)}, u32[]{:S(2)}) collective-permute-start(f32[8,128]{1,0:T(8,128)S(1)} %get-tuple-element.27), channel_id=1, source_target_pairs={{0,1},{1,0},{2,3},{3,2},{4,5},{5,4},{6,7},{7,6},{8,9},{9,8},{10,11... | collective-permute-start | bytes 12296 | tf_op jit(solution)/shard_map/ppermute | solution.py:346
  10.5 3.8 %collective-permute-start.2 = (f32[8,128]{1,0:T(8,128)S(1)}, f32[8,128]{1,0:T(8,128)S(1)}, u32[]{:S(2)}, u32[]{:S(2)}) collective-permute-start(f32[8,128]{1,0:T(8,128)S(1)} %add.6), channel_id=1, source_target_pairs={{0,2},{1,3},{2,0},{3,1},{4,6},{5,7},{6,4},{7,5},{8,10},{9,11},{10,... | collective-permute-start | bytes 12296 | tf_op jit(solution)/shard_map/ppermute | solution.py:346
  11.9 5.6 %collective-permute-start.3 = (bf16[784,128]{1,0:T(8,128)(2,1)S(1)}, bf16[784,128]{1,0:T(8,128)(2,1)S(1)}, u32[]{:S(2)}, u32[]{:S(2)}) collective-permute-start(bf16[784,128]{1,0:T(8,128)(2,1)S(1)} %get-tuple-element.30), channel_id=1, source_target_pairs={{0,4},{4,0},{1,5},{5,1},{2,6},{6,2},{3,7},{7,3},{8,12},{12,8},{9,1... | collective-permute-start | bytes 602120 | tf_op jit(solution)/shard_map/ppermute | solution.py:339
  14.6 18.6 %copy-start.1 = (f32[4,24,24,128]{3,2,1,0:T(8,128)S(1)}, f32[4,24,24,128]{3,2,1,0:T(8,128)}, u32[]{:S(2)}) copy-start(f32[4,24,24,128]{3,2,1,0:T(8,128)} %param.8) | copy-start | bytes 3538948
  14.6 4.1 %collective-permute-start.5 = (bf16[784,128]{1,0:T(8,128)(2,1)S(1)}, bf16[784,128]{1,0:T(8,128)(2,1)S(1)}, u32[]{:S(2)}, u32[]{:S(2)}) collective-permute-start(bf16[784,128]{1,0:T(8,128)(2,1)S(1)} %collective-permute-done.refs_5_), channel_id=1, source_target_pairs={{0,4},{4,0},{1,5},{5,1},{2,6},{6,2},{3,7},{7,3},{8,12},{12,8},{9,1... | collective-permute-start | bytes 602120 | tf_op jit(solution)/shard_map/ppermute | solution.py:364
  16.7 2.0 %collective-permute-start.6 = (bf16[784,128]{1,0:T(8,128)(2,1)S(1)}, bf16[784,128]{1,0:T(8,128)(2,1)S(1)}, u32[]{:S(2)}, u32[]{:S(2)}) collective-permute-start(bf16[784,128]{1,0:T(8,128)(2,1)S(1)} %collective-permute-done.4.refs_6_), channel_id=1, source_target_pairs={{0,4},{4,0},{1,5},{5,1},{2,6},{6,2},{3,7},{7,3},{8,12},{12,8},{9,1... | collective-permute-start | bytes 602120 | tf_op jit(solution)/shard_map/ppermute | solution.py:364
  19.1 3.8 %collective-permute-start.9 = (f32[80,128]{1,0:T(8,128)S(1)}, f32[80,128]{1,0:T(8,128)S(1)}, u32[]{:S(2)}, u32[]{:S(2)}) collective-permute-start(f32[80,128]{1,0:T(8,128)S(1)} %shard_map.98.refs_0_), channel_id=1, source_target_pairs={{0,3},{1,2},{2,1},{3,0},{4,7},{5,6},{6,5},{7,4},{8,11},{9,10},{10,... | collective-permute-start | bytes 122888 | tf_op jit(solution)/shard_map/ppermute | solution.py:30
  21.4 2.9 %collective-permute-start.8 = (f32[80,128]{1,0:T(8,128)S(1)}, f32[80,128]{1,0:T(8,128)S(1)}, u32[]{:S(2)}, u32[]{:S(2)}) collective-permute-start(f32[80,128]{1,0:T(8,128)S(1)} %shard_map.98.refs_0_), channel_id=1, source_target_pairs={{0,2},{1,3},{2,0},{3,1},{4,6},{5,7},{6,4},{7,5},{8,10},{9,11},{10,... | collective-permute-start | bytes 122888 | tf_op jit(solution)/shard_map/ppermute | solution.py:30
  21.6 2.9 %collective-permute-start.7 = (f32[80,128]{1,0:T(8,128)S(1)}, f32[80,128]{1,0:T(8,128)S(1)}, u32[]{:S(2)}, u32[]{:S(2)}) collective-permute-start(f32[80,128]{1,0:T(8,128)S(1)} %shard_map.98.refs_0_), channel_id=1, source_target_pairs={{0,1},{1,0},{2,3},{3,2},{4,5},{5,4},{6,7},{7,6},{8,9},{9,8},{10,11... | collective-permute-start | bytes 122888 | tf_op jit(solution)/shard_map/ppermute | solution.py:30
  24.6 6.8 %collective-permute-start.10 = (bf16[64,512]{1,0:T(8,128)(2,1)S(1)}, bf16[64,512]{1,0:T(8,128)(2,1)S(1)}, u32[]{:S(2)}, u32[]{:S(2)}) collective-permute-start(bf16[64,512]{1,0:T(8,128)(2,1)S(1)} %get-tuple-element.39.refs_0_), channel_id=1, source_target_pairs={{0,8},{8,0},{16,24},{24,16},{1,9},{9,1},{17,25},{25,17},{2,10},{10... | collective-permute-start | bytes 196616 | tf_op jit(solution)/shard_map/ppermute | solution.py:381
  24.9 6.5 %collective-permute-start.13 = (bf16[64,512]{1,0:T(8,128)(2,1)S(1)}, bf16[64,512]{1,0:T(8,128)(2,1)S(1)}, u32[]{:S(2)}, u32[]{:S(2)}) collective-permute-start(bf16[64,512]{1,0:T(8,128)(2,1)S(1)} %get-tuple-element.39.refs_0_), channel_id=1, source_target_pairs={{0,24},{8,16},{16,8},{24,0},{1,25},{9,17},{17,9},{25,1},{2,26},{10... | collective-permute-start | bytes 196616 | tf_op jit(solution)/shard_map/ppermute | solution.py:381
  27.3 5.9 %collective-permute-start.11 = (bf16[64,512]{1,0:T(8,128)(2,1)S(1)}, bf16[64,512]{1,0:T(8,128)(2,1)S(1)}, u32[]{:S(2)}, u32[]{:S(2)}) collective-permute-start(bf16[64,512]{1,0:T(8,128)(2,1)S(1)} %get-tuple-element.39.refs_0_), channel_id=1, source_target_pairs={{0,4},{4,0},{1,5},{5,1},{2,6},{6,2},{3,7},{7,3},{8,12},{12,8},{9,1... | collective-permute-start | bytes 196616 | tf_op jit(solution)/shard_map/ppermute | solution.py:391
  31.4 1.8 %collective-permute-start.12 = (bf16[64,512]{1,0:T(8,128)(2,1)S(1)}, bf16[64,512]{1,0:T(8,128)(2,1)S(1)}, u32[]{:S(2)}, u32[]{:S(2)}) collective-permute-start(bf16[64,512]{1,0:T(8,128)(2,1)S(1)} %collective-permute-done.10.refs_2_), channel_id=1, source_target_pairs={{0,4},{4,0},{1,5},{5,1},{2,6},{6,2},{3,7},{7,3},{8,12},{12,8},{9,1... | collective-permute-start | bytes 196616 | tf_op jit(solution)/shard_map/ppermute | solution.py:391
  31.4 3.1 %collective-permute-start.14 = (bf16[64,512]{1,0:T(8,128)(2,1)S(1)}, bf16[64,512]{1,0:T(8,128)(2,1)S(1)}, u32[]{:S(2)}, u32[]{:S(2)}) collective-permute-start(bf16[64,512]{1,0:T(8,128)(2,1)S(1)} %collective-permute-done.13.refs_0_), channel_id=1, source_target_pairs={{0,4},{4,0},{1,5},{5,1},{2,6},{6,2},{3,7},{7,3},{8,12},{12,8},{9,1... | collective-permute-start | bytes 196616 | tf_op jit(solution)/shard_map/ppermute | solution.py:391

commit v5 on v4

--- a/solution.py
+++ b/solution.py
@@ -76,9 +76,10 @@
 
 
 def band(distance, taps_ref):
+    taps = taps_ref[...].astype(bf16).astype(f32)
     out = jnp.zeros_like(distance)
-    for k in range(taps_ref.shape[0]):
-        out = jnp.where(distance == float(k), taps_ref[k], out)
+    for k in range(taps.shape[1]):
+        out = jnp.where(distance == float(k), taps[:, k:k + 1], out)
     return out
 
 
@@ -90,10 +91,11 @@
     return pltpu.CompilerParams(vmem_limit_bytes=mib * 1024 * 1024)
 
 
-def start_kernel(dims, con_ref, col_ref, low_ref, rim1_ref, rim2_ref, info_ref, *side_refs):
+def start_kernel(dims, low_ref, col_ref, rim1_ref, rim2_ref, info_ref, *refs):
     rim, lon_tile, lat_tile, blocks = dims
-    edge = rim * lat_tile
-    members, cells, levels = con_ref.shape
+    side_refs, con_ref = refs[:-1], refs[-1]
+    edge, cells = rim * lat_tile, lon_tile * lat_tile
+    members, levels = low_ref.shape[0] // cells, low_ref.shape[1]
     n_slots = col_ref.shape[1]
     mem = lax.axis_index("mem")
     column = col_ref[...].astype(f32)
@@ -112,18 +114,17 @@
     far = cells - edge
     for at, ref in ((jnp.where(even, far, 0), rim1_ref), (jnp.where(even, 0, far), rim2_ref)):
         for m in range(members):
-            ref[m * edge:(m + 1) * edge, :] = con_ref[m, pl.ds(pl.multiple_of(at, 16), edge), :].astype(bf16)
+            ref[m * edge:(m + 1) * edge, :] = low_ref[pl.ds(pl.multiple_of(at + m * cells, 16), edge), :]
         ref[members * edge:, :] = placed
+    con_ref[...] = low_ref[...].astype(f32)
     for ref, sign in zip(side_refs, signs("lat")):
         at = jnp.where(sign > 0, lat_tile - rim, 0)
         for m in range(members):
             for i in range(0, lon_tile, 2):
-                pair = [con_ref[m, pl.ds(pl.multiple_of(at + (i + k) * lat_tile, 8), rim), :] for k in range(2)]
+                pair = [con_ref[pl.ds(pl.multiple_of(at + (m * lon_tile + i + k) * lat_tile, 8), rim), :] for k in range(2)]
                 row_at = (m * lon_tile + i) * rim
                 ref[row_at:row_at + 2 * rim, :] = jnp.concatenate(pair, axis=0).astype(bf16)
         ref[members * lon_tile * rim:, :] = placed
-    for m in range(members):
-        low_ref[m * cells:(m + 1) * cells, :] = con_ref[m].astype(bf16)
 
 
 def pick_kernel(lat_tile, blocks, info_ref, ens_ref, out_ref):
@@ -182,8 +183,8 @@
 
 def part_kernel(blocks, base_ref, own_ref, values_ref, scale_ref, *refs):
     out_ref = refs[-1]
-    count = len(refs) // 5
-    tiles, weights, halos = refs[:count - 1], refs[count - 1:3 * count - 1], refs[3 * count - 1:-1]
+    count = (len(refs) + 2) // 5
+    tails, weights, halos = refs[:count - 1], refs[count - 1:3 * count - 2], refs[3 * count - 2:-1]
     n_slots, levels = values_ref.shape
     slots, wide = base_ref.shape
     members = wide // levels
@@ -198,16 +199,31 @@
     out_ref[slots:, :] = jnp.zeros((out_ref.shape[0] - slots, levels), f32)
     at = slots
     for t in range(count):
-        for ref in (halos[2 * t], halos[2 * t + 1]) + ((tiles[t],) if t < count - 1 else ()):
+        for ref in halos[2 * t:2 * t + 2] + tails[t:t + 1]:
             rows = ref[...] if ref.shape[0] == tail else ref[members * block:, :]
             out_ref[at:at + 2 * blocks, :] = rows.astype(f32)[0:2 * blocks]
             at += 2 * blocks
+    at += 2 * blocks
     mem = lax.axis_index("mem")
     for r in range(blocks):
         out_ref[at + r:at + r + 1, :] = owner_lanes(scale_ref[...], mem * n_slots - r * levels, levels)
     out_ref[0:slots, :] = total
     mine = pl.ds(pl.multiple_of(mem * n_slots, n_slots), n_slots)
     out_ref[mine, :] = out_ref[mine, :] - values_ref[...]
+
+
+def last_kernel(blocks, count, part_ref, own_ref, weight_ref, halo_ref, out_ref):
+    slots, block = weight_ref.shape
+    levels = part_ref.shape[1]
+    members = own_ref.shape[1] // levels
+    total = part_ref[0:slots, :]
+    for m in range(members):
+        lanes = slice(m * levels, (m + 1) * levels)
+        total += dot(weight_ref[...], halo_ref[m * block:(m + 1) * block, :]) * own_ref[:, lanes].astype(f32)
+    out_ref[0:slots, :] = total
+    out_ref[slots:, :] = part_ref[slots:, :]
+    at = slots + 2 * blocks * (3 * count - 2)
+    out_ref[at:at + 2 * blocks, :] = halo_ref[members * block:, :].astype(f32)[0:2 * blocks]
 
 
 def resid_kernel(blocks, tiles, own_ref, *refs):
@@ -230,7 +246,7 @@
     slots, levels = resid_ref.shape
     n_slots = mine_ref.shape[0]
     mine_ref[...] = resid_ref[pl.ds(pl.multiple_of(lax.axis_index("mem") * n_slots, n_slots), n_slots), :]
-    rim = taps_lon.shape[0] // 2
+    rim = taps_lon.shape[1] // 2
     lon_sign, lat_sign = signs("lon"), signs("lat")
     at = 0
     placed = []
@@ -321,20 +337,20 @@
     lon_pairs = pairings(lax.axis_size("lon"), True)
     lat_pairs = pairings(lax.axis_size("lat"), False)
     vmem = pl.BlockSpec(memory_space=pltpu.VMEM)
-    smem = pl.BlockSpec(memory_space=pltpu.SMEM)
     hbm = pl.BlockSpec(memory_space=pltpu.HBM)
     shape = jax.ShapeDtypeStruct
-    taps_lon = taps_lon.astype(bf16).astype(f32)
-    taps_lat = taps_lat.astype(bf16).astype(f32)
+    taps_lon, taps_lat = taps_lon.reshape(1, -1), taps_lat.reshape(1, -1)
     flat = controls.reshape(members, cells, levels)
 
     flank = rim * lon_tile
-    low, rim1, rim2, info, *sides = pl.pallas_call(
+    low = controls.astype(bf16).reshape(members * cells, levels)
+    rim1, rim2, info, *sides = pl.pallas_call(
         functools.partial(start_kernel, (rim, lon_tile, lat_tile, blocks)),
-        out_shape=[shape((members * cells, levels), bf16)] + [shape((members * edge + tail, levels), bf16)] * 2
-        + [shape((up8(2 * blocks), levels), f32)] + [shape((members * flank + tail, levels), bf16)] * len(lat_pairs),
-        in_specs=[vmem] * 2, out_specs=[vmem] * (4 + len(lat_pairs)), compiler_params=params(),
-    )(flat, obs_columns.reshape(1, n_slots))
+        out_shape=[shape((members * edge + tail, levels), bf16)] * 2 + [shape((up8(2 * blocks), levels), f32)]
+        + [shape((members * flank + tail, levels), bf16)] * len(lat_pairs),
+        in_specs=[vmem] * 2, out_specs=[vmem] * (3 + len(lat_pairs)),
+        scratch_shapes=[pltpu.VMEM((members * cells, levels), f32)], compiler_params=params(),
+    )(low, obs_columns.reshape(1, n_slots))
     halos = [lax.ppermute(r, "lon", p) for r, p in zip((rim1, rim2), lon_pairs)]
     sides = [lax.ppermute(r, "lat", p) for r, p in zip(sides, lat_pairs)]
     n_tiles = 1 + len(lat_pairs)
@@ -355,7 +371,7 @@
     base, *weights = pl.pallas_call(
         functools.partial(prep_kernel, (lon_tile, lat_tile, rim, members, blocks)),
         out_shape=[shape((slots, wide), f32)] + [shape((slots, edge), bf16)] * n_rims,
-        in_specs=[smem] * 2 + [vmem] * (1 + n_tiles), out_specs=[vmem] * (1 + n_rims), compiler_params=params(),
+        in_specs=[vmem] * (3 + n_tiles), out_specs=[vmem] * (1 + n_rims), compiler_params=params(),
     )(taps_lon, taps_lat, info, low, *sides)
 
     halos[0], own = lax.optimization_barrier((halos[0], own))
@@ -365,11 +381,16 @@
 
     tall = slots + up8(2 * blocks * (3 * n_tiles - 1) + blocks)
     tails = [t[members * flank:] for t in sides]
-    mine = pl.pallas_call(
+    part = pl.pallas_call(
         functools.partial(part_kernel, blocks),
         out_shape=shape((tall, levels), f32),
-        in_specs=[vmem] * (4 + len(tails) + 2 * len(rims)), out_specs=vmem, compiler_params=params(),
-    )(base, own, obs_values.reshape(n_slots, levels), scale, *tails, *weights, *rims)
+        in_specs=[vmem] * (2 + len(tails) + 2 * len(rims)), out_specs=vmem, compiler_params=params(),
+    )(base, own, obs_values.reshape(n_slots, levels), scale, *tails, *weights[:-1], *rims[:-1])
+    mine = pl.pallas_call(
+        functools.partial(last_kernel, blocks, n_tiles),
+        out_shape=shape((tall, levels), f32),
+        in_specs=[vmem] * 4, out_specs=vmem, compiler_params=params(),
+    )(part, own, weights[-1], rims[-1])
     terms = sum_terms(mine, n_mem)
 
     resid, send, extra = pl.pallas_call(
@@ -383,7 +404,7 @@
     weight, resid = pl.pallas_call(
         functools.partial(weight_kernel, (lon_tile, lat_tile, blocks, n_tiles)),
         out_shape=[shape((cells, count * slots), bf16), shape((n_slots, levels), f32)],
-        in_specs=[smem] * 2 + [vmem] * 3, out_specs=[vmem] * 2, compiler_params=params(),
+        in_specs=[vmem] * 5, out_specs=[vmem] * 2, compiler_params=params(),
     )(taps_lon, taps_lat, info, extra, resid)
     row[1], weight = lax.optimization_barrier((row[1], weight))
     around = []

time: 35.6 us -> 34.9 us (0.980)
  local copies, waits for them, and re-layouts: 1.96 us -> 0.04 us
  other arithmetic: 0.01 us -> 1.42 us
  Pallas kernels: 6 us -> 5.11 us
  starting transfers between devices: 22 us -> 22.7 us
    unnamed x16 -> x14, local copies, waits for them, and re-layouts: 1.96 us -> 0.03 us
    convert_element_type x1, other arithmetic: 0.01 us -> 1.41 us  [shards(): low = controls.astype(bf16).reshape(members * cells, levels)]
    ppermute x3, starting transfers between devices: 4.26 us -> 4.93 us  [shards(): around += [r] + [lax.ppermute(r, 'lat', q) for q in lat_pairs]]
    pallas_call x1, Pallas kernels: 1.62 us -> 1.1 us  [shards(): pl.pallas_call(functools.partial(weight_kernel, (lon_tile, lat_tile, bloc...]
    pallas_call x1, Pallas kernels: 1.19 us -> 0.68 us  [shards(): pl.pallas_call(functools.partial(prep_kernel, (lon_tile, lat_tile, rim, m...]
  transfers between devices with their start and end apart: 15 -> 15, of which waited for: 4 -> 4; matrix products, arithmetic and copies ran while one was open for 0% -> 0% of each run, Pallas kernels for 12% -> 11%
where the time goes in v5:
time: 34.9 us; the launch traced here: 34.7 us
  starting transfers between devices  22.7 us (65%)
  Pallas kernels  5.11 us (15%)
  waiting for transfers between devices  4.03 us (12%)
  between operations  1.48 us (4%)
  other arithmetic  1.42 us (4%)
    ppermute x3, starting transfers between devices, shards(): around += [r] + [lax.ppermute(r, 'lat', q) for q in lat_pairs]  4.93 us
    ppermute x2, starting transfers between devices, shards(): halos = [lax.ppermute(r, 'lon', p) for r, p in zip((rim1, rim2), lon_pairs)]  4.39 us
    ppermute x2, starting transfers between devices, shards(): rims += [lax.ppermute(h, 'lat', p) for h in halos]  2.89 us
    ppermute x2, starting transfers between devices, shards(): row = [send] + [lax.ppermute(send, 'lon', p) for p in lon_pairs]  2.72 us
    ppermute x3, starting transfers between devices, sum_terms(): lax.ppermute(x, 'mem', [(i, i ^ b) for i in range(count)])  2.71 us
    ppermute x2, starting transfers between devices, shards(): lax.ppermute(info, 'mem', [(i, i ^ step) for i in range(n_mem)])  2.65 us
    ppermute x3, waiting for transfers between devices, sum_terms(): lax.ppermute(x, 'mem', [(i, i ^ b) for i in range(count)])  2.59 us
    ppermute x1, starting transfers between devices, shards(): sides = [lax.ppermute(r, 'lat', p) for r, p in zip(sides, lat_pairs)]  2.37 us
  transfers between devices with their start and end apart: 15, of which 4 were waited for; matrix products, arithmetic and copies ran while one was open for 0% of the time, Pallas kernels for 11%

profile of v5, /device:TPU:1, one launch (start us, length us, event | category | flops | bytes accessed | tf_op | source)
XLA Modules:
  0.0 34.7 jit_solution(13235074167998099673)
XLA Ops:
  0.7 1.4 %convert_element_type.15 = bf16[4,24,24,128]{3,2,1,0:T(8,128)(2,1)S(1)} convert(f32[4,24,24,128]{3,2,1,0:T(8,128)} %param.8) | non-fusion elementwise | flops 294912 | bytes 1769472 | tf_op jit(solution)/shard_map/convert_element_type | solution.py:346
  2.3 2.2 %collective-permute-start = (bf16[784,128]{1,0:T(8,128)(2,1)S(1)}, bf16[784,128]{1,0:T(8,128)(2,1)S(1)}, u32[]{:S(2)}, u32[]{:S(2)}) collective-permute-start(bf16[784,128]{1,0:T(8,128)(2,1)S(1)} %get-tuple-element.24), channel_id=1, source_target_pairs={{0,8},{8,0},{16,24},{24,16},{1,9},{9,1},{17,25},{25,17},{2,10},{10... | collective-permute-start | bytes 602120 | tf_op jit(solution)/shard_map/ppermute | solution.py:354
  4.5 2.2 %collective-permute-start.4 = (bf16[784,128]{1,0:T(8,128)(2,1)S(1)}, bf16[784,128]{1,0:T(8,128)(2,1)S(1)}, u32[]{:S(2)}, u32[]{:S(2)}) collective-permute-start(bf16[784,128]{1,0:T(8,128)(2,1)S(1)} %get-tuple-element.35), channel_id=1, source_target_pairs={{0,24},{8,16},{16,8},{24,0},{1,25},{9,17},{17,9},{25,1},{2,26},{10... | collective-permute-start | bytes 602120 | tf_op jit(solution)/shard_map/ppermute | solution.py:354
  7.3 1.3 %collective-permute-start.1 = (f32[8,128]{1,0:T(8,128)S(1)}, f32[8,128]{1,0:T(8,128)S(1)}, u32[]{:S(2)}, u32[]{:S(2)}) collective-permute-start(f32[8,128]{1,0:T(8,128)S(1)} %get-tuple-element.26), channel_id=1, source_target_pairs={{0,1},{1,0},{2,3},{3,2},{4,5},{5,4},{6,7},{7,6},{8,9},{9,8},{10,11... | collective-permute-start | bytes 12296 | tf_op jit(solution)/shard_map/ppermute | solution.py:362
  8.6 1.4 %collective-permute-done.1 = f32[8,128]{1,0:T(8,128)S(1)} collective-permute-done((f32[8,128]{1,0:T(8,128)S(1)}, f32[8,128]{1,0:T(8,128)S(1)}, u32[]{:S(2)}, u32[]{:S(2)}) %collective-permute-start.1) | collective-permute-done | bytes 4128 | tf_op jit(solution)/shard_map/ppermute | solution.py:362
  10.0 1.4 %collective-permute-start.2 = (f32[8,128]{1,0:T(8,128)S(1)}, f32[8,128]{1,0:T(8,128)S(1)}, u32[]{:S(2)}, u32[]{:S(2)}) collective-permute-start(f32[8,128]{1,0:T(8,128)S(1)} %add.6), channel_id=1, source_target_pairs={{0,2},{1,3},{2,0},{3,1},{4,6},{5,7},{6,4},{7,5},{8,10},{9,11},{10,... | collective-permute-start | bytes 12296 | tf_op jit(solution)/shard_map/ppermute | solution.py:362
  11.4 2.4 %collective-permute-start.3 = (bf16[784,128]{1,0:T(8,128)(2,1)S(1)}, bf16[784,128]{1,0:T(8,128)(2,1)S(1)}, u32[]{:S(2)}, u32[]{:S(2)}) collective-permute-start(bf16[784,128]{1,0:T(8,128)(2,1)S(1)} %get-tuple-element.28), channel_id=1, source_target_pairs={{0,4},{4,0},{1,5},{5,1},{2,6},{6,2},{3,7},{7,3},{8,12},{12,8},{9,1... | collective-permute-start | bytes 602120 | tf_op jit(solution)/shard_map/ppermute | solution.py:355
  13.8 0.3 shard_map.96.own_ref
  14.1 2.1 %collective-permute-start.5 = (bf16[784,128]{1,0:T(8,128)(2,1)S(1)}, bf16[784,128]{1,0:T(8,128)(2,1)S(1)}, u32[]{:S(2)}, u32[]{:S(2)}) collective-permute-start(bf16[784,128]{1,0:T(8,128)(2,1)S(1)} %collective-permute-done.refs_4_), channel_id=1, source_target_pairs={{0,4},{4,0},{1,5},{5,1},{2,6},{6,2},{3,7},{7,3},{8,12},{12,8},{9,1... | collective-permute-start | bytes 602120 | tf_op jit(solution)/shard_map/ppermute | solution.py:380
  16.2 0.7 %collective-permute-start.6 = (bf16[784,128]{1,0:T(8,128)(2,1)S(1)}, bf16[784,128]{1,0:T(8,128)(2,1)S(1)}, u32[]{:S(2)}, u32[]{:S(2)}) collective-permute-start(bf16[784,128]{1,0:T(8,128)(2,1)S(1)} %collective-permute-done.4.refs_5_), channel_id=1, source_target_pairs={{0,4},{4,0},{1,5},{5,1},{2,6},{6,2},{3,7},{7,3},{8,12},{12,8},{9,1... | collective-permute-start | bytes 602120 | tf_op jit(solution)/shard_map/ppermute | solution.py:380
  17.0 0.7 %shard_map.97 = (f32[64,512]{1,0:T(8,128)S(1)}, bf16[64,192]{1,0:T(8,128)(2,1)S(1)}, bf16[64,192]{1,0:T(8,128)(2,1)S(1)}, bf16[64,192]{1,0:T(8,128)(2,1)S(1)}, bf16[64,192]{1,0:T(8,128)(2,1)S(1)}) custom-call(f32[1,17]{1,0:T(1,128)S(1)} %bitcast.18, f32[1,17]{1,0:T(1,128)S(1)} %bitcast.20, f32[8,128]{1,0:T(8,128)S(1)} %add.7.info_ref, ...), custom_call_target="tpu_custom_call" | custom-call | tf_op jit(solution)/shard_map/pallas_call | solution.py:371
  17.7 0.3 shard_map.98.part_ref
  18.3 2.2 %collective-permute-start.9 = (f32[80,128]{1,0:T(8,128)S(1)}, f32[80,128]{1,0:T(8,128)S(1)}, u32[]{:S(2)}, u32[]{:S(2)}) collective-permute-start(f32[80,128]{1,0:T(8,128)S(1)} %shard_map.99.refs_0_), channel_id=1, source_target_pairs={{0,3},{1,2},{2,1},{3,0},{4,7},{5,6},{6,5},{7,4},{8,11},{9,10},{10,... | collective-permute-start | bytes 122888 | tf_op jit(solution)/shard_map/ppermute | solution.py:30
  20.5 0.2 collective-permute-start.8
  20.7 0.3 collective-permute-start.7
  21.0 1.1 %collective-permute-done.9.refs_3_ = f32[80,128]{1,0:T(8,128)S(1)} collective-permute-done((f32[80,128]{1,0:T(8,128)S(1)}, f32[80,128]{1,0:T(8,128)S(1)}, u32[]{:S(2)}, u32[]{:S(2)}) %collective-permute-start.9) | collective-permute-done | bytes 40992 | tf_op jit(solution)/shard_map/ppermute | solution.py:30
  22.1 1.3 %collective-permute-done.8.refs_2_ = f32[80,128]{1,0:T(8,128)S(1)} collective-permute-done((f32[80,128]{1,0:T(8,128)S(1)}, f32[80,128]{1,0:T(8,128)S(1)}, u32[]{:S(2)}, u32[]{:S(2)}) %collective-permute-start.8) | collective-permute-done | bytes 40992 | tf_op jit(solution)/shard_map/ppermute | solution.py:30
  23.7 0.4 %collective-permute-start.10 = (bf16[64,512]{1,0:T(8,128)(2,1)S(1)}, bf16[64,512]{1,0:T(8,128)(2,1)S(1)}, u32[]{:S(2)}, u32[]{:S(2)}) collective-permute-start(bf16[64,512]{1,0:T(8,128)(2,1)S(1)} %get-tuple-element.37.refs_0_), channel_id=1, source_target_pairs={{0,8},{8,0},{16,24},{24,16},{1,9},{9,1},{17,25},{25,17},{2,10},{10... | collective-permute-start | bytes 196616 | tf_op jit(solution)/shard_map/ppermute | solution.py:402
  24.1 2.4 %collective-permute-start.13 = (bf16[64,512]{1,0:T(8,128)(2,1)S(1)}, bf16[64,512]{1,0:T(8,128)(2,1)S(1)}, u32[]{:S(2)}, u32[]{:S(2)}) collective-permute-start(bf16[64,512]{1,0:T(8,128)(2,1)S(1)} %get-tuple-element.37.refs_0_), channel_id=1, source_target_pairs={{0,24},{8,16},{16,8},{24,0},{1,25},{9,17},{17,9},{25,1},{2,26},{10... | collective-permute-start | bytes 196616 | tf_op jit(solution)/shard_map/ppermute | solution.py:402
  26.4 2.6 %collective-permute-start.11 = (bf16[64,512]{1,0:T(8,128)(2,1)S(1)}, bf16[64,512]{1,0:T(8,128)(2,1)S(1)}, u32[]{:S(2)}, u32[]{:S(2)}) collective-permute-start(bf16[64,512]{1,0:T(8,128)(2,1)S(1)} %get-tuple-element.37.refs_0_), channel_id=1, source_target_pairs={{0,4},{4,0},{1,5},{5,1},{2,6},{6,2},{3,7},{7,3},{8,12},{12,8},{9,1... | collective-permute-start | bytes 196616 | tf_op jit(solution)/shard_map/ppermute | solution.py:412
  29.1 1.1 %shard_map.101 = (bf16[576,384]{1,0:T(8,128)(2,1)S(1)}, f32[16,128]{1,0:T(8,128)}) custom-call(f32[1,17]{1,0:T(1,128)S(1)} %bitcast.19, f32[1,17]{1,0:T(1,128)S(1)} %bitcast.21, f32[8,128]{1,0:T(8,128)S(1)} %add.7.info_ref, f32[16,128]{1,0:T(8,128)S(1)} %get-tuple-element.38.extra_ref, f32[64,128]{1,0:T(8,128)S(1)} %get-tuple-element.39.resid_ref), custom_call_target="tpu_custom_call" | custom-call | tf_op jit(solution)/shard_map/pallas_call | solution.py:404
  30.4 2.1 %collective-permute-start.14 = (bf16[64,512]{1,0:T(8,128)(2,1)S(1)}, bf16[64,512]{1,0:T(8,128)(2,1)S(1)}, u32[]{:S(2)}, u32[]{:S(2)}) collective-permute-start(bf16[64,512]{1,0:T(8,128)(2,1)S(1)} %collective-permute-done.13.refs_0_), channel_id=1, source_target_pairs={{0,4},{4,0},{1,5},{5,1},{2,6},{6,2},{3,7},{7,3},{8,12},{12,8},{9,1... | collective-permute-start | bytes 196616 | tf_op jit(solution)/shard_map/ppermute | solution.py:412
  32.5 1.3 %shard_map.102 = (f32[4,576,128]{2,1,0:T(8,128)}, f32[4,192,128]{2,1,0:T(8,128)S(1)}) custom-call(bf16[576,384]{1,0:T(8,128)(2,1)S(1)} %get-tuple-element.41.weight_ref, f32[4,576,128]{2,1,0:T(8,128)S(1)} %bitcast.15, bf16[64,512]{1,0:T(8,128)(2,1)S(1)} %get-tuple-element.37.refs_0_, bf16[64,512]{1,0:T(8,128)(2,1)S(1)} %collective-permute-done.11.refs_1_, ...), custom_call_target="tpu_custom_call" | custom-call | tf_op jit(solution)/shard_map/pallas_call | solution.py:415
  33.8 1.0 %shard_map.103 = f32[4,576,128]{2,1,0:T(8,128)} custom-call(bf16[576,384]{1,0:T(8,128)(2,1)S(1)} %get-tuple-element.41.weight_ref, f32[4,192,128]{2,1,0:T(8,128)S(1)} %get-tuple-element.43.rest_ref, f32[4,576,128]{2,1,0:T(8,128)} %get-tuple-element.44.begun_hbm, bf16[64,512]{1,0:T(8,128)(2,1)S(1)} %collective-permute-done.13.refs_0_, ...), custom_call_target="tpu_custom_call", output_to_operand_aliasing={{}: (2, {})} | custom-call | tf_op jit(solution)/shard_map/pallas_call | solution.py:426
  (34 shorter events, 0.9 us)
Async XLA Ops:
  0.6 1.5 %copy-start.5 = (s32[1,1,1,16]{3,2,1,0:T(1,128)S(1)}, s32[1,1,1,16]{3,2,1,0:T(1,128)}, u32[]{:S(2)}) copy-start(s32[1,1,1,16]{3,2,1,0:T(1,128)} %param.12) | copy-start | bytes 196
  0.6 6.7 %copy-start.6 = (s32[1,1,1,16]{3,2,1,0:T(1,128)S(1)}, s32[1,1,1,16]{3,2,1,0:T(1,128)}, u32[]{:S(2)}) copy-start(s32[1,1,1,16]{3,2,1,0:T(1,128)} %param.14) | copy-start | bytes 196
  0.7 13.1 %copy-start.1 = (bf16[4,24,24,128]{3,2,1,0:T(8,128)(2,1)S(1)}, bf16[4,24,24,128]{3,2,1,0:T(8,128)(2,1)}, u32[]{:S(2)}) copy-start(bf16[4,24,24,128]{3,2,1,0:T(8,128)(2,1)} %param.9) | copy-start | bytes 1769476
  0.7 16.3 %copy-start.4 = (f32[17]{0:T(128)S(1)}, f32[17]{0:T(128)}, u32[]{:S(2)}) copy-start(f32[17]{0:T(128)} %param.11) | copy-start | bytes 208
  0.7 16.3 %copy-start.3 = (f32[17]{0:T(128)S(1)}, f32[17]{0:T(128)}, u32[]{:S(2)}) copy-start(f32[17]{0:T(128)} %param.10) | copy-start | bytes 208
  2.1 15.6 %copy-start.2 = (f32[1,1,1,16,128]{4,3,2,1,0:T(8,128)S(1)}, f32[1,1,1,16,128]{4,3,2,1,0:T(8,128)}, u32[]{:S(2)}) copy-start(f32[1,1,1,16,128]{4,3,2,1,0:T(8,128)} %param.15) | copy-start | bytes 24580
  2.3 11.8 %collective-permute-start = (bf16[784,128]{1,0:T(8,128)(2,1)S(1)}, bf16[784,128]{1,0:T(8,128)(2,1)S(1)}, u32[]{:S(2)}, u32[]{:S(2)}) collective-permute-start(bf16[784,128]{1,0:T(8,128)(2,1)S(1)} %get-tuple-element.24), channel_id=1, source_target_pairs={{0,8},{8,0},{16,24},{24,16},{1,9},{9,1},{17,25},{25,17},{2,10},{10... | collective-permute-start | bytes 602120 | tf_op jit(solution)/shard_map/ppermute | solution.py:354
  4.5 11.8 %collective-permute-start.4 = (bf16[784,128]{1,0:T(8,128)(2,1)S(1)}, bf16[784,128]{1,0:T(8,128)(2,1)S(1)}, u32[]{:S(2)}, u32[]{:S(2)}) collective-permute-start(bf16[784,128]{1,0:T(8,128)(2,1)S(1)} %get-tuple-element.35), channel_id=1, source_target_pairs={{0,24},{8,16},{16,8},{24,0},{1,25},{9,17},{17,9},{25,1},{2,26},{10... | collective-permute-start | bytes 602120 | tf_op jit(solution)/shard_map/ppermute | solution.py:354
  7.3 2.7 %collective-permute-start.1 = (f32[8,128]{1,0:T(8,128)S(1)}, f32[8,128]{1,0:T(8,128)S(1)}, u32[]{:S(2)}, u32[]{:S(2)}) collective-permute-start(f32[8,128]{1,0:T(8,128)S(1)} %get-tuple-element.26), channel_id=1, source_target_pairs={{0,1},{1,0},{2,3},{3,2},{4,5},{5,4},{6,7},{7,6},{8,9},{9,8},{10,11... | collective-permute-start | bytes 12296 | tf_op jit(solution)/shard_map/ppermute | solution.py:362
  10.0 3.8 %collective-permute-start.2 = (f32[8,128]{1,0:T(8,128)S(1)}, f32[8,128]{1,0:T(8,128)S(1)}, u32[]{:S(2)}, u32[]{:S(2)}) collective-permute-start(f32[8,128]{1,0:T(8,128)S(1)} %add.6), channel_id=1, source_target_pairs={{0,2},{1,3},{2,0},{3,1},{4,6},{5,7},{6,4},{7,5},{8,10},{9,11},{10,... | collective-permute-start | bytes 12296 | tf_op jit(solution)/shard_map/ppermute | solution.py:362
  11.4 5.6 %collective-permute-start.3 = (bf16[784,128]{1,0:T(8,128)(2,1)S(1)}, bf16[784,128]{1,0:T(8,128)(2,1)S(1)}, u32[]{:S(2)}, u32[]{:S(2)}) collective-permute-start(bf16[784,128]{1,0:T(8,128)(2,1)S(1)} %get-tuple-element.28), channel_id=1, source_target_pairs={{0,4},{4,0},{1,5},{5,1},{2,6},{6,2},{3,7},{7,3},{8,12},{12,8},{9,1... | collective-permute-start | bytes 602120 | tf_op jit(solution)/shard_map/ppermute | solution.py:355
  14.1 3.6 %collective-permute-start.5 = (bf16[784,128]{1,0:T(8,128)(2,1)S(1)}, bf16[784,128]{1,0:T(8,128)(2,1)S(1)}, u32[]{:S(2)}, u32[]{:S(2)}) collective-permute-start(bf16[784,128]{1,0:T(8,128)(2,1)S(1)} %collective-permute-done.refs_4_), channel_id=1, source_target_pairs={{0,4},{4,0},{1,5},{5,1},{2,6},{6,2},{3,7},{7,3},{8,12},{12,8},{9,1... | collective-permute-start | bytes 602120 | tf_op jit(solution)/shard_map/ppermute | solution.py:380
  16.2 1.8 %collective-permute-start.6 = (bf16[784,128]{1,0:T(8,128)(2,1)S(1)}, bf16[784,128]{1,0:T(8,128)(2,1)S(1)}, u32[]{:S(2)}, u32[]{:S(2)}) collective-permute-start(bf16[784,128]{1,0:T(8,128)(2,1)S(1)} %collective-permute-done.4.refs_5_), channel_id=1, source_target_pairs={{0,4},{4,0},{1,5},{5,1},{2,6},{6,2},{3,7},{7,3},{8,12},{12,8},{9,1... | collective-permute-start | bytes 602120 | tf_op jit(solution)/shard_map/ppermute | solution.py:380
  17.0 15.5 %copy-start = (f32[4,24,24,128]{3,2,1,0:T(8,128)S(1)}, f32[4,24,24,128]{3,2,1,0:T(8,128)}, u32[]{:S(2)}) copy-start(f32[4,24,24,128]{3,2,1,0:T(8,128)} %param.8) | copy-start | bytes 3538948
  18.3 3.8 %collective-permute-start.9 = (f32[80,128]{1,0:T(8,128)S(1)}, f32[80,128]{1,0:T(8,128)S(1)}, u32[]{:S(2)}, u32[]{:S(2)}) collective-permute-start(f32[80,128]{1,0:T(8,128)S(1)} %shard_map.99.refs_0_), channel_id=1, source_target_pairs={{0,3},{1,2},{2,1},{3,0},{4,7},{5,6},{6,5},{7,4},{8,11},{9,10},{10,... | collective-permute-start | bytes 122888 | tf_op jit(solution)/shard_map/ppermute | solution.py:30
  20.5 2.9 %collective-permute-start.8 = (f32[80,128]{1,0:T(8,128)S(1)}, f32[80,128]{1,0:T(8,128)S(1)}, u32[]{:S(2)}, u32[]{:S(2)}) collective-permute-start(f32[80,128]{1,0:T(8,128)S(1)} %shard_map.99.refs_0_), channel_id=1, source_target_pairs={{0,2},{1,3},{2,0},{3,1},{4,6},{5,7},{6,4},{7,5},{8,10},{9,11},{10,... | collective-permute-start | bytes 122888 | tf_op jit(solution)/shard_map/ppermute | solution.py:30
  20.7 2.9 %collective-permute-start.7 = (f32[80,128]{1,0:T(8,128)S(1)}, f32[80,128]{1,0:T(8,128)S(1)}, u32[]{:S(2)}, u32[]{:S(2)}) collective-permute-start(f32[80,128]{1,0:T(8,128)S(1)} %shard_map.99.refs_0_), channel_id=1, source_target_pairs={{0,1},{1,0},{2,3},{3,2},{4,5},{5,4},{6,7},{7,6},{8,9},{9,8},{10,11... | collective-permute-start | bytes 122888 | tf_op jit(solution)/shard_map/ppermute | solution.py:30
  23.7 6.5 %collective-permute-start.10 = (bf16[64,512]{1,0:T(8,128)(2,1)S(1)}, bf16[64,512]{1,0:T(8,128)(2,1)S(1)}, u32[]{:S(2)}, u32[]{:S(2)}) collective-permute-start(bf16[64,512]{1,0:T(8,128)(2,1)S(1)} %get-tuple-element.37.refs_0_), channel_id=1, source_target_pairs={{0,8},{8,0},{16,24},{24,16},{1,9},{9,1},{17,25},{25,17},{2,10},{10... | collective-permute-start | bytes 196616 | tf_op jit(solution)/shard_map/ppermute | solution.py:402
  24.1 6.3 %collective-permute-start.13 = (bf16[64,512]{1,0:T(8,128)(2,1)S(1)}, bf16[64,512]{1,0:T(8,128)(2,1)S(1)}, u32[]{:S(2)}, u32[]{:S(2)}) collective-permute-start(bf16[64,512]{1,0:T(8,128)(2,1)S(1)} %get-tuple-element.37.refs_0_), channel_id=1, source_target_pairs={{0,24},{8,16},{16,8},{24,0},{1,25},{9,17},{17,9},{25,1},{2,26},{10... | collective-permute-start | bytes 196616 | tf_op jit(solution)/shard_map/ppermute | solution.py:402
  26.4 6.0 %collective-permute-start.11 = (bf16[64,512]{1,0:T(8,128)(2,1)S(1)}, bf16[64,512]{1,0:T(8,128)(2,1)S(1)}, u32[]{:S(2)}, u32[]{:S(2)}) collective-permute-start(bf16[64,512]{1,0:T(8,128)(2,1)S(1)} %get-tuple-element.37.refs_0_), channel_id=1, source_target_pairs={{0,4},{4,0},{1,5},{5,1},{2,6},{6,2},{3,7},{7,3},{8,12},{12,8},{9,1... | collective-permute-start | bytes 196616 | tf_op jit(solution)/shard_map/ppermute | solution.py:412
  30.2 2.3 %collective-permute-start.12 = (bf16[64,512]{1,0:T(8,128)(2,1)S(1)}, bf16[64,512]{1,0:T(8,128)(2,1)S(1)}, u32[]{:S(2)}, u32[]{:S(2)}) collective-permute-start(bf16[64,512]{1,0:T(8,128)(2,1)S(1)} %collective-permute-done.10.refs_2_), channel_id=1, source_target_pairs={{0,4},{4,0},{1,5},{5,1},{2,6},{6,2},{3,7},{7,3},{8,12},{12,8},{9,1... | collective-permute-start | bytes 196616 | tf_op jit(solution)/shard_map/ppermute | solution.py:412
  30.4 3.4 %collective-permute-start.14 = (bf16[64,512]{1,0:T(8,128)(2,1)S(1)}, bf16[64,512]{1,0:T(8,128)(2,1)S(1)}, u32[]{:S(2)}, u32[]{:S(2)}) collective-permute-start(bf16[64,512]{1,0:T(8,128)(2,1)S(1)} %collective-permute-done.13.refs_0_), channel_id=1, source_target_pairs={{0,4},{4,0},{1,5},{5,1},{2,6},{6,2},{3,7},{7,3},{8,12},{12,8},{9,1... | collective-permute-start | bytes 196616 | tf_op jit(solution)/shard_map/ppermute | solution.py:412

commit v6 on v5

--- a/solution.py
+++ b/solution.py
@@ -91,11 +91,9 @@
     return pltpu.CompilerParams(vmem_limit_bytes=mib * 1024 * 1024)
 
 
-def start_kernel(dims, low_ref, col_ref, rim1_ref, rim2_ref, info_ref, *refs):
-    rim, lon_tile, lat_tile, blocks = dims
-    side_refs, con_ref = refs[:-1], refs[-1]
-    edge, cells = rim * lat_tile, lon_tile * lat_tile
-    members, levels = low_ref.shape[0] // cells, low_ref.shape[1]
+def start_kernel(dims, first_ref, last_ref, col_ref, rim1_ref, rim2_ref, info_ref):
+    lat_tile, blocks = dims
+    edge, levels = first_ref.shape
     n_slots = col_ref.shape[1]
     mem = lax.axis_index("mem")
     column = col_ref[...].astype(f32)
@@ -109,22 +107,39 @@
             moved = owner_lanes(lanes, mem * n_slots - r * levels, levels)
             info_ref[f * blocks + r:f * blocks + r + 1, :] = moved
             placed = jnp.where(row == f * blocks + r, moved, placed)
-    placed = placed.astype(bf16)
     even = lax.axis_index("lon") % 2 == 0
-    far = cells - edge
-    for at, ref in ((jnp.where(even, far, 0), rim1_ref), (jnp.where(even, 0, far), rim2_ref)):
-        for m in range(members):
-            ref[m * edge:(m + 1) * edge, :] = low_ref[pl.ds(pl.multiple_of(at + m * cells, 16), edge), :]
-        ref[members * edge:, :] = placed
-    con_ref[...] = low_ref[...].astype(f32)
+
+    @pl.when(even)
+    def _():
+        rim1_ref[0:edge, :] = last_ref[...].astype(bf16)
+        rim2_ref[0:edge, :] = first_ref[...].astype(bf16)
+
+    @pl.when(jnp.logical_not(even))
+    def _():
+        rim1_ref[0:edge, :] = first_ref[...].astype(bf16)
+        rim2_ref[0:edge, :] = last_ref[...].astype(bf16)
+
+    for ref in (rim1_ref, rim2_ref):
+        ref[edge:, :] = placed.astype(bf16)
+
+
+def low_kernel(dims, con_ref, info_ref, low_ref, *side_refs):
+    rim, lon_tile, lat_tile, blocks = dims
+    members, cells, levels = con_ref.shape
+    row = lax.broadcasted_iota(jnp.int32, (tail, levels), 0)
+    placed = jnp.zeros((tail, levels), f32)
+    for r in range(2 * blocks):
+        placed = jnp.where(row == r, info_ref[r:r + 1, :], placed)
     for ref, sign in zip(side_refs, signs("lat")):
         at = jnp.where(sign > 0, lat_tile - rim, 0)
         for m in range(members):
             for i in range(0, lon_tile, 2):
-                pair = [con_ref[pl.ds(pl.multiple_of(at + (m * lon_tile + i + k) * lat_tile, 8), rim), :] for k in range(2)]
+                pair = [con_ref[m, pl.ds(pl.multiple_of(at + (i + k) * lat_tile, 8), rim), :] for k in range(2)]
                 row_at = (m * lon_tile + i) * rim
                 ref[row_at:row_at + 2 * rim, :] = jnp.concatenate(pair, axis=0).astype(bf16)
-        ref[members * lon_tile * rim:, :] = placed
+        ref[members * lon_tile * rim:, :] = placed.astype(bf16)
+    for m in range(members):
+        low_ref[m * cells:(m + 1) * cells, :] = con_ref[m].astype(bf16)
 
 
 def pick_kernel(lat_tile, blocks, info_ref, ens_ref, out_ref):
@@ -343,14 +358,18 @@
     flat = controls.reshape(members, cells, levels)
 
     flank = rim * lon_tile
-    low = controls.astype(bf16).reshape(members * cells, levels)
-    rim1, rim2, info, *sides = pl.pallas_call(
-        functools.partial(start_kernel, (rim, lon_tile, lat_tile, blocks)),
-        out_shape=[shape((members * edge + tail, levels), bf16)] * 2 + [shape((up8(2 * blocks), levels), f32)]
-        + [shape((members * flank + tail, levels), bf16)] * len(lat_pairs),
-        in_specs=[vmem] * 2, out_specs=[vmem] * (3 + len(lat_pairs)),
-        scratch_shapes=[pltpu.VMEM((members * cells, levels), f32)], compiler_params=params(),
-    )(low, obs_columns.reshape(1, n_slots))
+    first = controls[:, :rim].reshape(members * edge, levels)
+    last = controls[:, lon_tile - rim:].reshape(members * edge, levels)
+    rim1, rim2, info = pl.pallas_call(
+        functools.partial(start_kernel, (lat_tile, blocks)),
+        out_shape=[shape((members * edge + tail, levels), bf16)] * 2 + [shape((up8(2 * blocks), levels), f32)],
+        in_specs=[vmem] * 3, out_specs=[vmem] * 3, compiler_params=params(),
+    )(first, last, obs_columns.reshape(1, n_slots))
+    low, *sides = pl.pallas_call(
+        functools.partial(low_kernel, (rim, lon_tile, lat_tile, blocks)),
+        out_shape=[shape((members * cells, levels), bf16)] + [shape((members * flank + tail, levels), bf16)] * len(lat_pairs),
+        in_specs=[vmem] * 2, out_specs=[vmem] * (1 + len(lat_pairs)), compiler_params=params(),
+    )(flat, info)
     halos = [lax.ppermute(r, "lon", p) for r, p in zip((rim1, rim2), lon_pairs)]
     sides = [lax.ppermute(r, "lat", p) for r, p in zip(sides, lat_pairs)]
     n_tiles = 1 + len(lat_pairs)

time: 34.9 us -> 34.8 us (level)
  other arithmetic: 1.42 us -> 0.01 us
  local copies, waits for them, and re-layouts: 0.04 us -> 1.3 us
    convert_element_type x1 -> x0, other arithmetic: 1.41 us -> none  [shards(): low = controls.astype(bf16).reshape(members * cells, levels)]
    slice x0 -> x1, local copies, waits for them, and re-layouts: none -> 1.26 us  [shards(): last = controls[:, lon_tile - rim:].reshape(members * edge, levels)]
where the time goes in v6:
time: 34.8 us; the launch traced here: 34.6 us
  starting transfers between devices  22.6 us (65%)
  Pallas kernels  5.15 us (15%)
  waiting for transfers between devices  4.06 us (12%)
  between operations  1.47 us (4%)
  local copies, waits for them, and re-layouts  1.3 us (4%)
    ppermute x3, starting transfers between devices, shards(): around += [r] + [lax.ppermute(r, 'lat', q) for q in lat_pairs]  4.95 us
    ppermute x2, starting transfers between devices, shards(): halos = [lax.ppermute(r, 'lon', p) for r, p in zip((rim1, rim2), lon_pairs)]  4.39 us
    ppermute x2, starting transfers between devices, shards(): row = [send] + [lax.ppermute(send, 'lon', p) for p in lon_pairs]  2.75 us
    ppermute x2, starting transfers between devices, shards(): rims += [lax.ppermute(h, 'lat', p) for h in halos]  2.74 us
    ppermute x3, starting transfers between devices, sum_terms(): lax.ppermute(x, 'mem', [(i, i ^ b) for i in range(count)])  2.71 us
    ppermute x2, starting transfers between devices, shards(): lax.ppermute(info, 'mem', [(i, i ^ step) for i in range(n_mem)])  2.63 us
    ppermute x3, waiting for transfers between devices, sum_terms(): lax.ppermute(x, 'mem', [(i, i ^ b) for i in range(count)])  2.6 us
    ppermute x1, starting transfers between devices, shards(): sides = [lax.ppermute(r, 'lat', p) for r, p in zip(sides, lat_pairs)]  2.44 us
  transfers between devices with their start and end apart: 15, of which 4 were waited for; matrix products, arithmetic and copies ran while one was open for 0% of the time, Pallas kernels for 11%

profile of v6, /device:TPU:1, one launch (start us, length us, event | category | flops | bytes accessed | tf_op | source)
XLA Modules:
  0.0 34.6 jit_solution(4568419106843255201)
XLA Ops:
  0.7 1.3 %fusion = (f32[4,8,24,128]{3,2,1,0:T(8,128)S(1)}, f32[4,8,24,128]{3,2,1,0:T(8,128)S(1)}) fusion(f32[4,24,24,128]{3,2,1,0:T(8,128)} %param.8), kind=kLoop, calls=%fused_computation.1 | loop fusion | bytes 1572864 | tf_op jit(solution)/shard_map/slice | solution.py:362
  2.1 2.2 %collective-permute-start = (bf16[784,128]{1,0:T(8,128)(2,1)S(1)}, bf16[784,128]{1,0:T(8,128)(2,1)S(1)}, u32[]{:S(2)}, u32[]{:S(2)}) collective-permute-start(bf16[784,128]{1,0:T(8,128)(2,1)S(1)} %get-tuple-element.25), channel_id=1, source_target_pairs={{0,8},{8,0},{16,24},{24,16},{1,9},{9,1},{17,25},{25,17},{2,10},{10... | collective-permute-start | bytes 602120 | tf_op jit(solution)/shard_map/ppermute | solution.py:373
  4.3 2.2 %collective-permute-start.4 = (bf16[784,128]{1,0:T(8,128)(2,1)S(1)}, bf16[784,128]{1,0:T(8,128)(2,1)S(1)}, u32[]{:S(2)}, u32[]{:S(2)}) collective-permute-start(bf16[784,128]{1,0:T(8,128)(2,1)S(1)} %get-tuple-element.37), channel_id=1, source_target_pairs={{0,24},{8,16},{16,8},{24,0},{1,25},{9,17},{17,9},{25,1},{2,26},{10... | collective-permute-start | bytes 602120 | tf_op jit(solution)/shard_map/ppermute | solution.py:373
  7.1 1.3 %collective-permute-start.1 = (f32[8,128]{1,0:T(8,128)S(1)}, f32[8,128]{1,0:T(8,128)S(1)}, u32[]{:S(2)}, u32[]{:S(2)}) collective-permute-start(f32[8,128]{1,0:T(8,128)S(1)} %get-tuple-element.27.info_ref), channel_id=1, source_target_pairs={{0,1},{1,0},{2,3},{3,2},{4,5},{5,4},{6,7},{7,6},{8,9},{9,8},{10,11... | collective-permute-start | bytes 12296 | tf_op jit(solution)/shard_map/ppermute | solution.py:381
  8.4 1.4 %collective-permute-done.1 = f32[8,128]{1,0:T(8,128)S(1)} collective-permute-done((f32[8,128]{1,0:T(8,128)S(1)}, f32[8,128]{1,0:T(8,128)S(1)}, u32[]{:S(2)}, u32[]{:S(2)}) %collective-permute-start.1) | collective-permute-done | bytes 4128 | tf_op jit(solution)/shard_map/ppermute | solution.py:381
  9.9 1.3 %collective-permute-start.2 = (f32[8,128]{1,0:T(8,128)S(1)}, f32[8,128]{1,0:T(8,128)S(1)}, u32[]{:S(2)}, u32[]{:S(2)}) collective-permute-start(f32[8,128]{1,0:T(8,128)S(1)} %add.6), channel_id=1, source_target_pairs={{0,2},{1,3},{2,0},{3,1},{4,6},{5,7},{6,4},{7,5},{8,10},{9,11},{10,... | collective-permute-start | bytes 12296 | tf_op jit(solution)/shard_map/ppermute | solution.py:381
  11.3 2.4 %collective-permute-start.3 = (bf16[784,128]{1,0:T(8,128)(2,1)S(1)}, bf16[784,128]{1,0:T(8,128)(2,1)S(1)}, u32[]{:S(2)}, u32[]{:S(2)}) collective-permute-start(bf16[784,128]{1,0:T(8,128)(2,1)S(1)} %get-tuple-element.30), channel_id=1, source_target_pairs={{0,4},{4,0},{1,5},{5,1},{2,6},{6,2},{3,7},{7,3},{8,12},{12,8},{9,1... | collective-permute-start | bytes 602120 | tf_op jit(solution)/shard_map/ppermute | solution.py:374
  13.7 0.3 shard_map.96.own_ref
  14.1 2.0 %collective-permute-start.5 = (bf16[784,128]{1,0:T(8,128)(2,1)S(1)}, bf16[784,128]{1,0:T(8,128)(2,1)S(1)}, u32[]{:S(2)}, u32[]{:S(2)}) collective-permute-start(bf16[784,128]{1,0:T(8,128)(2,1)S(1)} %collective-permute-done.refs_4_), channel_id=1, source_target_pairs={{0,4},{4,0},{1,5},{5,1},{2,6},{6,2},{3,7},{7,3},{8,12},{12,8},{9,1... | collective-permute-start | bytes 602120 | tf_op jit(solution)/shard_map/ppermute | solution.py:399
  16.1 0.7 %collective-permute-start.6 = (bf16[784,128]{1,0:T(8,128)(2,1)S(1)}, bf16[784,128]{1,0:T(8,128)(2,1)S(1)}, u32[]{:S(2)}, u32[]{:S(2)}) collective-permute-start(bf16[784,128]{1,0:T(8,128)(2,1)S(1)} %collective-permute-done.4.refs_5_), channel_id=1, source_target_pairs={{0,4},{4,0},{1,5},{5,1},{2,6},{6,2},{3,7},{7,3},{8,12},{12,8},{9,1... | collective-permute-start | bytes 602120 | tf_op jit(solution)/shard_map/ppermute | solution.py:399
  16.8 0.7 %shard_map.98 = (f32[64,512]{1,0:T(8,128)S(1)}, bf16[64,192]{1,0:T(8,128)(2,1)S(1)}, bf16[64,192]{1,0:T(8,128)(2,1)S(1)}, bf16[64,192]{1,0:T(8,128)(2,1)S(1)}, bf16[64,192]{1,0:T(8,128)(2,1)S(1)}) custom-call(f32[1,17]{1,0:T(1,128)S(1)} %bitcast.20, f32[1,17]{1,0:T(1,128)S(1)} %bitcast.22, f32[8,128]{1,0:T(8,128)S(1)} %add.7.info_ref, ...), custom_call_target="tpu_custom_call" | custom-call | tf_op jit(solution)/shard_map/pallas_call | solution.py:390
  17.5 0.3 shard_map.99.part_ref
  18.1 2.2 %collective-permute-start.9 = (f32[80,128]{1,0:T(8,128)S(1)}, f32[80,128]{1,0:T(8,128)S(1)}, u32[]{:S(2)}, u32[]{:S(2)}) collective-permute-start(f32[80,128]{1,0:T(8,128)S(1)} %shard_map.100.refs_0_), channel_id=1, source_target_pairs={{0,3},{1,2},{2,1},{3,0},{4,7},{5,6},{6,5},{7,4},{8,11},{9,10},{10,... | collective-permute-start | bytes 122888 | tf_op jit(solution)/shard_map/ppermute | solution.py:30
  20.3 0.2 collective-permute-start.8
  20.6 0.3 collective-permute-start.7
  20.8 1.1 %collective-permute-done.9.refs_3_ = f32[80,128]{1,0:T(8,128)S(1)} collective-permute-done((f32[80,128]{1,0:T(8,128)S(1)}, f32[80,128]{1,0:T(8,128)S(1)}, u32[]{:S(2)}, u32[]{:S(2)}) %collective-permute-start.9) | collective-permute-done | bytes 40992 | tf_op jit(solution)/shard_map/ppermute | solution.py:30
  21.9 1.3 %collective-permute-done.8.refs_2_ = f32[80,128]{1,0:T(8,128)S(1)} collective-permute-done((f32[80,128]{1,0:T(8,128)S(1)}, f32[80,128]{1,0:T(8,128)S(1)}, u32[]{:S(2)}, u32[]{:S(2)}) %collective-permute-start.8) | collective-permute-done | bytes 40992 | tf_op jit(solution)/shard_map/ppermute | solution.py:30
  23.5 0.4 %collective-permute-start.10 = (bf16[64,512]{1,0:T(8,128)(2,1)S(1)}, bf16[64,512]{1,0:T(8,128)(2,1)S(1)}, u32[]{:S(2)}, u32[]{:S(2)}) collective-permute-start(bf16[64,512]{1,0:T(8,128)(2,1)S(1)} %get-tuple-element.39.refs_0_), channel_id=1, source_target_pairs={{0,8},{8,0},{16,24},{24,16},{1,9},{9,1},{17,25},{25,17},{2,10},{10... | collective-permute-start | bytes 196616 | tf_op jit(solution)/shard_map/ppermute | solution.py:421
  23.9 2.4 %collective-permute-start.13 = (bf16[64,512]{1,0:T(8,128)(2,1)S(1)}, bf16[64,512]{1,0:T(8,128)(2,1)S(1)}, u32[]{:S(2)}, u32[]{:S(2)}) collective-permute-start(bf16[64,512]{1,0:T(8,128)(2,1)S(1)} %get-tuple-element.39.refs_0_), channel_id=1, source_target_pairs={{0,24},{8,16},{16,8},{24,0},{1,25},{9,17},{17,9},{25,1},{2,26},{10... | collective-permute-start | bytes 196616 | tf_op jit(solution)/shard_map/ppermute | solution.py:421
  26.3 2.6 %collective-permute-start.11 = (bf16[64,512]{1,0:T(8,128)(2,1)S(1)}, bf16[64,512]{1,0:T(8,128)(2,1)S(1)}, u32[]{:S(2)}, u32[]{:S(2)}) collective-permute-start(bf16[64,512]{1,0:T(8,128)(2,1)S(1)} %get-tuple-element.39.refs_0_), channel_id=1, source_target_pairs={{0,4},{4,0},{1,5},{5,1},{2,6},{6,2},{3,7},{7,3},{8,12},{12,8},{9,1... | collective-permute-start | bytes 196616 | tf_op jit(solution)/shard_map/ppermute | solution.py:431
  28.9 1.1 %shard_map.102 = (bf16[576,384]{1,0:T(8,128)(2,1)S(1)}, f32[16,128]{1,0:T(8,128)}) custom-call(f32[1,17]{1,0:T(1,128)S(1)} %bitcast.21, f32[1,17]{1,0:T(1,128)S(1)} %bitcast.23, f32[8,128]{1,0:T(8,128)S(1)} %add.7.info_ref, f32[16,128]{1,0:T(8,128)S(1)} %get-tuple-element.40.extra_ref, f32[64,128]{1,0:T(8,128)S(1)} %get-tuple-element.41.resid_ref), custom_call_target="tpu_custom_call" | custom-call | tf_op jit(solution)/shard_map/pallas_call | solution.py:423
  30.2 2.1 %collective-permute-start.14 = (bf16[64,512]{1,0:T(8,128)(2,1)S(1)}, bf16[64,512]{1,0:T(8,128)(2,1)S(1)}, u32[]{:S(2)}, u32[]{:S(2)}) collective-permute-start(bf16[64,512]{1,0:T(8,128)(2,1)S(1)} %collective-permute-done.13.refs_0_), channel_id=1, source_target_pairs={{0,4},{4,0},{1,5},{5,1},{2,6},{6,2},{3,7},{7,3},{8,12},{12,8},{9,1... | collective-permute-start | bytes 196616 | tf_op jit(solution)/shard_map/ppermute | solution.py:431
  32.3 1.3 %shard_map.103 = (f32[4,576,128]{2,1,0:T(8,128)}, f32[4,192,128]{2,1,0:T(8,128)S(1)}) custom-call(bf16[576,384]{1,0:T(8,128)(2,1)S(1)} %get-tuple-element.43.weight_ref, f32[4,576,128]{2,1,0:T(8,128)S(1)} %bitcast.15, bf16[64,512]{1,0:T(8,128)(2,1)S(1)} %get-tuple-element.39.refs_0_, bf16[64,512]{1,0:T(8,128)(2,1)S(1)} %collective-permute-done.11.refs_1_, ...), custom_call_target="tpu_custom_call" | custom-call | tf_op jit(solution)/shard_map/pallas_call | solution.py:434
  33.6 1.0 %shard_map.104 = f32[4,576,128]{2,1,0:T(8,128)} custom-call(bf16[576,384]{1,0:T(8,128)(2,1)S(1)} %get-tuple-element.43.weight_ref, f32[4,192,128]{2,1,0:T(8,128)S(1)} %get-tuple-element.45.rest_ref, f32[4,576,128]{2,1,0:T(8,128)} %get-tuple-element.46.begun_hbm, bf16[64,512]{1,0:T(8,128)(2,1)S(1)} %collective-permute-done.13.refs_0_, ...), custom_call_target="tpu_custom_call", output_to_operand_aliasing={{}: (2, {})} | custom-call | tf_op jit(solution)/shard_map/pallas_call | solution.py:445
  (35 shorter events, 1.0 us)
Async XLA Ops:
  0.6 10.6 %copy-start = (f32[4,24,24,128]{3,2,1,0:T(8,128)S(1)}, f32[4,24,24,128]{3,2,1,0:T(8,128)}, u32[]{:S(2)}) copy-start(f32[4,24,24,128]{3,2,1,0:T(8,128)} %param.8) | copy-start | bytes 3538948
  0.6 1.3 %copy-start.5 = (s32[1,1,1,16]{3,2,1,0:T(1,128)S(1)}, s32[1,1,1,16]{3,2,1,0:T(1,128)}, u32[]{:S(2)}) copy-start(s32[1,1,1,16]{3,2,1,0:T(1,128)} %param.12) | copy-start | bytes 196
  0.6 6.5 %copy-start.6 = (s32[1,1,1,16]{3,2,1,0:T(1,128)S(1)}, s32[1,1,1,16]{3,2,1,0:T(1,128)}, u32[]{:S(2)}) copy-start(s32[1,1,1,16]{3,2,1,0:T(1,128)} %param.14) | copy-start | bytes 196
  1.9 11.8 %copy-start.1 = (bf16[4,24,24,128]{3,2,1,0:T(8,128)(2,1)S(1)}, bf16[4,24,24,128]{3,2,1,0:T(8,128)(2,1)}, u32[]{:S(2)}) copy-start(bf16[4,24,24,128]{3,2,1,0:T(8,128)(2,1)} %param.9) | copy-start | bytes 1769476
  2.0 14.9 %copy-start.3 = (f32[17]{0:T(128)S(1)}, f32[17]{0:T(128)}, u32[]{:S(2)}) copy-start(f32[17]{0:T(128)} %param.10) | copy-start | bytes 208
  2.0 14.9 %copy-start.4 = (f32[17]{0:T(128)S(1)}, f32[17]{0:T(128)}, u32[]{:S(2)}) copy-start(f32[17]{0:T(128)} %param.11) | copy-start | bytes 208
  2.1 12.0 %collective-permute-start = (bf16[784,128]{1,0:T(8,128)(2,1)S(1)}, bf16[784,128]{1,0:T(8,128)(2,1)S(1)}, u32[]{:S(2)}, u32[]{:S(2)}) collective-permute-start(bf16[784,128]{1,0:T(8,128)(2,1)S(1)} %get-tuple-element.25), channel_id=1, source_target_pairs={{0,8},{8,0},{16,24},{24,16},{1,9},{9,1},{17,25},{25,17},{2,10},{10... | collective-permute-start | bytes 602120 | tf_op jit(solution)/shard_map/ppermute | solution.py:373
  4.3 11.8 %collective-permute-start.4 = (bf16[784,128]{1,0:T(8,128)(2,1)S(1)}, bf16[784,128]{1,0:T(8,128)(2,1)S(1)}, u32[]{:S(2)}, u32[]{:S(2)}) collective-permute-start(bf16[784,128]{1,0:T(8,128)(2,1)S(1)} %get-tuple-element.37), channel_id=1, source_target_pairs={{0,24},{8,16},{16,8},{24,0},{1,25},{9,17},{17,9},{25,1},{2,26},{10... | collective-permute-start | bytes 602120 | tf_op jit(solution)/shard_map/ppermute | solution.py:373
  7.1 2.7 %collective-permute-start.1 = (f32[8,128]{1,0:T(8,128)S(1)}, f32[8,128]{1,0:T(8,128)S(1)}, u32[]{:S(2)}, u32[]{:S(2)}) collective-permute-start(f32[8,128]{1,0:T(8,128)S(1)} %get-tuple-element.27.info_ref), channel_id=1, source_target_pairs={{0,1},{1,0},{2,3},{3,2},{4,5},{5,4},{6,7},{7,6},{8,9},{9,8},{10,11... | collective-permute-start | bytes 12296 | tf_op jit(solution)/shard_map/ppermute | solution.py:381
  9.9 3.9 %collective-permute-start.2 = (f32[8,128]{1,0:T(8,128)S(1)}, f32[8,128]{1,0:T(8,128)S(1)}, u32[]{:S(2)}, u32[]{:S(2)}) collective-permute-start(f32[8,128]{1,0:T(8,128)S(1)} %add.6), channel_id=1, source_target_pairs={{0,2},{1,3},{2,0},{3,1},{4,6},{5,7},{6,4},{7,5},{8,10},{9,11},{10,... | collective-permute-start | bytes 12296 | tf_op jit(solution)/shard_map/ppermute | solution.py:381
  11.2 6.3 %copy-start.2 = (f32[1,1,1,16,128]{4,3,2,1,0:T(8,128)S(1)}, f32[1,1,1,16,128]{4,3,2,1,0:T(8,128)}, u32[]{:S(2)}) copy-start(f32[1,1,1,16,128]{4,3,2,1,0:T(8,128)} %param.15) | copy-start | bytes 24580
  11.3 5.5 %collective-permute-start.3 = (bf16[784,128]{1,0:T(8,128)(2,1)S(1)}, bf16[784,128]{1,0:T(8,128)(2,1)S(1)}, u32[]{:S(2)}, u32[]{:S(2)}) collective-permute-start(bf16[784,128]{1,0:T(8,128)(2,1)S(1)} %get-tuple-element.30), channel_id=1, source_target_pairs={{0,4},{4,0},{1,5},{5,1},{2,6},{6,2},{3,7},{7,3},{8,12},{12,8},{9,1... | collective-permute-start | bytes 602120 | tf_op jit(solution)/shard_map/ppermute | solution.py:374
  14.1 3.4 %collective-permute-start.5 = (bf16[784,128]{1,0:T(8,128)(2,1)S(1)}, bf16[784,128]{1,0:T(8,128)(2,1)S(1)}, u32[]{:S(2)}, u32[]{:S(2)}) collective-permute-start(bf16[784,128]{1,0:T(8,128)(2,1)S(1)} %collective-permute-done.refs_4_), channel_id=1, source_target_pairs={{0,4},{4,0},{1,5},{5,1},{2,6},{6,2},{3,7},{7,3},{8,12},{12,8},{9,1... | collective-permute-start | bytes 602120 | tf_op jit(solution)/shard_map/ppermute | solution.py:399
  16.1 1.8 %collective-permute-start.6 = (bf16[784,128]{1,0:T(8,128)(2,1)S(1)}, bf16[784,128]{1,0:T(8,128)(2,1)S(1)}, u32[]{:S(2)}, u32[]{:S(2)}) collective-permute-start(bf16[784,128]{1,0:T(8,128)(2,1)S(1)} %collective-permute-done.4.refs_5_), channel_id=1, source_target_pairs={{0,4},{4,0},{1,5},{5,1},{2,6},{6,2},{3,7},{7,3},{8,12},{12,8},{9,1... | collective-permute-start | bytes 602120 | tf_op jit(solution)/shard_map/ppermute | solution.py:399
  18.1 3.8 %collective-permute-start.9 = (f32[80,128]{1,0:T(8,128)S(1)}, f32[80,128]{1,0:T(8,128)S(1)}, u32[]{:S(2)}, u32[]{:S(2)}) collective-permute-start(f32[80,128]{1,0:T(8,128)S(1)} %shard_map.100.refs_0_), channel_id=1, source_target_pairs={{0,3},{1,2},{2,1},{3,0},{4,7},{5,6},{6,5},{7,4},{8,11},{9,10},{10,... | collective-permute-start | bytes 122888 | tf_op jit(solution)/shard_map/ppermute | solution.py:30
  20.3 2.9 %collective-permute-start.8 = (f32[80,128]{1,0:T(8,128)S(1)}, f32[80,128]{1,0:T(8,128)S(1)}, u32[]{:S(2)}, u32[]{:S(2)}) collective-permute-start(f32[80,128]{1,0:T(8,128)S(1)} %shard_map.100.refs_0_), channel_id=1, source_target_pairs={{0,2},{1,3},{2,0},{3,1},{4,6},{5,7},{6,4},{7,5},{8,10},{9,11},{10,... | collective-permute-start | bytes 122888 | tf_op jit(solution)/shard_map/ppermute | solution.py:30
  20.6 2.9 %collective-permute-start.7 = (f32[80,128]{1,0:T(8,128)S(1)}, f32[80,128]{1,0:T(8,128)S(1)}, u32[]{:S(2)}, u32[]{:S(2)}) collective-permute-start(f32[80,128]{1,0:T(8,128)S(1)} %shard_map.100.refs_0_), channel_id=1, source_target_pairs={{0,1},{1,0},{2,3},{3,2},{4,5},{5,4},{6,7},{7,6},{8,9},{9,8},{10,11... | collective-permute-start | bytes 122888 | tf_op jit(solution)/shard_map/ppermute | solution.py:30
  23.5 6.5 %collective-permute-start.10 = (bf16[64,512]{1,0:T(8,128)(2,1)S(1)}, bf16[64,512]{1,0:T(8,128)(2,1)S(1)}, u32[]{:S(2)}, u32[]{:S(2)}) collective-permute-start(bf16[64,512]{1,0:T(8,128)(2,1)S(1)} %get-tuple-element.39.refs_0_), channel_id=1, source_target_pairs={{0,8},{8,0},{16,24},{24,16},{1,9},{9,1},{17,25},{25,17},{2,10},{10... | collective-permute-start | bytes 196616 | tf_op jit(solution)/shard_map/ppermute | solution.py:421
  23.9 6.3 %collective-permute-start.13 = (bf16[64,512]{1,0:T(8,128)(2,1)S(1)}, bf16[64,512]{1,0:T(8,128)(2,1)S(1)}, u32[]{:S(2)}, u32[]{:S(2)}) collective-permute-start(bf16[64,512]{1,0:T(8,128)(2,1)S(1)} %get-tuple-element.39.refs_0_), channel_id=1, source_target_pairs={{0,24},{8,16},{16,8},{24,0},{1,25},{9,17},{17,9},{25,1},{2,26},{10... | collective-permute-start | bytes 196616 | tf_op jit(solution)/shard_map/ppermute | solution.py:421
  26.3 6.1 %collective-permute-start.11 = (bf16[64,512]{1,0:T(8,128)(2,1)S(1)}, bf16[64,512]{1,0:T(8,128)(2,1)S(1)}, u32[]{:S(2)}, u32[]{:S(2)}) collective-permute-start(bf16[64,512]{1,0:T(8,128)(2,1)S(1)} %get-tuple-element.39.refs_0_), channel_id=1, source_target_pairs={{0,4},{4,0},{1,5},{5,1},{2,6},{6,2},{3,7},{7,3},{8,12},{12,8},{9,1... | collective-permute-start | bytes 196616 | tf_op jit(solution)/shard_map/ppermute | solution.py:431
  30.0 2.3 %collective-permute-start.12 = (bf16[64,512]{1,0:T(8,128)(2,1)S(1)}, bf16[64,512]{1,0:T(8,128)(2,1)S(1)}, u32[]{:S(2)}, u32[]{:S(2)}) collective-permute-start(bf16[64,512]{1,0:T(8,128)(2,1)S(1)} %collective-permute-done.10.refs_2_), channel_id=1, source_target_pairs={{0,4},{4,0},{1,5},{5,1},{2,6},{6,2},{3,7},{7,3},{8,12},{12,8},{9,1... | collective-permute-start | bytes 196616 | tf_op jit(solution)/shard_map/ppermute | solution.py:431
  30.2 3.4 %collective-permute-start.14 = (bf16[64,512]{1,0:T(8,128)(2,1)S(1)}, bf16[64,512]{1,0:T(8,128)(2,1)S(1)}, u32[]{:S(2)}, u32[]{:S(2)}) collective-permute-start(bf16[64,512]{1,0:T(8,128)(2,1)S(1)} %collective-permute-done.13.refs_0_), channel_id=1, source_target_pairs={{0,4},{4,0},{1,5},{5,1},{2,6},{6,2},{3,7},{7,3},{8,12},{12,8},{9,1... | collective-permute-start | bytes 196616 | tf_op jit(solution)/shard_map/ppermute | solution.py:431

commit v7 on v6

--- a/solution.py
+++ b/solution.py
@@ -25,15 +25,16 @@
     return [even, odd] if odd else [even]
 
 
-def sum_terms(x, count):
+def sum_terms(x, sent, count):
     if count <= 4:
-        return [x] + [lax.ppermute(x, "mem", [(i, i ^ b) for i in range(count)]) for b in range(1, count)]
+        return [x] + [lax.ppermute(sent, "mem", [(i, i ^ b) for i in range(count)]) for b in range(1, count)]
     step = 1
     while step < count:
-        other = lax.ppermute(x, "mem", [(i, i ^ step) for i in range(count)])
+        other = lax.ppermute(sent, "mem", [(i, i ^ step) for i in range(count)])
         step *= 2
         if step < count:
-            x = x + other
+            x = x + other.astype(f32)
+            sent = x.astype(bf16)
     return [x, other]
 
 
@@ -227,7 +228,7 @@
     out_ref[mine, :] = out_ref[mine, :] - values_ref[...]
 
 
-def last_kernel(blocks, count, part_ref, own_ref, weight_ref, halo_ref, out_ref):
+def last_kernel(blocks, count, part_ref, own_ref, weight_ref, halo_ref, out_ref, sent_ref):
     slots, block = weight_ref.shape
     levels = part_ref.shape[1]
     members = own_ref.shape[1] // levels
@@ -239,6 +240,7 @@
     out_ref[slots:, :] = part_ref[slots:, :]
     at = slots + 2 * blocks * (3 * count - 2)
     out_ref[at:at + 2 * blocks, :] = halo_ref[members * block:, :].astype(f32)[0:2 * blocks]
+    sent_ref[...] = out_ref[...].astype(bf16)
 
 
 def resid_kernel(blocks, tiles, own_ref, *refs):
@@ -247,7 +249,7 @@
     levels = resid_ref.shape[1]
     total = terms[0][...]
     for t in terms[1:]:
-        total = total + t[...]
+        total = total + t[...].astype(f32)
     extra_ref[...] = total[slots:]
     resid = to_rows(lane_row(extra_ref, 2 * blocks * (3 * tiles - 1), blocks, slots)) * total[0:slots]
     for m in range(wide // levels):
@@ -398,19 +400,19 @@
     for p in lat_pairs:
         rims += [lax.ppermute(h, "lat", p) for h in halos]
 
-    tall = slots + up8(2 * blocks * (3 * n_tiles - 1) + blocks)
+    tall = slots + (2 * blocks * (3 * n_tiles - 1) + blocks + 15) // 16 * 16
     tails = [t[members * flank:] for t in sides]
     part = pl.pallas_call(
         functools.partial(part_kernel, blocks),
         out_shape=shape((tall, levels), f32),
         in_specs=[vmem] * (2 + len(tails) + 2 * len(rims)), out_specs=vmem, compiler_params=params(),
     )(base, own, obs_values.reshape(n_slots, levels), scale, *tails, *weights[:-1], *rims[:-1])
-    mine = pl.pallas_call(
+    mine, sent = pl.pallas_call(
         functools.partial(last_kernel, blocks, n_tiles),
-        out_shape=shape((tall, levels), f32),
-        in_specs=[vmem] * 4, out_specs=vmem, compiler_params=params(),
+        out_shape=[shape((tall, levels), f32), shape((tall, levels), bf16)],
+        in_specs=[vmem] * 4, out_specs=[vmem] * 2, compiler_params=params(),
     )(part, own, weights[-1], rims[-1])
-    terms = sum_terms(mine, n_mem)
+    terms = sum_terms(mine, sent, n_mem)
 
     resid, send, extra = pl.pallas_call(
         functools.partial(resid_kernel, blocks, n_tiles),

time: 34.8 us -> 34.5 us (level)
  no operation moved by 1% of the time
where the time goes in v7:
time: 34.5 us; the launch traced here: 34.4 us
  starting transfers between devices  22.6 us (66%)
  Pallas kernels  5.16 us (15%)
  waiting for transfers between devices  3.84 us (11%)
  between operations  1.46 us (4%)
  local copies, waits for them, and re-layouts  1.3 us (4%)
    ppermute x3, starting transfers between devices, shards(): around += [r] + [lax.ppermute(r, 'lat', q) for q in lat_pairs]  4.95 us
    ppermute x2, starting transfers between devices, shards(): halos = [lax.ppermute(r, 'lon', p) for r, p in zip((rim1, rim2), lon_pairs)]  4.39 us
    ppermute x2, starting transfers between devices, shards(): row = [send] + [lax.ppermute(send, 'lon', p) for p in lon_pairs]  2.75 us
    ppermute x2, starting transfers between devices, shards(): rims += [lax.ppermute(h, 'lat', p) for h in halos]  2.74 us
    ppermute x3, starting transfers between devices, sum_terms(): lax.ppermute(sent, 'mem', [(i, i ^ b) for i in range(count)])  2.71 us
    ppermute x2, starting transfers between devices, shards(): lax.ppermute(info, 'mem', [(i, i ^ step) for i in range(n_mem)])  2.63 us
    ppermute x1, starting transfers between devices, shards(): sides = [lax.ppermute(r, 'lat', p) for r, p in zip(sides, lat_pairs)]  2.44 us
    ppermute x3, waiting for transfers between devices, sum_terms(): lax.ppermute(sent, 'mem', [(i, i ^ b) for i in range(count)])  2.38 us
  transfers between devices with their start and end apart: 15, of which 4 were waited for; matrix products, arithmetic and copies ran while one was open for 0% of the time, Pallas kernels for 11%

profile of v7, /device:TPU:1, one launch (start us, length us, event | category | flops | bytes accessed | tf_op | source)
XLA Modules:
  0.0 34.4 jit_solution(1730253742941821286)
XLA Ops:
  0.7 1.3 %fusion = (f32[4,8,24,128]{3,2,1,0:T(8,128)S(1)}, f32[4,8,24,128]{3,2,1,0:T(8,128)S(1)}) fusion(f32[4,24,24,128]{3,2,1,0:T(8,128)} %param.8), kind=kLoop, calls=%fused_computation.1 | loop fusion | bytes 1572864 | tf_op jit(solution)/shard_map/slice | solution.py:364
  2.1 2.2 %collective-permute-start = (bf16[784,128]{1,0:T(8,128)(2,1)S(1)}, bf16[784,128]{1,0:T(8,128)(2,1)S(1)}, u32[]{:S(2)}, u32[]{:S(2)}) collective-permute-start(bf16[784,128]{1,0:T(8,128)(2,1)S(1)} %get-tuple-element.27), channel_id=1, source_target_pairs={{0,8},{8,0},{16,24},{24,16},{1,9},{9,1},{17,25},{25,17},{2,10},{10... | collective-permute-start | bytes 602120 | tf_op jit(solution)/shard_map/ppermute | solution.py:375
  4.3 2.2 %collective-permute-start.4 = (bf16[784,128]{1,0:T(8,128)(2,1)S(1)}, bf16[784,128]{1,0:T(8,128)(2,1)S(1)}, u32[]{:S(2)}, u32[]{:S(2)}) collective-permute-start(bf16[784,128]{1,0:T(8,128)(2,1)S(1)} %get-tuple-element.39), channel_id=1, source_target_pairs={{0,24},{8,16},{16,8},{24,0},{1,25},{9,17},{17,9},{25,1},{2,26},{10... | collective-permute-start | bytes 602120 | tf_op jit(solution)/shard_map/ppermute | solution.py:375
  7.1 1.3 %collective-permute-start.1 = (f32[8,128]{1,0:T(8,128)S(1)}, f32[8,128]{1,0:T(8,128)S(1)}, u32[]{:S(2)}, u32[]{:S(2)}) collective-permute-start(f32[8,128]{1,0:T(8,128)S(1)} %get-tuple-element.29.info_ref), channel_id=1, source_target_pairs={{0,1},{1,0},{2,3},{3,2},{4,5},{5,4},{6,7},{7,6},{8,9},{9,8},{10,11... | collective-permute-start | bytes 12296 | tf_op jit(solution)/shard_map/ppermute | solution.py:383
  8.4 1.4 %collective-permute-done.1 = f32[8,128]{1,0:T(8,128)S(1)} collective-permute-done((f32[8,128]{1,0:T(8,128)S(1)}, f32[8,128]{1,0:T(8,128)S(1)}, u32[]{:S(2)}, u32[]{:S(2)}) %collective-permute-start.1) | collective-permute-done | bytes 4128 | tf_op jit(solution)/shard_map/ppermute | solution.py:383
  9.9 1.3 %collective-permute-start.2 = (f32[8,128]{1,0:T(8,128)S(1)}, f32[8,128]{1,0:T(8,128)S(1)}, u32[]{:S(2)}, u32[]{:S(2)}) collective-permute-start(f32[8,128]{1,0:T(8,128)S(1)} %add.6), channel_id=1, source_target_pairs={{0,2},{1,3},{2,0},{3,1},{4,6},{5,7},{6,4},{7,5},{8,10},{9,11},{10,... | collective-permute-start | bytes 12296 | tf_op jit(solution)/shard_map/ppermute | solution.py:383
  11.3 2.4 %collective-permute-start.3 = (bf16[784,128]{1,0:T(8,128)(2,1)S(1)}, bf16[784,128]{1,0:T(8,128)(2,1)S(1)}, u32[]{:S(2)}, u32[]{:S(2)}) collective-permute-start(bf16[784,128]{1,0:T(8,128)(2,1)S(1)} %get-tuple-element.32), channel_id=1, source_target_pairs={{0,4},{4,0},{1,5},{5,1},{2,6},{6,2},{3,7},{7,3},{8,12},{12,8},{9,1... | collective-permute-start | bytes 602120 | tf_op jit(solution)/shard_map/ppermute | solution.py:376
  13.7 0.3 shard_map.96.own_ref
  14.1 2.0 %collective-permute-start.5 = (bf16[784,128]{1,0:T(8,128)(2,1)S(1)}, bf16[784,128]{1,0:T(8,128)(2,1)S(1)}, u32[]{:S(2)}, u32[]{:S(2)}) collective-permute-start(bf16[784,128]{1,0:T(8,128)(2,1)S(1)} %collective-permute-done.refs_4_), channel_id=1, source_target_pairs={{0,4},{4,0},{1,5},{5,1},{2,6},{6,2},{3,7},{7,3},{8,12},{12,8},{9,1... | collective-permute-start | bytes 602120 | tf_op jit(solution)/shard_map/ppermute | solution.py:401
  16.1 0.7 %collective-permute-start.6 = (bf16[784,128]{1,0:T(8,128)(2,1)S(1)}, bf16[784,128]{1,0:T(8,128)(2,1)S(1)}, u32[]{:S(2)}, u32[]{:S(2)}) collective-permute-start(bf16[784,128]{1,0:T(8,128)(2,1)S(1)} %collective-permute-done.4.refs_5_), channel_id=1, source_target_pairs={{0,4},{4,0},{1,5},{5,1},{2,6},{6,2},{3,7},{7,3},{8,12},{12,8},{9,1... | collective-permute-start | bytes 602120 | tf_op jit(solution)/shard_map/ppermute | solution.py:401
  16.8 0.7 %shard_map.98 = (f32[64,512]{1,0:T(8,128)S(1)}, bf16[64,192]{1,0:T(8,128)(2,1)S(1)}, bf16[64,192]{1,0:T(8,128)(2,1)S(1)}, bf16[64,192]{1,0:T(8,128)(2,1)S(1)}, bf16[64,192]{1,0:T(8,128)(2,1)S(1)}) custom-call(f32[1,17]{1,0:T(1,128)S(1)} %bitcast.20, f32[1,17]{1,0:T(1,128)S(1)} %bitcast.22, f32[8,128]{1,0:T(8,128)S(1)} %add.7.info_ref, ...), custom_call_target="tpu_custom_call" | custom-call | tf_op jit(solution)/shard_map/pallas_call | solution.py:392
  17.5 0.3 shard_map.99.part_ref
  18.1 2.2 %collective-permute-start.9 = (bf16[80,128]{1,0:T(8,128)(2,1)S(1)}, bf16[80,128]{1,0:T(8,128)(2,1)S(1)}, u32[]{:S(2)}, u32[]{:S(2)}) collective-permute-start(bf16[80,128]{1,0:T(8,128)(2,1)S(1)} %get-tuple-element.42), channel_id=1, source_target_pairs={{0,3},{1,2},{2,1},{3,0},{4,7},{5,6},{6,5},{7,4},{8,11},{9,10},{10,... | collective-permute-start | bytes 61448 | tf_op jit(solution)/shard_map/ppermute | solution.py:30
  20.3 0.2 collective-permute-start.8
  20.6 0.3 collective-permute-start.7
  20.8 0.9 %collective-permute-done.9.refs_3_ = bf16[80,128]{1,0:T(8,128)(2,1)S(1)} collective-permute-done((bf16[80,128]{1,0:T(8,128)(2,1)S(1)}, bf16[80,128]{1,0:T(8,128)(2,1)S(1)}, u32[]{:S(2)}, u32[]{:S(2)}) %collective-permute-start.9) | collective-permute-done | bytes 20512 | tf_op jit(solution)/shard_map/ppermute | solution.py:30
  21.7 1.3 %collective-permute-done.8.refs_2_ = bf16[80,128]{1,0:T(8,128)(2,1)S(1)} collective-permute-done((bf16[80,128]{1,0:T(8,128)(2,1)S(1)}, bf16[80,128]{1,0:T(8,128)(2,1)S(1)}, u32[]{:S(2)}, u32[]{:S(2)}) %collective-permute-start.8) | collective-permute-done | bytes 20512 | tf_op jit(solution)/shard_map/ppermute | solution.py:30
  23.3 0.4 %collective-permute-start.10 = (bf16[64,512]{1,0:T(8,128)(2,1)S(1)}, bf16[64,512]{1,0:T(8,128)(2,1)S(1)}, u32[]{:S(2)}, u32[]{:S(2)}) collective-permute-start(bf16[64,512]{1,0:T(8,128)(2,1)S(1)} %get-tuple-element.43.refs_0_), channel_id=1, source_target_pairs={{0,8},{8,0},{16,24},{24,16},{1,9},{9,1},{17,25},{25,17},{2,10},{10... | collective-permute-start | bytes 196616 | tf_op jit(solution)/shard_map/ppermute | solution.py:423
  23.7 2.4 %collective-permute-start.13 = (bf16[64,512]{1,0:T(8,128)(2,1)S(1)}, bf16[64,512]{1,0:T(8,128)(2,1)S(1)}, u32[]{:S(2)}, u32[]{:S(2)}) collective-permute-start(bf16[64,512]{1,0:T(8,128)(2,1)S(1)} %get-tuple-element.43.refs_0_), channel_id=1, source_target_pairs={{0,24},{8,16},{16,8},{24,0},{1,25},{9,17},{17,9},{25,1},{2,26},{10... | collective-permute-start | bytes 196616 | tf_op jit(solution)/shard_map/ppermute | solution.py:423
  26.1 2.6 %collective-permute-start.11 = (bf16[64,512]{1,0:T(8,128)(2,1)S(1)}, bf16[64,512]{1,0:T(8,128)(2,1)S(1)}, u32[]{:S(2)}, u32[]{:S(2)}) collective-permute-start(bf16[64,512]{1,0:T(8,128)(2,1)S(1)} %get-tuple-element.43.refs_0_), channel_id=1, source_target_pairs={{0,4},{4,0},{1,5},{5,1},{2,6},{6,2},{3,7},{7,3},{8,12},{12,8},{9,1... | collective-permute-start | bytes 196616 | tf_op jit(solution)/shard_map/ppermute | solution.py:433
  28.7 1.1 %shard_map.102 = (bf16[576,384]{1,0:T(8,128)(2,1)S(1)}, f32[16,128]{1,0:T(8,128)}) custom-call(f32[1,17]{1,0:T(1,128)S(1)} %bitcast.21, f32[1,17]{1,0:T(1,128)S(1)} %bitcast.23, f32[8,128]{1,0:T(8,128)S(1)} %add.7.info_ref, f32[16,128]{1,0:T(8,128)S(1)} %get-tuple-element.44.extra_ref, f32[64,128]{1,0:T(8,128)S(1)} %get-tuple-element.45.resid_ref), custom_call_target="tpu_custom_call" | custom-call | tf_op jit(solution)/shard_map/pallas_call | solution.py:425
  30.0 2.1 %collective-permute-start.14 = (bf16[64,512]{1,0:T(8,128)(2,1)S(1)}, bf16[64,512]{1,0:T(8,128)(2,1)S(1)}, u32[]{:S(2)}, u32[]{:S(2)}) collective-permute-start(bf16[64,512]{1,0:T(8,128)(2,1)S(1)} %collective-permute-done.13.refs_0_), channel_id=1, source_target_pairs={{0,4},{4,0},{1,5},{5,1},{2,6},{6,2},{3,7},{7,3},{8,12},{12,8},{9,1... | collective-permute-start | bytes 196616 | tf_op jit(solution)/shard_map/ppermute | solution.py:433
  32.1 1.3 %shard_map.103 = (f32[4,576,128]{2,1,0:T(8,128)}, f32[4,192,128]{2,1,0:T(8,128)S(1)}) custom-call(bf16[576,384]{1,0:T(8,128)(2,1)S(1)} %get-tuple-element.47.weight_ref, f32[4,576,128]{2,1,0:T(8,128)S(1)} %bitcast.15, bf16[64,512]{1,0:T(8,128)(2,1)S(1)} %get-tuple-element.43.refs_0_, bf16[64,512]{1,0:T(8,128)(2,1)S(1)} %collective-permute-done.11.refs_1_, ...), custom_call_target="tpu_custom_call" | custom-call | tf_op jit(solution)/shard_map/pallas_call | solution.py:436
  33.4 1.0 %shard_map.104 = f32[4,576,128]{2,1,0:T(8,128)} custom-call(bf16[576,384]{1,0:T(8,128)(2,1)S(1)} %get-tuple-element.47.weight_ref, f32[4,192,128]{2,1,0:T(8,128)S(1)} %get-tuple-element.49.rest_ref, f32[4,576,128]{2,1,0:T(8,128)} %get-tuple-element.50.begun_hbm, bf16[64,512]{1,0:T(8,128)(2,1)S(1)} %collective-permute-done.13.refs_0_, ...), custom_call_target="tpu_custom_call", output_to_operand_aliasing={{}: (2, {})} | custom-call | tf_op jit(solution)/shard_map/pallas_call | solution.py:447
  (35 shorter events, 1.0 us)
Async XLA Ops:
  0.6 10.6 %copy-start = (f32[4,24,24,128]{3,2,1,0:T(8,128)S(1)}, f32[4,24,24,128]{3,2,1,0:T(8,128)}, u32[]{:S(2)}) copy-start(f32[4,24,24,128]{3,2,1,0:T(8,128)} %param.8) | copy-start | bytes 3538948
  0.6 1.3 %copy-start.5 = (s32[1,1,1,16]{3,2,1,0:T(1,128)S(1)}, s32[1,1,1,16]{3,2,1,0:T(1,128)}, u32[]{:S(2)}) copy-start(s32[1,1,1,16]{3,2,1,0:T(1,128)} %param.12) | copy-start | bytes 196
  0.6 6.5 %copy-start.6 = (s32[1,1,1,16]{3,2,1,0:T(1,128)S(1)}, s32[1,1,1,16]{3,2,1,0:T(1,128)}, u32[]{:S(2)}) copy-start(s32[1,1,1,16]{3,2,1,0:T(1,128)} %param.14) | copy-start | bytes 196
  1.9 11.8 %copy-start.1 = (bf16[4,24,24,128]{3,2,1,0:T(8,128)(2,1)S(1)}, bf16[4,24,24,128]{3,2,1,0:T(8,128)(2,1)}, u32[]{:S(2)}) copy-start(bf16[4,24,24,128]{3,2,1,0:T(8,128)(2,1)} %param.9) | copy-start | bytes 1769476
  2.0 14.9 %copy-start.3 = (f32[17]{0:T(128)S(1)}, f32[17]{0:T(128)}, u32[]{:S(2)}) copy-start(f32[17]{0:T(128)} %param.10) | copy-start | bytes 208
  2.0 14.9 %copy-start.4 = (f32[17]{0:T(128)S(1)}, f32[17]{0:T(128)}, u32[]{:S(2)}) copy-start(f32[17]{0:T(128)} %param.11) | copy-start | bytes 208
  2.1 12.0 %collective-permute-start = (bf16[784,128]{1,0:T(8,128)(2,1)S(1)}, bf16[784,128]{1,0:T(8,128)(2,1)S(1)}, u32[]{:S(2)}, u32[]{:S(2)}) collective-permute-start(bf16[784,128]{1,0:T(8,128)(2,1)S(1)} %get-tuple-element.27), channel_id=1, source_target_pairs={{0,8},{8,0},{16,24},{24,16},{1,9},{9,1},{17,25},{25,17},{2,10},{10... | collective-permute-start | bytes 602120 | tf_op jit(solution)/shard_map/ppermute | solution.py:375
  4.3 11.8 %collective-permute-start.4 = (bf16[784,128]{1,0:T(8,128)(2,1)S(1)}, bf16[784,128]{1,0:T(8,128)(2,1)S(1)}, u32[]{:S(2)}, u32[]{:S(2)}) collective-permute-start(bf16[784,128]{1,0:T(8,128)(2,1)S(1)} %get-tuple-element.39), channel_id=1, source_target_pairs={{0,24},{8,16},{16,8},{24,0},{1,25},{9,17},{17,9},{25,1},{2,26},{10... | collective-permute-start | bytes 602120 | tf_op jit(solution)/shard_map/ppermute | solution.py:375
  7.1 2.7 %collective-permute-start.1 = (f32[8,128]{1,0:T(8,128)S(1)}, f32[8,128]{1,0:T(8,128)S(1)}, u32[]{:S(2)}, u32[]{:S(2)}) collective-permute-start(f32[8,128]{1,0:T(8,128)S(1)} %get-tuple-element.29.info_ref), channel_id=1, source_target_pairs={{0,1},{1,0},{2,3},{3,2},{4,5},{5,4},{6,7},{7,6},{8,9},{9,8},{10,11... | collective-permute-start | bytes 12296 | tf_op jit(solution)/shard_map/ppermute | solution.py:383
  9.9 3.9 %collective-permute-start.2 = (f32[8,128]{1,0:T(8,128)S(1)}, f32[8,128]{1,0:T(8,128)S(1)}, u32[]{:S(2)}, u32[]{:S(2)}) collective-permute-start(f32[8,128]{1,0:T(8,128)S(1)} %add.6), channel_id=1, source_target_pairs={{0,2},{1,3},{2,0},{3,1},{4,6},{5,7},{6,4},{7,5},{8,10},{9,11},{10,... | collective-permute-start | bytes 12296 | tf_op jit(solution)/shard_map/ppermute | solution.py:383
  11.2 6.3 %copy-start.2 = (f32[1,1,1,16,128]{4,3,2,1,0:T(8,128)S(1)}, f32[1,1,1,16,128]{4,3,2,1,0:T(8,128)}, u32[]{:S(2)}) copy-start(f32[1,1,1,16,128]{4,3,2,1,0:T(8,128)} %param.15) | copy-start | bytes 24580
  11.3 5.5 %collective-permute-start.3 = (bf16[784,128]{1,0:T(8,128)(2,1)S(1)}, bf16[784,128]{1,0:T(8,128)(2,1)S(1)}, u32[]{:S(2)}, u32[]{:S(2)}) collective-permute-start(bf16[784,128]{1,0:T(8,128)(2,1)S(1)} %get-tuple-element.32), channel_id=1, source_target_pairs={{0,4},{4,0},{1,5},{5,1},{2,6},{6,2},{3,7},{7,3},{8,12},{12,8},{9,1... | collective-permute-start | bytes 602120 | tf_op jit(solution)/shard_map/ppermute | solution.py:376
  14.1 3.4 %collective-permute-start.5 = (bf16[784,128]{1,0:T(8,128)(2,1)S(1)}, bf16[784,128]{1,0:T(8,128)(2,1)S(1)}, u32[]{:S(2)}, u32[]{:S(2)}) collective-permute-start(bf16[784,128]{1,0:T(8,128)(2,1)S(1)} %collective-permute-done.refs_4_), channel_id=1, source_target_pairs={{0,4},{4,0},{1,5},{5,1},{2,6},{6,2},{3,7},{7,3},{8,12},{12,8},{9,1... | collective-permute-start | bytes 602120 | tf_op jit(solution)/shard_map/ppermute | solution.py:401
  16.1 1.8 %collective-permute-start.6 = (bf16[784,128]{1,0:T(8,128)(2,1)S(1)}, bf16[784,128]{1,0:T(8,128)(2,1)S(1)}, u32[]{:S(2)}, u32[]{:S(2)}) collective-permute-start(bf16[784,128]{1,0:T(8,128)(2,1)S(1)} %collective-permute-done.4.refs_5_), channel_id=1, source_target_pairs={{0,4},{4,0},{1,5},{5,1},{2,6},{6,2},{3,7},{7,3},{8,12},{12,8},{9,1... | collective-permute-start | bytes 602120 | tf_op jit(solution)/shard_map/ppermute | solution.py:401
  18.1 3.6 %collective-permute-start.9 = (bf16[80,128]{1,0:T(8,128)(2,1)S(1)}, bf16[80,128]{1,0:T(8,128)(2,1)S(1)}, u32[]{:S(2)}, u32[]{:S(2)}) collective-permute-start(bf16[80,128]{1,0:T(8,128)(2,1)S(1)} %get-tuple-element.42), channel_id=1, source_target_pairs={{0,3},{1,2},{2,1},{3,0},{4,7},{5,6},{6,5},{7,4},{8,11},{9,10},{10,... | collective-permute-start | bytes 61448 | tf_op jit(solution)/shard_map/ppermute | solution.py:30
  20.3 2.6 %collective-permute-start.8 = (bf16[80,128]{1,0:T(8,128)(2,1)S(1)}, bf16[80,128]{1,0:T(8,128)(2,1)S(1)}, u32[]{:S(2)}, u32[]{:S(2)}) collective-permute-start(bf16[80,128]{1,0:T(8,128)(2,1)S(1)} %get-tuple-element.42), channel_id=1, source_target_pairs={{0,2},{1,3},{2,0},{3,1},{4,6},{5,7},{6,4},{7,5},{8,10},{9,11},{10,... | collective-permute-start | bytes 61448 | tf_op jit(solution)/shard_map/ppermute | solution.py:30
  20.6 2.6 %collective-permute-start.7 = (bf16[80,128]{1,0:T(8,128)(2,1)S(1)}, bf16[80,128]{1,0:T(8,128)(2,1)S(1)}, u32[]{:S(2)}, u32[]{:S(2)}) collective-permute-start(bf16[80,128]{1,0:T(8,128)(2,1)S(1)} %get-tuple-element.42), channel_id=1, source_target_pairs={{0,1},{1,0},{2,3},{3,2},{4,5},{5,4},{6,7},{7,6},{8,9},{9,8},{10,11... | collective-permute-start | bytes 61448 | tf_op jit(solution)/shard_map/ppermute | solution.py:30
  23.3 6.5 %collective-permute-start.10 = (bf16[64,512]{1,0:T(8,128)(2,1)S(1)}, bf16[64,512]{1,0:T(8,128)(2,1)S(1)}, u32[]{:S(2)}, u32[]{:S(2)}) collective-permute-start(bf16[64,512]{1,0:T(8,128)(2,1)S(1)} %get-tuple-element.43.refs_0_), channel_id=1, source_target_pairs={{0,8},{8,0},{16,24},{24,16},{1,9},{9,1},{17,25},{25,17},{2,10},{10... | collective-permute-start | bytes 196616 | tf_op jit(solution)/shard_map/ppermute | solution.py:423
  23.7 6.3 %collective-permute-start.13 = (bf16[64,512]{1,0:T(8,128)(2,1)S(1)}, bf16[64,512]{1,0:T(8,128)(2,1)S(1)}, u32[]{:S(2)}, u32[]{:S(2)}) collective-permute-start(bf16[64,512]{1,0:T(8,128)(2,1)S(1)} %get-tuple-element.43.refs_0_), channel_id=1, source_target_pairs={{0,24},{8,16},{16,8},{24,0},{1,25},{9,17},{17,9},{25,1},{2,26},{10... | collective-permute-start | bytes 196616 | tf_op jit(solution)/shard_map/ppermute | solution.py:423
  26.1 6.1 %collective-permute-start.11 = (bf16[64,512]{1,0:T(8,128)(2,1)S(1)}, bf16[64,512]{1,0:T(8,128)(2,1)S(1)}, u32[]{:S(2)}, u32[]{:S(2)}) collective-permute-start(bf16[64,512]{1,0:T(8,128)(2,1)S(1)} %get-tuple-element.43.refs_0_), channel_id=1, source_target_pairs={{0,4},{4,0},{1,5},{5,1},{2,6},{6,2},{3,7},{7,3},{8,12},{12,8},{9,1... | collective-permute-start | bytes 196616 | tf_op jit(solution)/shard_map/ppermute | solution.py:433
  29.8 2.3 %collective-permute-start.12 = (bf16[64,512]{1,0:T(8,128)(2,1)S(1)}, bf16[64,512]{1,0:T(8,128)(2,1)S(1)}, u32[]{:S(2)}, u32[]{:S(2)}) collective-permute-start(bf16[64,512]{1,0:T(8,128)(2,1)S(1)} %collective-permute-done.10.refs_2_), channel_id=1, source_target_pairs={{0,4},{4,0},{1,5},{5,1},{2,6},{6,2},{3,7},{7,3},{8,12},{12,8},{9,1... | collective-permute-start | bytes 196616 | tf_op jit(solution)/shard_map/ppermute | solution.py:433
  30.0 3.4 %collective-permute-start.14 = (bf16[64,512]{1,0:T(8,128)(2,1)S(1)}, bf16[64,512]{1,0:T(8,128)(2,1)S(1)}, u32[]{:S(2)}, u32[]{:S(2)}) collective-permute-start(bf16[64,512]{1,0:T(8,128)(2,1)S(1)} %collective-permute-done.13.refs_0_), channel_id=1, source_target_pairs={{0,4},{4,0},{1,5},{5,1},{2,6},{6,2},{3,7},{7,3},{8,12},{12,8},{9,1... | collective-permute-start | bytes 196616 | tf_op jit(solution)/shard_map/ppermute | solution.py:433

commit v8 on v6

--- a/solution.py
+++ b/solution.py
@@ -429,7 +429,7 @@
     around = []
     for r in row:
         around += [r] + [lax.ppermute(r, "lat", q) for q in lat_pairs]
-    group = 2 if members % 2 == 0 else 1
+    group = members
     late = n_tiles
     begun, rest = pl.pallas_call(
         functools.partial(begin_kernel, group, edge),

time: 34.8 us -> 34.8 us (level)
  no operation moved by 1% of the time
where the time goes in v8:
time: 34.8 us; the launch traced here: 34.6 us
  starting transfers between devices  22.6 us (65%)
  Pallas kernels  5.15 us (15%)
  waiting for transfers between devices  4.06 us (12%)
  between operations  1.47 us (4%)
  local copies, waits for them, and re-layouts  1.3 us (4%)
    ppermute x3, starting transfers between devices, shards(): around += [r] + [lax.ppermute(r, 'lat', q) for q in lat_pairs]  4.95 us
    ppermute x2, starting transfers between devices, shards(): halos = [lax.ppermute(r, 'lon', p) for r, p in zip((rim1, rim2), lon_pairs)]  4.39 us
    ppermute x2, starting transfers between devices, shards(): row = [send] + [lax.ppermute(send, 'lon', p) for p in lon_pairs]  2.75 us
    ppermute x2, starting transfers between devices, shards(): rims += [lax.ppermute(h, 'lat', p) for h in halos]  2.74 us
    ppermute x3, starting transfers between devices, sum_terms(): lax.ppermute(x, 'mem', [(i, i ^ b) for i in range(count)])  2.71 us
    ppermute x2, starting transfers between devices, shards(): lax.ppermute(info, 'mem', [(i, i ^ step) for i in range(n_mem)])  2.63 us
    ppermute x3, waiting for transfers between devices, sum_terms(): lax.ppermute(x, 'mem', [(i, i ^ b) for i in range(count)])  2.6 us
    ppermute x1, starting transfers between devices, shards(): sides = [lax.ppermute(r, 'lat', p) for r, p in zip(sides, lat_pairs)]  2.44 us
  transfers between devices with their start and end apart: 15, of which 4 were waited for; matrix products, arithmetic and copies ran while one was open for 0% of the time, Pallas kernels for 11%

profile of v8, /device:TPU:1, one launch (start us, length us, event | category | flops | bytes accessed | tf_op | source)
XLA Modules:
  0.0 34.6 jit_solution(4568419106843255201)
XLA Ops:
  0.7 1.3 %fusion = (f32[4,8,24,128]{3,2,1,0:T(8,128)S(1)}, f32[4,8,24,128]{3,2,1,0:T(8,128)S(1)}) fusion(f32[4,24,24,128]{3,2,1,0:T(8,128)} %param.8), kind=kLoop, calls=%fused_computation.1 | loop fusion | bytes 1572864 | tf_op jit(solution)/shard_map/slice | solution.py:362
  2.1 2.2 %collective-permute-start = (bf16[784,128]{1,0:T(8,128)(2,1)S(1)}, bf16[784,128]{1,0:T(8,128)(2,1)S(1)}, u32[]{:S(2)}, u32[]{:S(2)}) collective-permute-start(bf16[784,128]{1,0:T(8,128)(2,1)S(1)} %get-tuple-element.25), channel_id=1, source_target_pairs={{0,8},{8,0},{16,24},{24,16},{1,9},{9,1},{17,25},{25,17},{2,10},{10... | collective-permute-start | bytes 602120 | tf_op jit(solution)/shard_map/ppermute | solution.py:373
  4.3 2.2 %collective-permute-start.4 = (bf16[784,128]{1,0:T(8,128)(2,1)S(1)}, bf16[784,128]{1,0:T(8,128)(2,1)S(1)}, u32[]{:S(2)}, u32[]{:S(2)}) collective-permute-start(bf16[784,128]{1,0:T(8,128)(2,1)S(1)} %get-tuple-element.37), channel_id=1, source_target_pairs={{0,24},{8,16},{16,8},{24,0},{1,25},{9,17},{17,9},{25,1},{2,26},{10... | collective-permute-start | bytes 602120 | tf_op jit(solution)/shard_map/ppermute | solution.py:373
  7.1 1.3 %collective-permute-start.1 = (f32[8,128]{1,0:T(8,128)S(1)}, f32[8,128]{1,0:T(8,128)S(1)}, u32[]{:S(2)}, u32[]{:S(2)}) collective-permute-start(f32[8,128]{1,0:T(8,128)S(1)} %get-tuple-element.27.info_ref), channel_id=1, source_target_pairs={{0,1},{1,0},{2,3},{3,2},{4,5},{5,4},{6,7},{7,6},{8,9},{9,8},{10,11... | collective-permute-start | bytes 12296 | tf_op jit(solution)/shard_map/ppermute | solution.py:381
  8.4 1.4 %collective-permute-done.1 = f32[8,128]{1,0:T(8,128)S(1)} collective-permute-done((f32[8,128]{1,0:T(8,128)S(1)}, f32[8,128]{1,0:T(8,128)S(1)}, u32[]{:S(2)}, u32[]{:S(2)}) %collective-permute-start.1) | collective-permute-done | bytes 4128 | tf_op jit(solution)/shard_map/ppermute | solution.py:381
  9.9 1.3 %collective-permute-start.2 = (f32[8,128]{1,0:T(8,128)S(1)}, f32[8,128]{1,0:T(8,128)S(1)}, u32[]{:S(2)}, u32[]{:S(2)}) collective-permute-start(f32[8,128]{1,0:T(8,128)S(1)} %add.6), channel_id=1, source_target_pairs={{0,2},{1,3},{2,0},{3,1},{4,6},{5,7},{6,4},{7,5},{8,10},{9,11},{10,... | collective-permute-start | bytes 12296 | tf_op jit(solution)/shard_map/ppermute | solution.py:381
  11.3 2.4 %collective-permute-start.3 = (bf16[784,128]{1,0:T(8,128)(2,1)S(1)}, bf16[784,128]{1,0:T(8,128)(2,1)S(1)}, u32[]{:S(2)}, u32[]{:S(2)}) collective-permute-start(bf16[784,128]{1,0:T(8,128)(2,1)S(1)} %get-tuple-element.30), channel_id=1, source_target_pairs={{0,4},{4,0},{1,5},{5,1},{2,6},{6,2},{3,7},{7,3},{8,12},{12,8},{9,1... | collective-permute-start | bytes 602120 | tf_op jit(solution)/shard_map/ppermute | solution.py:374
  13.7 0.3 shard_map.96.own_ref
  14.1 2.0 %collective-permute-start.5 = (bf16[784,128]{1,0:T(8,128)(2,1)S(1)}, bf16[784,128]{1,0:T(8,128)(2,1)S(1)}, u32[]{:S(2)}, u32[]{:S(2)}) collective-permute-start(bf16[784,128]{1,0:T(8,128)(2,1)S(1)} %collective-permute-done.refs_4_), channel_id=1, source_target_pairs={{0,4},{4,0},{1,5},{5,1},{2,6},{6,2},{3,7},{7,3},{8,12},{12,8},{9,1... | collective-permute-start | bytes 602120 | tf_op jit(solution)/shard_map/ppermute | solution.py:399
  16.1 0.7 %collective-permute-start.6 = (bf16[784,128]{1,0:T(8,128)(2,1)S(1)}, bf16[784,128]{1,0:T(8,128)(2,1)S(1)}, u32[]{:S(2)}, u32[]{:S(2)}) collective-permute-start(bf16[784,128]{1,0:T(8,128)(2,1)S(1)} %collective-permute-done.4.refs_5_), channel_id=1, source_target_pairs={{0,4},{4,0},{1,5},{5,1},{2,6},{6,2},{3,7},{7,3},{8,12},{12,8},{9,1... | collective-permute-start | bytes 602120 | tf_op jit(solution)/shard_map/ppermute | solution.py:399
  16.8 0.7 %shard_map.98 = (f32[64,512]{1,0:T(8,128)S(1)}, bf16[64,192]{1,0:T(8,128)(2,1)S(1)}, bf16[64,192]{1,0:T(8,128)(2,1)S(1)}, bf16[64,192]{1,0:T(8,128)(2,1)S(1)}, bf16[64,192]{1,0:T(8,128)(2,1)S(1)}) custom-call(f32[1,17]{1,0:T(1,128)S(1)} %bitcast.20, f32[1,17]{1,0:T(1,128)S(1)} %bitcast.22, f32[8,128]{1,0:T(8,128)S(1)} %add.7.info_ref, ...), custom_call_target="tpu_custom_call" | custom-call | tf_op jit(solution)/shard_map/pallas_call | solution.py:390
  17.5 0.3 shard_map.99.part_ref
  18.1 2.2 %collective-permute-start.9 = (f32[80,128]{1,0:T(8,128)S(1)}, f32[80,128]{1,0:T(8,128)S(1)}, u32[]{:S(2)}, u32[]{:S(2)}) collective-permute-start(f32[80,128]{1,0:T(8,128)S(1)} %shard_map.100.refs_0_), channel_id=1, source_target_pairs={{0,3},{1,2},{2,1},{3,0},{4,7},{5,6},{6,5},{7,4},{8,11},{9,10},{10,... | collective-permute-start | bytes 122888 | tf_op jit(solution)/shard_map/ppermute | solution.py:30
  20.3 0.2 collective-permute-start.8
  20.6 0.3 collective-permute-start.7
  20.8 1.1 %collective-permute-done.9.refs_3_ = f32[80,128]{1,0:T(8,128)S(1)} collective-permute-done((f32[80,128]{1,0:T(8,128)S(1)}, f32[80,128]{1,0:T(8,128)S(1)}, u32[]{:S(2)}, u32[]{:S(2)}) %collective-permute-start.9) | collective-permute-done | bytes 40992 | tf_op jit(solution)/shard_map/ppermute | solution.py:30
  21.9 1.3 %collective-permute-done.8.refs_2_ = f32[80,128]{1,0:T(8,128)S(1)} collective-permute-done((f32[80,128]{1,0:T(8,128)S(1)}, f32[80,128]{1,0:T(8,128)S(1)}, u32[]{:S(2)}, u32[]{:S(2)}) %collective-permute-start.8) | collective-permute-done | bytes 40992 | tf_op jit(solution)/shard_map/ppermute | solution.py:30
  23.5 0.4 %collective-permute-start.10 = (bf16[64,512]{1,0:T(8,128)(2,1)S(1)}, bf16[64,512]{1,0:T(8,128)(2,1)S(1)}, u32[]{:S(2)}, u32[]{:S(2)}) collective-permute-start(bf16[64,512]{1,0:T(8,128)(2,1)S(1)} %get-tuple-element.39.refs_0_), channel_id=1, source_target_pairs={{0,8},{8,0},{16,24},{24,16},{1,9},{9,1},{17,25},{25,17},{2,10},{10... | collective-permute-start | bytes 196616 | tf_op jit(solution)/shard_map/ppermute | solution.py:421
  23.9 2.4 %collective-permute-start.13 = (bf16[64,512]{1,0:T(8,128)(2,1)S(1)}, bf16[64,512]{1,0:T(8,128)(2,1)S(1)}, u32[]{:S(2)}, u32[]{:S(2)}) collective-permute-start(bf16[64,512]{1,0:T(8,128)(2,1)S(1)} %get-tuple-element.39.refs_0_), channel_id=1, source_target_pairs={{0,24},{8,16},{16,8},{24,0},{1,25},{9,17},{17,9},{25,1},{2,26},{10... | collective-permute-start | bytes 196616 | tf_op jit(solution)/shard_map/ppermute | solution.py:421
  26.3 2.6 %collective-permute-start.11 = (bf16[64,512]{1,0:T(8,128)(2,1)S(1)}, bf16[64,512]{1,0:T(8,128)(2,1)S(1)}, u32[]{:S(2)}, u32[]{:S(2)}) collective-permute-start(bf16[64,512]{1,0:T(8,128)(2,1)S(1)} %get-tuple-element.39.refs_0_), channel_id=1, source_target_pairs={{0,4},{4,0},{1,5},{5,1},{2,6},{6,2},{3,7},{7,3},{8,12},{12,8},{9,1... | collective-permute-start | bytes 196616 | tf_op jit(solution)/shard_map/ppermute | solution.py:431
  28.9 1.1 %shard_map.102 = (bf16[576,384]{1,0:T(8,128)(2,1)S(1)}, f32[16,128]{1,0:T(8,128)}) custom-call(f32[1,17]{1,0:T(1,128)S(1)} %bitcast.21, f32[1,17]{1,0:T(1,128)S(1)} %bitcast.23, f32[8,128]{1,0:T(8,128)S(1)} %add.7.info_ref, f32[16,128]{1,0:T(8,128)S(1)} %get-tuple-element.40.extra_ref, f32[64,128]{1,0:T(8,128)S(1)} %get-tuple-element.41.resid_ref), custom_call_target="tpu_custom_call" | custom-call | tf_op jit(solution)/shard_map/pallas_call | solution.py:423
  30.2 2.1 %collective-permute-start.14 = (bf16[64,512]{1,0:T(8,128)(2,1)S(1)}, bf16[64,512]{1,0:T(8,128)(2,1)S(1)}, u32[]{:S(2)}, u32[]{:S(2)}) collective-permute-start(bf16[64,512]{1,0:T(8,128)(2,1)S(1)} %collective-permute-done.13.refs_0_), channel_id=1, source_target_pairs={{0,4},{4,0},{1,5},{5,1},{2,6},{6,2},{3,7},{7,3},{8,12},{12,8},{9,1... | collective-permute-start | bytes 196616 | tf_op jit(solution)/shard_map/ppermute | solution.py:431
  32.3 1.3 %shard_map.103 = (f32[4,576,128]{2,1,0:T(8,128)}, f32[4,192,128]{2,1,0:T(8,128)S(1)}) custom-call(bf16[576,384]{1,0:T(8,128)(2,1)S(1)} %get-tuple-element.43.weight_ref, f32[4,576,128]{2,1,0:T(8,128)S(1)} %bitcast.15, bf16[64,512]{1,0:T(8,128)(2,1)S(1)} %get-tuple-element.39.refs_0_, bf16[64,512]{1,0:T(8,128)(2,1)S(1)} %collective-permute-done.11.refs_1_, ...), custom_call_target="tpu_custom_call" | custom-call | tf_op jit(solution)/shard_map/pallas_call | solution.py:434
  33.6 1.0 %shard_map.104 = f32[4,576,128]{2,1,0:T(8,128)} custom-call(bf16[576,384]{1,0:T(8,128)(2,1)S(1)} %get-tuple-element.43.weight_ref, f32[4,192,128]{2,1,0:T(8,128)S(1)} %get-tuple-element.45.rest_ref, f32[4,576,128]{2,1,0:T(8,128)} %get-tuple-element.46.begun_hbm, bf16[64,512]{1,0:T(8,128)(2,1)S(1)} %collective-permute-done.13.refs_0_, ...), custom_call_target="tpu_custom_call", output_to_operand_aliasing={{}: (2, {})} | custom-call | tf_op jit(solution)/shard_map/pallas_call | solution.py:445
  (35 shorter events, 1.0 us)
Async XLA Ops:
  0.6 10.6 %copy-start = (f32[4,24,24,128]{3,2,1,0:T(8,128)S(1)}, f32[4,24,24,128]{3,2,1,0:T(8,128)}, u32[]{:S(2)}) copy-start(f32[4,24,24,128]{3,2,1,0:T(8,128)} %param.8) | copy-start | bytes 3538948
  0.6 1.3 %copy-start.5 = (s32[1,1,1,16]{3,2,1,0:T(1,128)S(1)}, s32[1,1,1,16]{3,2,1,0:T(1,128)}, u32[]{:S(2)}) copy-start(s32[1,1,1,16]{3,2,1,0:T(1,128)} %param.12) | copy-start | bytes 196
  0.6 6.5 %copy-start.6 = (s32[1,1,1,16]{3,2,1,0:T(1,128)S(1)}, s32[1,1,1,16]{3,2,1,0:T(1,128)}, u32[]{:S(2)}) copy-start(s32[1,1,1,16]{3,2,1,0:T(1,128)} %param.14) | copy-start | bytes 196
  1.9 11.8 %copy-start.1 = (bf16[4,24,24,128]{3,2,1,0:T(8,128)(2,1)S(1)}, bf16[4,24,24,128]{3,2,1,0:T(8,128)(2,1)}, u32[]{:S(2)}) copy-start(bf16[4,24,24,128]{3,2,1,0:T(8,128)(2,1)} %param.9) | copy-start | bytes 1769476
  2.0 14.9 %copy-start.3 = (f32[17]{0:T(128)S(1)}, f32[17]{0:T(128)}, u32[]{:S(2)}) copy-start(f32[17]{0:T(128)} %param.10) | copy-start | bytes 208
  2.0 14.9 %copy-start.4 = (f32[17]{0:T(128)S(1)}, f32[17]{0:T(128)}, u32[]{:S(2)}) copy-start(f32[17]{0:T(128)} %param.11) | copy-start | bytes 208
  2.1 12.0 %collective-permute-start = (bf16[784,128]{1,0:T(8,128)(2,1)S(1)}, bf16[784,128]{1,0:T(8,128)(2,1)S(1)}, u32[]{:S(2)}, u32[]{:S(2)}) collective-permute-start(bf16[784,128]{1,0:T(8,128)(2,1)S(1)} %get-tuple-element.25), channel_id=1, source_target_pairs={{0,8},{8,0},{16,24},{24,16},{1,9},{9,1},{17,25},{25,17},{2,10},{10... | collective-permute-start | bytes 602120 | tf_op jit(solution)/shard_map/ppermute | solution.py:373
  4.3 11.8 %collective-permute-start.4 = (bf16[784,128]{1,0:T(8,128)(2,1)S(1)}, bf16[784,128]{1,0:T(8,128)(2,1)S(1)}, u32[]{:S(2)}, u32[]{:S(2)}) collective-permute-start(bf16[784,128]{1,0:T(8,128)(2,1)S(1)} %get-tuple-element.37), channel_id=1, source_target_pairs={{0,24},{8,16},{16,8},{24,0},{1,25},{9,17},{17,9},{25,1},{2,26},{10... | collective-permute-start | bytes 602120 | tf_op jit(solution)/shard_map/ppermute | solution.py:373
  7.1 2.7 %collective-permute-start.1 = (f32[8,128]{1,0:T(8,128)S(1)}, f32[8,128]{1,0:T(8,128)S(1)}, u32[]{:S(2)}, u32[]{:S(2)}) collective-permute-start(f32[8,128]{1,0:T(8,128)S(1)} %get-tuple-element.27.info_ref), channel_id=1, source_target_pairs={{0,1},{1,0},{2,3},{3,2},{4,5},{5,4},{6,7},{7,6},{8,9},{9,8},{10,11... | collective-permute-start | bytes 12296 | tf_op jit(solution)/shard_map/ppermute | solution.py:381
  9.9 3.9 %collective-permute-start.2 = (f32[8,128]{1,0:T(8,128)S(1)}, f32[8,128]{1,0:T(8,128)S(1)}, u32[]{:S(2)}, u32[]{:S(2)}) collective-permute-start(f32[8,128]{1,0:T(8,128)S(1)} %add.6), channel_id=1, source_target_pairs={{0,2},{1,3},{2,0},{3,1},{4,6},{5,7},{6,4},{7,5},{8,10},{9,11},{10,... | collective-permute-start | bytes 12296 | tf_op jit(solution)/shard_map/ppermute | solution.py:381
  11.2 6.3 %copy-start.2 = (f32[1,1,1,16,128]{4,3,2,1,0:T(8,128)S(1)}, f32[1,1,1,16,128]{4,3,2,1,0:T(8,128)}, u32[]{:S(2)}) copy-start(f32[1,1,1,16,128]{4,3,2,1,0:T(8,128)} %param.15) | copy-start | bytes 24580
  11.3 5.5 %collective-permute-start.3 = (bf16[784,128]{1,0:T(8,128)(2,1)S(1)}, bf16[784,128]{1,0:T(8,128)(2,1)S(1)}, u32[]{:S(2)}, u32[]{:S(2)}) collective-permute-start(bf16[784,128]{1,0:T(8,128)(2,1)S(1)} %get-tuple-element.30), channel_id=1, source_target_pairs={{0,4},{4,0},{1,5},{5,1},{2,6},{6,2},{3,7},{7,3},{8,12},{12,8},{9,1... | collective-permute-start | bytes 602120 | tf_op jit(solution)/shard_map/ppermute | solution.py:374
  14.1 3.4 %collective-permute-start.5 = (bf16[784,128]{1,0:T(8,128)(2,1)S(1)}, bf16[784,128]{1,0:T(8,128)(2,1)S(1)}, u32[]{:S(2)}, u32[]{:S(2)}) collective-permute-start(bf16[784,128]{1,0:T(8,128)(2,1)S(1)} %collective-permute-done.refs_4_), channel_id=1, source_target_pairs={{0,4},{4,0},{1,5},{5,1},{2,6},{6,2},{3,7},{7,3},{8,12},{12,8},{9,1... | collective-permute-start | bytes 602120 | tf_op jit(solution)/shard_map/ppermute | solution.py:399
  16.1 1.8 %collective-permute-start.6 = (bf16[784,128]{1,0:T(8,128)(2,1)S(1)}, bf16[784,128]{1,0:T(8,128)(2,1)S(1)}, u32[]{:S(2)}, u32[]{:S(2)}) collective-permute-start(bf16[784,128]{1,0:T(8,128)(2,1)S(1)} %collective-permute-done.4.refs_5_), channel_id=1, source_target_pairs={{0,4},{4,0},{1,5},{5,1},{2,6},{6,2},{3,7},{7,3},{8,12},{12,8},{9,1... | collective-permute-start | bytes 602120 | tf_op jit(solution)/shard_map/ppermute | solution.py:399
  18.1 3.8 %collective-permute-start.9 = (f32[80,128]{1,0:T(8,128)S(1)}, f32[80,128]{1,0:T(8,128)S(1)}, u32[]{:S(2)}, u32[]{:S(2)}) collective-permute-start(f32[80,128]{1,0:T(8,128)S(1)} %shard_map.100.refs_0_), channel_id=1, source_target_pairs={{0,3},{1,2},{2,1},{3,0},{4,7},{5,6},{6,5},{7,4},{8,11},{9,10},{10,... | collective-permute-start | bytes 122888 | tf_op jit(solution)/shard_map/ppermute | solution.py:30
  20.3 2.9 %collective-permute-start.8 = (f32[80,128]{1,0:T(8,128)S(1)}, f32[80,128]{1,0:T(8,128)S(1)}, u32[]{:S(2)}, u32[]{:S(2)}) collective-permute-start(f32[80,128]{1,0:T(8,128)S(1)} %shard_map.100.refs_0_), channel_id=1, source_target_pairs={{0,2},{1,3},{2,0},{3,1},{4,6},{5,7},{6,4},{7,5},{8,10},{9,11},{10,... | collective-permute-start | bytes 122888 | tf_op jit(solution)/shard_map/ppermute | solution.py:30
  20.6 2.9 %collective-permute-start.7 = (f32[80,128]{1,0:T(8,128)S(1)}, f32[80,128]{1,0:T(8,128)S(1)}, u32[]{:S(2)}, u32[]{:S(2)}) collective-permute-start(f32[80,128]{1,0:T(8,128)S(1)} %shard_map.100.refs_0_), channel_id=1, source_target_pairs={{0,1},{1,0},{2,3},{3,2},{4,5},{5,4},{6,7},{7,6},{8,9},{9,8},{10,11... | collective-permute-start | bytes 122888 | tf_op jit(solution)/shard_map/ppermute | solution.py:30
  23.5 6.5 %collective-permute-start.10 = (bf16[64,512]{1,0:T(8,128)(2,1)S(1)}, bf16[64,512]{1,0:T(8,128)(2,1)S(1)}, u32[]{:S(2)}, u32[]{:S(2)}) collective-permute-start(bf16[64,512]{1,0:T(8,128)(2,1)S(1)} %get-tuple-element.39.refs_0_), channel_id=1, source_target_pairs={{0,8},{8,0},{16,24},{24,16},{1,9},{9,1},{17,25},{25,17},{2,10},{10... | collective-permute-start | bytes 196616 | tf_op jit(solution)/shard_map/ppermute | solution.py:421
  23.9 6.3 %collective-permute-start.13 = (bf16[64,512]{1,0:T(8,128)(2,1)S(1)}, bf16[64,512]{1,0:T(8,128)(2,1)S(1)}, u32[]{:S(2)}, u32[]{:S(2)}) collective-permute-start(bf16[64,512]{1,0:T(8,128)(2,1)S(1)} %get-tuple-element.39.refs_0_), channel_id=1, source_target_pairs={{0,24},{8,16},{16,8},{24,0},{1,25},{9,17},{17,9},{25,1},{2,26},{10... | collective-permute-start | bytes 196616 | tf_op jit(solution)/shard_map/ppermute | solution.py:421
  26.3 6.1 %collective-permute-start.11 = (bf16[64,512]{1,0:T(8,128)(2,1)S(1)}, bf16[64,512]{1,0:T(8,128)(2,1)S(1)}, u32[]{:S(2)}, u32[]{:S(2)}) collective-permute-start(bf16[64,512]{1,0:T(8,128)(2,1)S(1)} %get-tuple-element.39.refs_0_), channel_id=1, source_target_pairs={{0,4},{4,0},{1,5},{5,1},{2,6},{6,2},{3,7},{7,3},{8,12},{12,8},{9,1... | collective-permute-start | bytes 196616 | tf_op jit(solution)/shard_map/ppermute | solution.py:431
  30.0 2.3 %collective-permute-start.12 = (bf16[64,512]{1,0:T(8,128)(2,1)S(1)}, bf16[64,512]{1,0:T(8,128)(2,1)S(1)}, u32[]{:S(2)}, u32[]{:S(2)}) collective-permute-start(bf16[64,512]{1,0:T(8,128)(2,1)S(1)} %collective-permute-done.10.refs_2_), channel_id=1, source_target_pairs={{0,4},{4,0},{1,5},{5,1},{2,6},{6,2},{3,7},{7,3},{8,12},{12,8},{9,1... | collective-permute-start | bytes 196616 | tf_op jit(solution)/shard_map/ppermute | solution.py:431
  30.2 3.4 %collective-permute-start.14 = (bf16[64,512]{1,0:T(8,128)(2,1)S(1)}, bf16[64,512]{1,0:T(8,128)(2,1)S(1)}, u32[]{:S(2)}, u32[]{:S(2)}) collective-permute-start(bf16[64,512]{1,0:T(8,128)(2,1)S(1)} %collective-permute-done.13.refs_0_), channel_id=1, source_target_pairs={{0,4},{4,0},{1,5},{5,1},{2,6},{6,2},{3,7},{7,3},{8,12},{12,8},{9,1... | collective-permute-start | bytes 196616 | tf_op jit(solution)/shard_map/ppermute | solution.py:431
